TPU v7x, 32 devices: a whole 2x2x4 slice. The times are simulated.
32 devices in a mesh: dp: 8 (over z, y), seq: 4 (over x, core).
Axes of the slice: x: 2, y: 2, z: 4, core: 2. Of those that a mesh axis runs over, the one named last changes fastest.
Arguments:
- layer_input: bfloat16 [16384, 768], P(('dp', 'seq')), may hold values from -6 to 6
- cotangent: bfloat16 [16384, 768], P(('dp', 'seq')), may hold values from -6 to 6
- segments: int32 [8, 2048], P('dp'), may hold values from 0 to 3, as said below
- routes: int32 [16384, 2], P(('dp', 'seq')), may hold values from 0 to 7, all different within a row
- order: int32 [16384], P(('dp', 'seq')), may hold values from 0 to 511, as said below
- norm1_gain: bfloat16 [768], P(('dp', 'seq')), may hold values from 0.5 to 1.5
- attn_qkv: bfloat16 [768, 2304], P(('dp', 'seq')), may hold values from -0.21875 to 0.21875
- attn_out: bfloat16 [768, 768], P(('dp', 'seq')), may hold values from -0.875 to 0.875
- norm2_gain: bfloat16 [768], P(('dp', 'seq')), may hold values from 0.5 to 1.5
- router: bfloat16 [768, 8], P(('dp', 'seq')), may hold values from -0.15625 to 0.15625
- shared_in: bfloat16 [768, 4096], P(('dp', 'seq')), may hold values from -0.21875 to 0.21875
- shared_out: bfloat16 [2048, 768], P(('dp', 'seq')), may hold values from -0.125 to 0.125
- expert_in: bfloat16 [8, 768, 4096], P('dp'), may hold values from -0.21875 to 0.21875
- expert_out: bfloat16 [8, 2048, 768], P('dp'), may hold values from -0.125 to 0.125
Outputs:
- layer_output: float32 [16384, 768], P(('dp', 'seq'))
- input_grad: float32 [16384, 768], P(('dp', 'seq'))
- norm1_gain_grad: float32 [768], P(('dp', 'seq'))
- attn_qkv_grad: float32 [768, 2304], P(('dp', 'seq'))
- attn_out_grad: float32 [768, 768], P(('dp', 'seq'))
- norm2_gain_grad: float32 [768], P(('dp', 'seq'))
- router_grad: float32 [768, 8], P(('dp', 'seq'))
- shared_in_grad: float32 [768, 4096], P(('dp', 'seq'))
- shared_out_grad: float32 [2048, 768], P(('dp', 'seq'))
- expert_in_grad: float32 [8, 768, 4096], P('dp', None, 'seq')
- expert_out_grad: float32 [8, 2048, 768], P('dp', 'seq')
Inputs may be any that keep to these rules, and one draw needn't show every extreme that they name: `segments`: each sequence holds four documents numbered 0, 1, 2, 3 in order, each of one token or more. `routes`: each token names two different experts. `order`: within the tokens of one device (512 in a row) each number from 0 to 511 stands once.
All inputs are finite; a program needn't handle non-finite values.
Results may differ from a plain program's by a relative error of at most 0.015.
Values may be sent and summed in bfloat16 or wider, within the bound.
No kernel may reach another device: no remote copies, remote signals or barrier semaphores. Data moves between devices by JAX's collectives and lax.ppermute only.
A program may use at most 192 MiB of HBM per device.

v0:
```python
import jax
import jax.numpy as jnp
from jax import lax
from jax.sharding import PartitionSpec as P

D = 768
HEADS = 12


EPS = 1e-06
BASE = 10000.0
MASKED = -1e30


def swish(values):
    return values * jax.nn.sigmoid(values)


def swiglu_back(d_act, pre_act, width):
    gate_part = pre_act[:, :width]
    up_part = pre_act[:, width:]
    sigma = jax.nn.sigmoid(gate_part)
    d_gate = d_act * up_part * sigma * (1.0 + gate_part * (1.0 - sigma))
    d_up = d_act * gate_part * sigma
    return jnp.concatenate([d_gate, d_up], axis=1)


def rotate(values, places, direction):
    half_width = values.shape[-1] // 2
    frequency = BASE ** (-(jnp.arange(half_width, dtype=jnp.float32) * 2.0 / values.shape[-1]))
    bcast_shape = (places.shape[0],) + (1,) * (values.ndim - 1)
    angles = places.astype(jnp.float32).reshape(bcast_shape) * frequency
    cosine = jnp.cos(angles)
    sine_part = jnp.sin(angles) * direction
    leading = values[..., :half_width]
    trailing = values[..., half_width:]
    return jnp.concatenate(
        [leading * cosine - trailing * sine_part, trailing * cosine + leading * sine_part], axis=-1
    )


def slot_plan(route_ids, ranks, experts, capacity):
    row_count = route_ids.shape[0]
    rank_of = ranks[:, None] + row_count * jnp.arange(2, dtype=jnp.int32)[None, :]
    flat_rank = rank_of.reshape(-1)
    by_rank = jnp.zeros((2 * row_count,), jnp.int32).at[flat_rank].set(route_ids.reshape(-1))
    onehot = (by_rank[:, None] == jnp.arange(experts, dtype=jnp.int32)[None, :]).astype(jnp.int32)
    earlier = jnp.cumsum(onehot, axis=0, dtype=jnp.int32) - onehot
    place_by_rank = jnp.sum(earlier * onehot, axis=1, dtype=jnp.int32)
    position = place_by_rank[flat_rank].reshape(row_count, 2)
    slot_of = jnp.where(position < capacity, route_ids * capacity + position, experts * capacity)
    owner_ids = jnp.full((experts * capacity + 1,), 2 * row_count, jnp.int32)
    owner_ids = owner_ids.at[slot_of.reshape(-1)].set(jnp.arange(2 * row_count, dtype=jnp.int32))
    return (slot_of, owner_ids[: experts * capacity])


def on_device(
    layer_input,
    cotangent,
    segments,
    routes,
    order,
    norm1_gain,
    attn_qkv,
    attn_out,
    norm2_gain,
    router,
    shared_in,
    shared_out,
    expert_in,
    expert_out,
):
    tok_rows = layer_input.shape[0]
    seq_devs = lax.axis_size("seq")
    experts = lax.axis_size("dp")
    heads_here = HEADS // seq_devs
    head_dim = D // HEADS
    length = tok_rows * seq_devs
    qblock = min(512, length)
    scale = head_dim ** (-0.5)
    capacity = max(2, (18 * tok_rows + 8 * experts - 1) // (8 * experts))
    gain_one, w_qkv, w_attn, gain_two, w_router, w_sin, w_sout = (
        lax.all_gather(norm1_gain, ("dp", "seq"), axis=0, tiled=True),
        lax.all_gather(attn_qkv, ("dp", "seq"), axis=0, tiled=True),
        lax.all_gather(attn_out, ("dp", "seq"), axis=0, tiled=True),
        lax.all_gather(norm2_gain, ("dp", "seq"), axis=0, tiled=True),
        lax.all_gather(router, ("dp", "seq"), axis=0, tiled=True),
        lax.all_gather(shared_in, ("dp", "seq"), axis=0, tiled=True),
        lax.all_gather(shared_out, ("dp", "seq"), axis=0, tiled=True),
    )
    gain_onef = gain_one.astype(jnp.float32)
    gain_twof = gain_two.astype(jnp.float32)
    shared_width = w_sout.shape[0]
    tokens = layer_input.astype(jnp.float32)
    rms_one = lax.rsqrt(jnp.mean(tokens * tokens, axis=-1, keepdims=True) + EPS)
    scaled_one = tokens * rms_one
    normed = (scaled_one * gain_onef).astype(jnp.bfloat16)
    projected = jnp.dot(normed, w_qkv, preferred_element_type=jnp.float32).reshape(
        tok_rows, HEADS, 3, head_dim
    )
    places = lax.axis_index("seq") * tok_rows + jnp.arange(tok_rows, dtype=jnp.int32)
    turned = jnp.concatenate(
        [rotate(projected[:, :, :2], places, 1.0), projected[:, :, 2:]], axis=2
    )
    turned = turned.astype(jnp.bfloat16).reshape(tok_rows, HEADS, 3 * head_dim)
    head_rows = lax.all_to_all(turned, "seq", split_axis=1, concat_axis=0, tiled=True)
    query_heads = head_rows[:, :, :head_dim]
    key_heads = head_rows[:, :, head_dim : 2 * head_dim]
    value_heads = head_rows[:, :, 2 * head_dim :]
    doc_ids = segments[0]
    key_places = jnp.arange(length, dtype=jnp.int32)
    starts = jnp.arange(length // qblock, dtype=jnp.int32) * qblock

    def block_scores(q_rows, start):
        q_places = start + jnp.arange(qblock, dtype=jnp.int32)
        q_docs = lax.dynamic_slice_in_dim(doc_ids, start, qblock, 0)
        scores = (
            jnp.einsum("qhd,khd->hqk", q_rows, key_heads, preferred_element_type=jnp.float32)
            * scale
        )
        allowed = (key_places[None, :] <= q_places[:, None]) & (doc_ids[None, :] == q_docs[:, None])
        return (jnp.where(allowed[None], scores, MASKED), allowed)

    def forward_block(start):
        q_rows = lax.dynamic_slice_in_dim(query_heads, start, qblock, 0)
        scores, allowed = block_scores(q_rows, start)
        top_score = jnp.max(scores, axis=-1, keepdims=True)
        weights = jnp.exp(scores - top_score)
        totals = jnp.sum(weights, axis=-1, keepdims=True)
        probs = weights / totals
        log_total = (top_score + jnp.log(totals))[..., 0]
        context_rows = jnp.einsum(
            "hqk,khd->qhd",
            probs.astype(jnp.bfloat16),
            value_heads,
            preferred_element_type=jnp.float32,
        )
        return (context_rows.astype(jnp.bfloat16), log_total)

    context_blocks, log_totals = lax.map(forward_block, starts)
    context_heads = context_blocks.reshape(length, heads_here * head_dim)
    context = lax.all_to_all(context_heads, "seq", split_axis=0, concat_axis=1, tiled=True)
    hidden = tokens + jnp.dot(context, w_attn, preferred_element_type=jnp.float32)
    rms_two = lax.rsqrt(jnp.mean(hidden * hidden, axis=-1, keepdims=True) + EPS)
    scaled_two = hidden * rms_two
    normed_two = (scaled_two * gain_twof).astype(jnp.bfloat16)
    logits = jnp.dot(normed_two, w_router, preferred_element_type=jnp.float32)
    picker = (routes[:, :, None] == jnp.arange(experts, dtype=jnp.int32)[None, None, :]).astype(
        jnp.float32
    )
    chosen = jnp.sum(picker * logits[:, None, :], axis=-1)
    top_logit = jnp.max(chosen, axis=-1, keepdims=True)
    expd = jnp.exp(chosen - top_logit)
    gates = expd / jnp.sum(expd, axis=-1, keepdims=True)
    shared_pre = jnp.dot(normed_two, w_sin, preferred_element_type=jnp.float32)
    shared_act = (swish(shared_pre[:, :shared_width]) * shared_pre[:, shared_width:]).astype(
        jnp.bfloat16
    )
    shared_res = jnp.dot(shared_act, w_sout, preferred_element_type=jnp.float32)
    slot_of, owner_ids = slot_plan(routes, order, experts, capacity)
    normed_pad = jnp.concatenate([normed_two, jnp.zeros((1, D), jnp.bfloat16)], axis=0)
    send_rows = normed_pad[owner_ids // 2].reshape(experts, capacity, D)
    w_ein = expert_in[0]
    w_eout = expert_out[0]
    ff_width = w_eout.shape[0]
    rows = lax.all_to_all(send_rows, "dp", split_axis=0, concat_axis=0, tiled=True)
    flat_rows = rows.reshape(-1, D)
    pre_act = jnp.dot(flat_rows, w_ein, preferred_element_type=jnp.float32)
    activity = (swish(pre_act[:, :ff_width]) * pre_act[:, ff_width:]).astype(jnp.bfloat16)
    result = jnp.dot(activity, w_eout, preferred_element_type=jnp.float32).astype(jnp.bfloat16)
    result, pre_act = (
        result.reshape(rows.shape),
        pre_act.reshape(rows.shape[0], rows.shape[1], 2 * ff_width),
    )
    results = (result, pre_act, rows)
    received = results[-1]
    returned = lax.all_to_all(results[0], "dp", split_axis=0, concat_axis=0, tiled=True)
    returned_pad = jnp.concatenate(
        [returned.reshape(experts * capacity, D), jnp.zeros((1, D), jnp.bfloat16)], axis=0
    )
    picked = returned_pad[slot_of].astype(jnp.float32)
    mixture = jnp.sum(gates[:, :, None] * picked, axis=1)
    output = hidden + shared_res + mixture
    d_out = cotangent.astype(jnp.float32)
    d_gates = jnp.sum(d_out[:, None, :] * picked, axis=-1)
    d_chosen = gates * (d_gates - jnp.sum(gates * d_gates, axis=-1, keepdims=True))
    d_logits = jnp.sum(picker * d_chosen[:, :, None], axis=1).astype(jnp.bfloat16)
    gate_pad = jnp.concatenate([gates.reshape(-1), jnp.zeros((1,), jnp.float32)], axis=0)
    d_out_pad = jnp.concatenate([d_out, jnp.zeros((1, D), jnp.float32)], axis=0)
    d_slots = (
        (gate_pad[owner_ids][:, None] * d_out_pad[owner_ids // 2])
        .astype(jnp.bfloat16)
        .reshape(experts, capacity, D)
    )
    d_received = lax.all_to_all(d_slots, "dp", split_axis=0, concat_axis=0, tiled=True)
    flat_rows = received.reshape(-1, D)
    d_rows = d_received.reshape(-1, D)
    pre_rows = results[1].reshape(-1, 2 * ff_width)
    activity = (swish(pre_rows[:, :ff_width]) * pre_rows[:, ff_width:]).astype(jnp.bfloat16)
    d_activity = jnp.dot(d_rows, w_eout.T, preferred_element_type=jnp.float32)
    d_pre = swiglu_back(d_activity, pre_rows, ff_width).astype(jnp.bfloat16)
    d_inputs = jnp.dot(d_pre, w_ein.T, preferred_element_type=jnp.float32).astype(jnp.bfloat16)
    eout_grad = jnp.einsum("rf,rd->fd", activity, d_rows, preferred_element_type=jnp.float32)
    ein_grad = jnp.einsum("rd,rf->df", flat_rows, d_pre, preferred_element_type=jnp.float32)
    d_sent = lax.all_to_all(
        d_inputs.reshape(experts, capacity, D), "dp", split_axis=0, concat_axis=0, tiled=True
    )
    d_sent_pad = jnp.concatenate(
        [d_sent.reshape(experts * capacity, D), jnp.zeros((1, D), jnp.bfloat16)], axis=0
    )
    d_normed_moe = jnp.sum(d_sent_pad[slot_of].astype(jnp.float32), axis=1)
    ein_part, eout_part = (
        lax.psum_scatter(
            ein_grad.astype(jnp.bfloat16), "seq", scatter_dimension=1, tiled=True
        ).astype(jnp.float32),
        lax.psum_scatter(
            eout_grad.astype(jnp.bfloat16), "seq", scatter_dimension=0, tiled=True
        ).astype(jnp.float32),
    )
    d_out_low = d_out.astype(jnp.bfloat16)
    sout_grad = jnp.einsum("ts,td->sd", shared_act, d_out_low, preferred_element_type=jnp.float32)
    d_shared_act = jnp.dot(d_out_low, w_sout.T, preferred_element_type=jnp.float32)
    d_shared_pre = swiglu_back(d_shared_act, shared_pre, shared_width).astype(jnp.bfloat16)
    sin_grad = jnp.einsum("td,ts->ds", normed_two, d_shared_pre, preferred_element_type=jnp.float32)
    router_grad = jnp.einsum("td,te->de", normed_two, d_logits, preferred_element_type=jnp.float32)
    d_normed_two = (
        jnp.dot(d_shared_pre, w_sin.T, preferred_element_type=jnp.float32)
        + jnp.dot(d_logits, w_router.T, preferred_element_type=jnp.float32)
        + d_normed_moe
    )
    gain_two_grad = jnp.sum(d_normed_two * scaled_two, axis=0)
    d_scaled_two = d_normed_two * gain_twof
    d_hidden = d_out + rms_two * (
        d_scaled_two - scaled_two * jnp.mean(d_scaled_two * scaled_two, axis=-1, keepdims=True)
    )
    d_hidden_low = d_hidden.astype(jnp.bfloat16)
    attn_grad = jnp.einsum("td,te->de", context, d_hidden_low, preferred_element_type=jnp.float32)
    d_context = jnp.dot(d_hidden_low, w_attn.T, preferred_element_type=jnp.float32).astype(
        jnp.bfloat16
    )
    d_context_heads = lax.all_to_all(
        d_context, "seq", split_axis=1, concat_axis=0, tiled=True
    ).reshape(length, heads_here, head_dim)

    def backward_block(carry, inputs):
        d_keys, d_values = carry
        start, log_total = inputs
        q_rows = lax.dynamic_slice_in_dim(query_heads, start, qblock, 0)
        d_rows_ctx = lax.dynamic_slice_in_dim(d_context_heads, start, qblock, 0)
        scores, allowed = block_scores(q_rows, start)
        probs = jnp.where(allowed[None], jnp.exp(scores - log_total[..., None]), 0.0)
        d_probs = jnp.einsum(
            "qhd,khd->hqk", d_rows_ctx, value_heads, preferred_element_type=jnp.float32
        )
        row_dot = jnp.sum(d_probs * probs, axis=-1, keepdims=True)
        d_scores = (probs * (d_probs - row_dot)).astype(jnp.bfloat16)
        d_query = (
            jnp.einsum("hqk,khd->qhd", d_scores, key_heads, preferred_element_type=jnp.float32)
            * scale
        )
        d_keys = (
            d_keys
            + jnp.einsum("hqk,qhd->khd", d_scores, q_rows, preferred_element_type=jnp.float32)
            * scale
        )
        d_values = d_values + jnp.einsum(
            "hqk,qhd->khd",
            probs.astype(jnp.bfloat16),
            d_rows_ctx,
            preferred_element_type=jnp.float32,
        )
        return ((d_keys, d_values), d_query.astype(jnp.bfloat16))

    zero_heads = jnp.zeros((length, heads_here, head_dim), jnp.float32)
    (d_keys, d_values), d_query_blocks = lax.scan(
        backward_block, (zero_heads, zero_heads), (starts, log_totals)
    )
    d_queries = d_query_blocks.reshape(length, heads_here, head_dim)
    d_heads = jnp.concatenate(
        [d_queries, d_keys.astype(jnp.bfloat16), d_values.astype(jnp.bfloat16)], axis=2
    )
    d_turned = lax.all_to_all(
        d_heads.reshape(length, heads_here * 3 * head_dim),
        "seq",
        split_axis=0,
        concat_axis=1,
        tiled=True,
    )
    d_turned = d_turned.reshape(tok_rows, HEADS, 3, head_dim).astype(jnp.float32)
    d_projected = jnp.concatenate(
        [rotate(d_turned[:, :, :2], places, -1.0), d_turned[:, :, 2:]], axis=2
    )
    d_projected = d_projected.astype(jnp.bfloat16).reshape(tok_rows, 3 * D)
    qkv_grad = jnp.einsum("td,tc->dc", normed, d_projected, preferred_element_type=jnp.float32)
    d_normed = jnp.dot(d_projected, w_qkv.T, preferred_element_type=jnp.float32)
    gain_one_grad = jnp.sum(d_normed * scaled_one, axis=0)
    d_scaled_one = d_normed * gain_onef
    input_grad = d_hidden + rms_one * (
        d_scaled_one - scaled_one * jnp.mean(d_scaled_one * scaled_one, axis=-1, keepdims=True)
    )
    grad_one, grad_qkv, grad_attn, grad_two, grad_router, grad_sin, grad_sout = (
        lax.psum_scatter(gain_one_grad, ("dp", "seq"), scatter_dimension=0, tiled=True),
        lax.psum_scatter(qkv_grad, ("dp", "seq"), scatter_dimension=0, tiled=True),
        lax.psum_scatter(attn_grad, ("dp", "seq"), scatter_dimension=0, tiled=True),
        lax.psum_scatter(gain_two_grad, ("dp", "seq"), scatter_dimension=0, tiled=True),
        lax.psum_scatter(router_grad, ("dp", "seq"), scatter_dimension=0, tiled=True),
        lax.psum_scatter(sin_grad, ("dp", "seq"), scatter_dimension=0, tiled=True),
        lax.psum_scatter(sout_grad, ("dp", "seq"), scatter_dimension=0, tiled=True),
    )
    return (
        output,
        input_grad,
        grad_one,
        grad_qkv,
        grad_attn,
        grad_two,
        grad_router,
        grad_sin,
        grad_sout,
        ein_part[None],
        eout_part[None],
    )


def solution(mesh):
    return jax.shard_map(
        on_device,
        mesh=mesh,
        in_specs=(
            P(("dp", "seq"), None),
            P(("dp", "seq"), None),
            P("dp", None),
            P(("dp", "seq"), None),
            P(("dp", "seq")),
            P(("dp", "seq")),
            P(("dp", "seq"), None),
            P(("dp", "seq"), None),
            P(("dp", "seq")),
            P(("dp", "seq"), None),
            P(("dp", "seq"), None),
            P(("dp", "seq"), None),
            P("dp", None, None),
            P("dp", None, None),
        ),
        out_specs=(
            P(("dp", "seq"), None),
            P(("dp", "seq"), None),
            P(("dp", "seq")),
            P(("dp", "seq"), None),
            P(("dp", "seq"), None),
            P(("dp", "seq")),
            P(("dp", "seq"), None),
            P(("dp", "seq"), None),
            P(("dp", "seq"), None),
            P("dp", None, "seq"),
            P("dp", "seq", None),
        ),
        check_vma=False,
    )
```

profile of v0, /device:TPU:0, one launch (start us, length us, event | category | flops | bytes accessed | tf_op | source)
XLA Modules:
  0.0 1088.6 jit_solution(4647852637507002377)
XLA Ops:
  12.5 42.1 %all-reduce.10 = (bf16[768]{0:T(1024)(128)(2,1)S(1)}, bf16[768]{0:T(1024)(128)(2,1)}) all-reduce(bf16[768]{0:T(1024)(128)(2,1)S(1)} %dynamic-update-slice, bf16[768]{0:T(1024)(128)(2,1)S(1)} %dynamic-update-slice.1), channel_id=1, replica_groups=mesh['dp'=8,'seq'=4] {'dp','seq'}, use_global_device_ids=true, to_apply=%add.4 | all-reduce | flops 1536 | bytes 6144
  56.4 17.5 %all-gather.6.cloned.1.call-done = bf16[768,2304]{1,0:T(8,128)(2,1)} async-done(((bf16[24,2304]{1,0:T(8,128)(2,1)}), bf16[768,2304]{1,0:T(8,128)(2,1)}) %all-gather.6.cloned.1.call-update) | async-done | bytes 3538960 | tf_op jit(solution)/shard_map/all_gather | solution.py:84
  74.0 4.4 fusion.67
  80.6 4.6 all-to-all-start
  88.3 4.8 scatter_custom_fusion
  95.9 4.5 gather_fusion
  101.3 13.5 %all-to-all-done = bf16[512,12,192]{0,2,1:T(8,128)(2,1)} async-done(((bf16[512,12,192]{0,2,1:T(8,128)(2,1)}), bf16[512,12,192]{0,2,1:T(8,128)(2,1)}, u32[]{:S(2)}, u32[]{:S(2)}) %all-to-all-start) | async-done | bytes 2359328 | tf_op jit(solution)/shard_map/all_to_all | solution.py:106
  119.2 110.7 %while.28 = (s32[]{:T(128)}, bf16[4,512,3,64]{1,3,2,0:T(8,128)(2,1)}, f32[4,3,512]{2,1,0:T(4,128)}, s32[4]{0:T(128)S(1)}, s32[1,2048]{1,0:T(1,128)S(1)}, /*index...) while((s32[]{:T(128)}, ...), condition=%wide.region_4.5_spmd.clone, body=%wide.region_1.4_spmd.clone.sunk | while | flops 846298112 | bytes 47124700 | solution.py:140
  123.5 8.5 fusion.152
  132.0 6.8 fusion.153
  138.8 7.5 fusion.154
  151.2 8.5 fusion.152
  159.7 6.8 fusion.153
  166.6 7.4 fusion.154
  178.9 8.5 fusion.152
  187.4 7.0 fusion.153
  194.4 7.4 fusion.154
  206.6 8.5 fusion.152
  215.1 6.8 fusion.153
  221.9 7.4 fusion.154
  241.5 4.4 all-to-all-done.1
  250.8 7.0 gather_fusion.1
  257.7 4.7 all-to-all-start.2
  262.5 64.1 %all-gather = bf16[32,24,8]{1,2,0:T(8,128)(2,1)S(1)} all-gather(bf16[1,24,8]{1,2,0:T(8,128)(2,1)S(1)} %bitcast.204), channel_id=1, replica_groups=mesh['dp'=8,'seq'=4] {'dp','seq'}, dimensions={0}, use_global_device_ids=true | all-gather | bytes 12672 | tf_op jit(solution)/shard_map/all_gather | solution.py:87
  329.2 7.2 gather_fusion.4
  338.2 6.5 gather_fusion.3
  348.3 5.3 all-to-all-start.4
  354.2 13.7 %fusion.41 = f32[1152,4096]{1,0:T(8,128)} fusion(bf16[1152,768]{1,0:T(8,128)(2,1)} %bitcast.14, bf16[1,768,4096]{2,1,0:T(8,128)(2,1)} %param.30), kind=kOutput, calls=%fused_computation.63 | convolution fusion | flops 7247757312 | bytes 26935296 | tf_op jit(solution)/shard_map/dot_general | solution.py:168
  367.9 32.0 %all-to-all-done.4 = bf16[8,144,768]{2,1,0:T(8,128)(2,1)} async-done(((bf16[8,144,768]{2,1,0:T(8,128)(2,1)}), bf16[8,144,768]{2,1,0:T(8,128)(2,1)}, u32[]{:S(2)}, u32[]{:S(2)}) %all-to-all-start.4) | async-done | bytes 1769504 | tf_op jit(solution)/shard_map/all_to_all | solution.py:195
  399.9 13.9 %multiply_convert_fusion.2 = (bf16[1152,2048]{1,0:T(8,128)(2,1)}, bf16[1152,2048]{1,0:T(8,128)(2,1)}, bf16[1152,2048]{1,0:T(8,128)(2,1)S(1)}) fusion(f32[1152,4096]{1,0:T(8,128)} %fusion.41, bf16[1152,768]{1,0:T(8,128)(2,1)} %bitcast.20, bf16[1,2048,768]{2,1,0:T(8,128)(2,1)S(1)} %copy-done), kind=kOutput, calls=%fused_computation.57 | convolution fusion | flops 3661627392 | bytes 37945344 | tf_op jit(solution)/shard_map/dot_general | solution.py:200
  416.0 7.3 convolution_convert_fusion.1
  423.6 14.6 %convolution_convert_fusion = bf16[768,4096]{1,0:T(8,128)(2,1)} fusion(bf16[1152,768]{1,0:T(8,128)(2,1)} %bitcast.14, bf16[1152,2048]{1,0:T(8,128)(2,1)} %get-tuple-element.259, bf16[1152,2048]{1,0:T(8,128)(2,1)} %get-tuple-element.258), kind=kOutput, calls=%fused_computation.60 | convolution fusion | flops 7269777408 | bytes 17498112 | tf_op jit(solution)/shard_map/rd,rf->df/dot_general | solution.py:204
  438.1 7.6 convolution_convert_fusion.2
  445.7 4.4 all-to-all-start.3
  451.6 13.0 %fusion.43 = bf16[1152,768]{1,0:T(8,128)(2,1)} fusion(bf16[1,768,4096]{2,1,0:T(8,128)(2,1)} %param.30, bf16[1152,2048]{1,0:T(8,128)(2,1)} %get-tuple-element.259, bf16[1152,2048]{1,0:T(8,128)(2,1)} %get-tuple-element.258), kind=kOutput, calls=%fused_computation.72 | convolution fusion | flops 7267516416 | bytes 17498112 | tf_op jit(solution)/shard_map/dot_general | solution.py:202
  464.6 27.0 %all-to-all-done.3 = bf16[8,144,768]{2,1,0:T(8,128)(2,1)} async-done(((bf16[8,144,768]{2,1,0:T(8,128)(2,1)}), bf16[8,144,768]{2,1,0:T(8,128)(2,1)}, u32[]{:S(2)}, u32[]{:S(2)}) %all-to-all-start.3) | async-done | bytes 1769504 | tf_op jit(solution)/shard_map/all_to_all | solution.py:177
  491.6 4.3 all-to-all-start.5
  496.4 8.3 fusion.89
  504.7 7.4 multiply_convert_fusion.5
  512.2 4.6 fusion.50
  518.4 5.2 gather_fusion.2
  523.6 5.0 reshape.624
  528.6 9.4 multiply_reduce_fusion.1
  539.7 5.2 gather_fusion.5
  544.9 5.0 reshape.625
  549.9 5.7 reduce_sum.153
  570.6 6.3 fusion.91
  576.9 5.3 all-to-all-done.6
  588.6 113.5 %while.29 = (s32[]{:T(128)}, f32[2048,3,64]{0,2,1:T(8,128)S(1)}, f32[2048,3,64]{0,2,1:T(8,128)S(1)}, bf16[4,512,3,64]{1,3,2,0:T(8,128)(2,1)}, s32[4]{0:T(128)S(1...) while((s32[]{:T(128)}, f32[2048,3,64]{0,2,1:T(8,128)S(1)}, ...), condition=%wide.region_22.23_spmd.clone, body=%wide.region_20.22_spmd.clone.sunk | while | flops 2050030592 | bytes 131318032 | solution.py:275
  593.8 5.5 exponential_select_fusion.2
  608.8 6.0 fusion.167
  622.2 5.5 exponential_select_fusion.2
  637.2 5.8 fusion.167
  650.5 5.5 exponential_select_fusion.2
  665.4 5.8 fusion.167
  678.7 5.5 exponential_select_fusion.2
  693.7 6.0 fusion.167
  709.3 42.2 %all_to_all.86 = bf16[4,512,576]{1,2,0:T(8,128)(2,1)S(1)} all-to-all(bf16[4,512,576]{1,2,0:T(8,128)(2,1)S(1)} %copy.88), channel_id=1, replica_groups=mesh['dp'=8,'seq'=4] {'seq'}, dimensions={0} | all-to-all | bytes 4718592 | tf_op jit(solution)/shard_map/all_to_all | solution.py:282
  754.3 5.1 fusion.65
  760.5 8.6 fusion.49
  770.6 6.1 add_add_fusion.1
  780.2 40.0 %all-reduce.9 = (f32[768]{0:T(1024)S(1)}, f32[768]{0:T(1024)S(1)}, f32[768,8]{0,1:T(8,128)S(1)}) all-reduce(f32[768]{0:T(1024)S(1)} %get-tuple-element.203, f32[768]{0:T(1024)S(1)} %copy-done.35, f32[768,8]{0,1:T(8,128)S(1)} %fusion.92), channel_id=2, replica_groups=mesh['dp'=8,'seq'=4] {'dp','seq'}, use_global_device_ids=true, to_apply=%region_25.26.clone | all-reduce | flops 7680 | bytes 61440
  831.9 87.2 %reduce-scatter.8.cloned.1.call-done = f32[24,2304]{1,0:T(8,128)} async-done(((f32[768,2304]{1,0:T(8,128)}), f32[24,2304]{1,0:T(8,128)}) %reduce-scatter.8.cloned.1.call-update) | async-done | bytes 221200 | tf_op jit(solution)/shard_map/reduce_scatter | solution.py:303
  919.2 162.2 %reduce-scatter.12.cloned.1.call-done = f32[24,4096]{1,0:T(8,128)} async-done(((f32[768,4096]{1,0:T(8,128)}), f32[24,4096]{1,0:T(8,128)}) %reduce-scatter.12.cloned.1.call-update) | async-done | bytes 393232 | tf_op jit(solution)/shard_map/reduce_scatter | solution.py:307
  (283 shorter events, 173.3 us)
Async XLA Ops:
  7.2 392.8 %copy-start = (bf16[1,2048,768]{2,1,0:T(8,128)(2,1)S(1)}, bf16[1,2048,768]{2,1,0:T(8,128)(2,1)}, u32[]{:S(2)}) copy-start(bf16[1,2048,768]{2,1,0:T(8,128)(2,1)} %param.31) | copy-start | bytes 9437188
  7.2 66.8 %all-gather.6.cloned.1.call-start = ((), (), s32[]{:S(2)}) async-start(), calls=%async_computation.14 | async-start | bytes 3649536 | tf_op jit(solution)/shard_map/all_gather | solution.py:84
  7.9 233.5 %all-gather.8.cloned.1.call-start = ((), (), s32[]{:S(2)}) async-start(), calls=%async_computation.15 | async-start | bytes 1216512 | tf_op jit(solution)/shard_map/all_gather | solution.py:85
  8.7 487.7 %all-gather.10.cloned.1.call-start = ((), (), s32[]{:S(2)}) async-start(), calls=%async_computation.16 | async-start | bytes 6488064 | tf_op jit(solution)/shard_map/all_gather | solution.py:88
  10.8 67.5 %copy-start.33 = (f32[512]{0:T(512)}, f32[512]{0:T(512)S(1)}, u32[]{:S(2)}) copy-start(f32[512]{0:T(512)S(1)} %add_rsqrt_fusion.1) | copy-start | bytes 6148
  54.7 23.7 %copy-start.27 = (f32[768]{0:T(1024)}, f32[768]{0:T(1024)S(1)}, u32[]{:S(2)}) copy-start(f32[768]{0:T(1024)S(1)} %convert_element_type.124) | copy-start | bytes 9220
  56.4 22.0 %copy-start.24 = (f32[512,32]{0,1:T(8,128)}, f32[512,32]{0,1:T(8,128)S(1)}, u32[]{:S(2)}) copy-start(f32[512,32]{0,1:T(8,128)S(1)} %get-tuple-element.275) | copy-start | bytes 196612
  80.6 4.6 copy-start.31
  80.6 5.5 copy-start.36
  80.6 34.3 %all-to-all-start = ((bf16[512,12,192]{0,2,1:T(8,128)(2,1)}), bf16[512,12,192]{0,2,1:T(8,128)(2,1)}, u32[]{:S(2)}, u32[]{:S(2)}) async-start(bf16[512,12,192]{0,2,1:T(8,128)(2,1)} %bitcast.183), calls=%async_computation | async-start | bytes 4718592 | tf_op jit(solution)/shard_map/all_to_all | solution.py:106
  116.8 2.4 copy-start.20
  119.2 114.9 %copy-start.23 = (s32[512,2]{1,0:T(8,128)S(1)}, s32[512,2]{1,0:T(8,128)}, u32[]{:S(2)}) copy-start(s32[512,2]{1,0:T(8,128)} %copy.81) | copy-start | bytes 12292
  119.2 116.7 %copy-start.38 = (bf16[768]{0:T(1024)(128)(2,1)S(1)}, bf16[768]{0:T(1024)(128)(2,1)}, u32[]{:S(2)}) copy-start(bf16[768]{0:T(1024)(128)(2,1)} %get-tuple-element.251) | copy-start | bytes 4612
  132.0 6.8 copy-start.3
  159.7 6.9 copy-start.3
  187.4 7.0 copy-start.3
  215.1 6.8 copy-start.3
  229.9 18.6 %copy-start.40 = (s32[4]{0:T(128)}, s32[4]{0:T(128)S(1)}, u32[]{:S(2)}) copy-start(s32[4]{0:T(128)S(1)} %get-tuple-element.555) | copy-start | bytes 52
  229.9 15.9 %all-to-all-start.1 = ((bf16[4,512,192]{1,2,0:T(8,128)(2,1)}), bf16[4,512,192]{1,2,0:T(8,128)(2,1)}, u32[]{:S(2)}, u32[]{:S(2)}) async-start(bf16[4,512,192]{1,2,0:T(8,128)(2,1)} %bitcast.192), calls=%async_computation.1 | async-start | bytes 1572864 | tf_op jit(solution)/shard_map/all_to_all | solution.py:142
  248.5 2.3 copy-start.7
  248.7 1.1 copy-start.4
  257.7 4.7 copy-start.37
  257.7 90.6 %all-to-all-start.2 = ((bf16[8,144,768]{2,1,0:T(8,128)(2,1)}), bf16[8,144,768]{2,1,0:T(8,128)(2,1)}, u32[]{:S(2)}, u32[]{:S(2)}) async-start(bf16[8,144,768]{2,1,0:T(8,128)(2,1)} %bitcast.187), calls=%async_computation.2 | async-start | bytes 3538944 | tf_op jit(solution)/shard_map/all_to_all | solution.py:166
  329.2 8.6 copy-start.32
  348.3 51.6 %all-to-all-start.4 = ((bf16[8,144,768]{2,1,0:T(8,128)(2,1)}), bf16[8,144,768]{2,1,0:T(8,128)(2,1)}, u32[]{:S(2)}, u32[]{:S(2)}) async-start(bf16[8,144,768]{2,1,0:T(8,128)(2,1)} %multiply_convert_fusion.7), calls=%async_computation.4 | async-start | bytes 3538944 | tf_op jit(solution)/shard_map/all_to_all | solution.py:195
  353.6 151.1 %all-gather.12.cloned.1.call-start = ((), (), s32[]{:S(2)}) async-start(), calls=%async_computation.17 | async-start | bytes 3244032 | tf_op jit(solution)/shard_map/all_gather | solution.py:89
  354.2 471.8 %reduce-scatter.18.cloned.1.call-start = ((), (), s32[]{:S(2)}) async-start(), calls=%async_computation.23 | async-start | bytes 3932160 | tf_op jit(solution)/shard_map/reduce_scatter | solution.py:216
  413.9 2.1 copy-start.42
  423.3 405.1 %reduce-scatter.16.cloned.1.call-start = ((), (), s32[]{:S(2)}) async-start(), calls=%async_computation.22 | async-start | bytes 7864320 | tf_op jit(solution)/shard_map/reduce_scatter | solution.py:213
  445.7 4.5 copy-start.11
  445.7 5.7 copy-start.22
  445.7 45.8 %all-to-all-start.3 = ((bf16[8,144,768]{2,1,0:T(8,128)(2,1)}), bf16[8,144,768]{2,1,0:T(8,128)(2,1)}, u32[]{:S(2)}, u32[]{:S(2)}) async-start(bf16[8,144,768]{2,1,0:T(8,128)(2,1)} %bitcast.194), calls=%async_computation.3 | async-start | bytes 3538944 | tf_op jit(solution)/shard_map/all_to_all | solution.py:177
  464.6 31.8 %copy-start.5 = (bf16[512,768]{1,0:T(8,128)(2,1)S(1)}, bf16[512,768]{1,0:T(8,128)(2,1)}, u32[]{:S(2)}) copy-start(bf16[512,768]{1,0:T(8,128)(2,1)} %copy-done.4) | copy-start | bytes 2359300
  491.6 46.5 %all-to-all-start.5 = ((bf16[8,144,768]{2,1,0:T(8,128)(2,1)}), bf16[8,144,768]{2,1,0:T(8,128)(2,1)}, u32[]{:S(2)}, u32[]{:S(2)}) async-start(bf16[8,144,768]{2,1,0:T(8,128)(2,1)} %bitcast.193), calls=%async_computation.5 | async-start | bytes 3538944 | tf_op jit(solution)/shard_map/all_to_all | solution.py:205
  495.9 336.0 %reduce-scatter.10.cloned.1.call-start = ((), (), s32[]{:S(2)}) async-start(), calls=%async_computation.19 | async-start | bytes 2433024 | tf_op jit(solution)/shard_map/reduce_scatter | solution.py:304
  504.7 7.4 copy-start.16
  512.1 4.6 copy-start.18
  512.1 4.6 copy-start.19
  523.6 5.0 copy-start.17
  549.9 5.8 copy-start.8
  555.7 2.8 copy-start.29
  555.7 2.8 copy-start.12
  559.0 4.0 copy-start.10
  566.3 15.9 %all-to-all-start.6 = ((bf16[512,4,192]{0,2,1:T(8,128)(2,1)}), bf16[512,4,192]{0,2,1:T(8,128)(2,1)}, u32[]{:S(2)}, u32[]{:S(2)}) async-start(bf16[512,4,192]{0,2,1:T(8,128)(2,1)} %bitcast.23), calls=%async_computation.6 | async-start | bytes 1572864 | tf_op jit(solution)/shard_map/all_to_all | solution.py:241
  570.5 261.4 %reduce-scatter.14.cloned.1.call-start = ((), (), s32[]{:S(2)}) async-start(), calls=%async_computation.21 | async-start | bytes 6488064 | tf_op jit(solution)/shard_map/reduce_scatter | solution.py:308
  576.9 11.8 %copy-start.21 = (s32[1,2048]{1,0:T(1,128)S(1)}, s32[1,2048]{1,0:T(1,128)}, u32[]{:S(2)}) copy-start(s32[1,2048]{1,0:T(1,128)} %param.20) | copy-start | bytes 24580
  576.9 11.7 %copy-start.41 = (s32[4]{0:T(128)S(1)}, s32[4]{0:T(128)}, u32[]{:S(2)}) copy-start(s32[4]{0:T(128)} %copy-done.40) | copy-start | bytes 52
  576.9 342.3 %reduce-scatter.8.cloned.1.call-start = ((), (), s32[]{:S(2)}) async-start(), calls=%async_computation.18 | async-start | bytes 7299072 | tf_op jit(solution)/shard_map/reduce_scatter | solution.py:303
  608.8 6.0 copy-start.2
  637.2 5.8 copy-start.2
  665.4 5.8 copy-start.2
  693.6 6.0 copy-start.2
  751.6 0.9 copy-start.26
  753.0 1.2 copy-start.15
  753.1 1.2 copy-start.28
  753.1 1.2 copy-start.34
  753.2 6.1 copy-start.13
  759.4 1.2 copy-start.6
  759.4 322.0 %reduce-scatter.12.cloned.1.call-start = ((), (), s32[]{:S(2)}) async-start(), calls=%async_computation.20 | async-start | bytes 12976128 | tf_op jit(solution)/shard_map/reduce_scatter | solution.py:307
  769.1 1.4 copy-start.9
  770.6 6.1 copy-start.14
  770.6 6.1 copy-start.39
  776.7 3.4 copy-start.35
  822.0 259.4 %copy-start.1 = (bf16[1,2048,768]{2,1,0:T(8,128)(2,1)S(1)}, bf16[1,2048,768]{2,1,0:T(8,128)(2,1)}, u32[]{:S(2)}) copy-start(bf16[1,2048,768]{2,1,0:T(8,128)(2,1)} %param.31) | copy-start | bytes 9437188
  (2 other events, 1.5 us)
Sparse Core Ops, SparseCore 0:
  10.9 62.9 all-gather.5
  76.9 53.6 all-gather.7
  133.4 68.4 all-gather.9
  357.0 70.5 all-gather.11
  430.0 36.7 reduce-scatter.17
  469.3 58.3 reduce-scatter.15
  563.1 99.4 reduce-scatter.9
  669.8 124.6 reduce-scatter.13
  800.8 118.3 reduce-scatter.7
  926.6 154.6 reduce-scatter.11
where the time goes:
time: 1100 us; the launch traced here: 1090 us
  waiting for transfers between devices  352 us (32%)
  matrix products  280 us (25%)
  blocking collectives  188 us (17%)
  local copies, waits for them, and re-layouts  105 us (10%)
  other arithmetic  99.4 us (9%)
  starting transfers between devices  32.8 us (3%)
  loops' own time  16.1 us (1%)
  between operations  15.3 us (1%)
    reduce_scatter x1, waiting for transfers between devices, on_device(): lax.psum_scatter(sin_grad, ('dp', 'seq'), scatter_dimension=0, tiled=True)  162 us
    reduce_scatter x1, waiting for transfers between devices, on_device(): lax.psum_scatter(qkv_grad, ('dp', 'seq'), scatter_dimension=0, tiled=True)  87.2 us
    unnamed x2, blocking collectives  82.1 us
    all_gather x1, blocking collectives, on_device(): lax.all_gather(router, ('dp', 'seq'), axis=0, tiled=True)  64.1 us
    dot_general x8, matrix products, block_scores(): jnp.einsum('qhd,khd->hqk', q_rows, key_heads, preferred_element_type=jnp....  55.8 us
    all_to_all x1, blocking collectives, on_device(): lax.all_to_all(d_heads.reshape(length, heads_here * 3 * head_dim), 'seq',...  42.2 us
    all_to_all x1, waiting for transfers between devices, on_device(): lax.all_to_all(d_slots, 'dp', split_axis=0, concat_axis=0, tiled=True)  32 us
    dot_general x4, matrix products, forward_block(): jnp.einsum('hqk,khd->qhd', probs.astype(jnp.bfloat16), value_heads, prefe...  29.7 us
  transfers between devices with their start and end apart: 17, of which 8 were waited for; matrix products, arithmetic and copies ran while one was open for 44% of the time, Pallas kernels for 0%

commit v1 on v0

v1 whole, which is shorter than its diff:
```python
import functools

import jax
import jax.numpy as jnp
from jax import lax
from jax.experimental import pallas as pl
from jax.experimental.pallas import tpu as pltpu
from jax.sharding import PartitionSpec as P

HEADS = 12
EPS = 1e-06
BASE = 10000.0
MASKED = -1e30
AXES = ("dp", "seq")
LANES = 128
F32 = jnp.float32
BF16 = jnp.bfloat16
NN = (((1,), (0,)), ((), ()))
NT = (((1,), (1,)), ((), ()))
TN = (((0,), (0,)), ((), ()))


def mm(left, right, dims=NN):
    return lax.dot_general(left, right, dims, preferred_element_type=F32)


def params(steps=0, mib=56):
    semantics = ("arbitrary",) * steps if steps else None
    return pltpu.CompilerParams(dimension_semantics=semantics, vmem_limit_bytes=mib << 20)


def cost(flops, moved):
    return pl.CostEstimate(flops=int(flops), bytes_accessed=int(moved), transcendentals=0)


def whole():
    return pl.BlockSpec(memory_space=pltpu.VMEM)


def pairs(place):
    found = []
    for device in range(32):
        z, y, x, c = device // 8, (device // 4) % 2, (device // 2) % 2, device % 2
        z, y, x, c = place(z, y, x, c)
        found.append((device, ((z * 2 + y) * 2 + x) * 2 + c))
    return found


FLIP = {
    "y": pairs(lambda z, y, x, c: (z, 1 - y, x, c)),
    "x": pairs(lambda z, y, x, c: (z, y, 1 - x, c)),
    "c": pairs(lambda z, y, x, c: (z, y, x, 1 - c)),
}


def turn_z(step):
    return pairs(lambda z, y, x, c: ((z + step) % 4, y, x, c))


def coordinates():
    dp, seq = lax.axis_index("dp"), lax.axis_index("seq")
    return {"z": dp // 2, "y": dp % 2, "x": seq // 2, "c": seq % 2}


def small_torus():
    return lax.axis_size("dp") == 8 and lax.axis_size("seq") == 4


def gather(shard, path):
    if not small_torus():
        return lax.all_gather(shard, AXES, axis=0, tiled=True)
    here = coordinates()
    block, done = shard, []
    for name in path:
        axis = sum(1 for other in done if "zyxc".index(other) < "zyxc".index(name))
        if name == "z":
            grown = jnp.zeros(block.shape[:axis] + (4,) + block.shape[axis:], block.dtype)
            parts = [(here["z"], block)]
            for step in (2, 1, 3):
                came = lax.ppermute(block, AXES, turn_z(-step))
                parts.append(((here["z"] + step) % 4, came))
            for place, part in parts:
                grown = lax.dynamic_update_slice_in_dim(
                    grown, jnp.expand_dims(part, axis), place, axis
                )
            block = grown
        else:
            came = lax.ppermute(block, AXES, FLIP[name])
            block = jnp.where(
                here[name] == 0,
                jnp.stack([block, came], axis),
                jnp.stack([came, block], axis),
            )
        done.append(name)
    return block.reshape((-1,) + shard.shape[1:])


def scatter_sum(grad, path):
    devices = lax.axis_size("dp") * lax.axis_size("seq")
    if not small_torus():
        return lax.psum_scatter(grad, AXES, scatter_dimension=0, tiled=True).astype(F32)
    here = coordinates()
    part = grad.reshape((4, 2, 2, 2, grad.shape[0] // devices) + grad.shape[1:])
    dims = list("zyxc")
    for count, name in enumerate(path):
        axis = dims.index(name)
        if name == "z":
            total = lax.dynamic_index_in_dim(part, here["z"], axis, False).astype(F32)
            for step in (2, 1, 3):
                away = lax.dynamic_index_in_dim(part, (here["z"] + step) % 4, axis, False)
                total = total + lax.ppermute(away, AXES, turn_z(step)).astype(F32)
        else:
            away = lax.dynamic_index_in_dim(part, 1 - here[name], axis, False)
            kept = lax.dynamic_index_in_dim(part, here[name], axis, False)
            total = kept.astype(F32) + lax.ppermute(away, AXES, FLIP[name]).astype(F32)
        part = total if count == 3 else total.astype(BF16)
        dims.pop(axis)
    return part


def copies_sum(parts):
    seq = lax.axis_size("seq")
    if not small_torus():
        flat = parts.reshape((seq * parts.shape[1],) + parts.shape[2:])
        return lax.psum_scatter(flat, "seq", scatter_dimension=0, tiled=True).astype(F32)
    here = coordinates()
    part = parts.reshape((2, 2) + parts.shape[1:])
    away = lax.dynamic_index_in_dim(part, 1 - here["c"], 1, False)
    kept = lax.dynamic_index_in_dim(part, here["c"], 1, False)
    part = (kept.astype(F32) + lax.ppermute(away, AXES, FLIP["c"]).astype(F32)).astype(BF16)
    away = lax.dynamic_index_in_dim(part, 1 - here["x"], 0, False)
    kept = lax.dynamic_index_in_dim(part, here["x"], 0, False)
    return kept.astype(F32) + lax.ppermute(away, AXES, FLIP["x"]).astype(F32)


def swap(blocks, axis):
    return lax.all_to_all(blocks, axis, split_axis=0, concat_axis=0, tiled=True)


def turned(rows, cosine, sine):
    a, b = rows[:32], rows[32:]
    return a * cosine - b * sine, b * cosine + a * sine


def qkv_kernel(x_ref, w1_ref, w2_ref, misc_ref, cos_ref, sin_ref, out_ref, xn_ref):
    step = pl.program_id(0)

    @pl.when(step == 0)
    def _():
        x = x_ref[...].astype(F32)
        r1 = lax.rsqrt(jnp.mean(x * x, axis=1, keepdims=True) + EPS)
        gain = misc_ref[...].astype(F32).T[0:1, :]
        xn_ref[...] = (x * r1 * gain).astype(BF16)

    def project(w_ref):
        rows = mm(xn_ref[...], w_ref[...]).T
        cosine, sine = cos_ref[...], sin_ref[...]
        for base in range(0, rows.shape[0], 192):
            for c in range(2):
                at = base + c * 64
                a, b = turned(rows[at : at + 64], cosine, sine)
                out_ref[at : at + 32, :] = a.astype(BF16)
                out_ref[at + 32 : at + 64, :] = b.astype(BF16)
            out_ref[base + 128 : base + 192, :] = rows[base + 128 : base + 192].astype(BF16)

    @pl.when(step < 3)
    def _():
        project(w1_ref)

    @pl.when(step >= 3)
    def _():
        project(w2_ref)


def qkv_project(x, w1, w2, cosine, sine):
    tokens, width = x.shape
    return pl.pallas_call(
        qkv_kernel,
        grid=(6,),
        in_specs=[
            pl.BlockSpec((tokens, width), lambda i: (0, 0)),
            pl.BlockSpec((width, 384), lambda i: (0, jnp.minimum(i, 2))),
            pl.BlockSpec((width, 384), lambda i: (0, jnp.maximum(i - 3, 0))),
            pl.BlockSpec((width, LANES), lambda i: (0, 9)),
            pl.BlockSpec(cosine.shape, lambda i: (0, 0)),
            pl.BlockSpec(sine.shape, lambda i: (0, 0)),
        ],
        out_specs=pl.BlockSpec((384, tokens), lambda i: (i, 0)),
        out_shape=jax.ShapeDtypeStruct((3 * width, tokens), BF16),
        scratch_shapes=[pltpu.VMEM((tokens, width), BF16)],
        compiler_params=params(1),
        cost_estimate=cost(6 * tokens * width * width, 8 << 20),
        name="qkv_project",
    )(x, w1, w2, w2, cosine, sine)


TILE = 256


def tile_of(ref, row, rows, index):
    per = ref.shape[2] // TILE
    at = (index % per) * TILE
    return ref[index // per, row : row + rows, at : at + TILE]


def flipped(block):
    return block.astype(F32).T.astype(BF16)


def masked(scores, start, i, j, diagonal):
    key = lax.broadcasted_iota(jnp.int32, scores.shape, 0)
    allowed = key >= start - j * TILE
    if diagonal:
        query = lax.broadcasted_iota(jnp.int32, scores.shape, 1)
        allowed = allowed & (key <= query)
    return jnp.where(allowed, scores, MASKED)


def attend_kernel(buf_ref, start_ref, ctx_ref, lse_ref, k_ref, s_ref):
    tiles = buf_ref.shape[0] * buf_ref.shape[2] // TILE
    per = buf_ref.shape[2] // TILE
    for i in range(tiles):
        rows = slice(i * TILE, (i + 1) * TILE)
        k_ref[rows, :] = flipped(tile_of(buf_ref, 64, 64, i))
        q = (tile_of(buf_ref, 0, 64, i).astype(F32) * 0.125).astype(BF16)
        start = start_ref[0:1, rows]
        top = jnp.full((1, TILE), MASKED, F32)
        for j in range(i + 1):
            keys = slice(j * TILE, (j + 1) * TILE)
            scores = masked(mm(k_ref[keys, :], q), start, i, j, i == j)
            s_ref[keys, :] = scores
            top = jnp.maximum(top, jnp.max(scores, axis=0, keepdims=True))
        total = jnp.zeros((1, TILE), F32)
        context = jnp.zeros((64, TILE), F32)
        for j in range(i + 1):
            probs = jnp.exp(s_ref[j * TILE : (j + 1) * TILE, :] - top)
            total = total + jnp.sum(probs, axis=0, keepdims=True)
            context = context + mm(tile_of(buf_ref, 128, 64, j), probs.astype(BF16))
        at = (i % per) * TILE
        ctx_ref[i // per, :, at : at + TILE] = (context / total).astype(BF16)
        lse_ref[0, 0:1, rows] = top + jnp.log(total)


def attend(buf, start):
    blocks, rows, tokens = buf.shape
    heads, length = rows // 192, blocks * tokens
    return pl.pallas_call(
        attend_kernel,
        grid=(heads,),
        in_specs=[
            pl.BlockSpec((blocks, 192, tokens), lambda h: (0, h, 0)),
            pl.BlockSpec((1, length), lambda h: (0, 0)),
        ],
        out_specs=[
            pl.BlockSpec((blocks, 64, tokens), lambda h: (0, h, 0)),
            pl.BlockSpec((1, 1, length), lambda h: (h, 0, 0)),
        ],
        out_shape=[
            jax.ShapeDtypeStruct((blocks, heads * 64, tokens), BF16),
            jax.ShapeDtypeStruct((heads, 1, length), F32),
        ],
        scratch_shapes=[pltpu.VMEM((length, 64), BF16), pltpu.VMEM((length, TILE), F32)],
        compiler_params=params(1),
        cost_estimate=cost(20e9, 4 << 20),
        name="attend",
    )(buf, start)


def attend_back_kernel(
    buf_ref, dctx_ref, ctx_ref, lse_ref, start_ref, out_ref, k_ref, v_ref, q_ref, d_ref, dk_ref, dv_ref
):
    tiles = buf_ref.shape[0] * buf_ref.shape[2] // TILE
    per = buf_ref.shape[2] // TILE
    for i in range(tiles):
        rows = slice(i * TILE, (i + 1) * TILE)
        k_ref[rows, :] = flipped(tile_of(buf_ref, 64, 64, i))
        v_ref[rows, :] = flipped(tile_of(buf_ref, 128, 64, i))
        q_t = (tile_of(buf_ref, 0, 64, i).astype(F32) * 0.125).astype(BF16)
        d_t = tile_of(dctx_ref, 0, 64, i)
        q_rows, d_rows = flipped(q_t), flipped(d_t)
        delta = jnp.sum(
            d_t.astype(F32) * tile_of(ctx_ref, 0, 64, i).astype(F32), axis=0, keepdims=True
        )
        start, log_total = start_ref[0:1, rows], lse_ref[0, 0:1, rows]
        d_query = jnp.zeros((64, TILE), F32)
        for j in range(i + 1):
            keys = slice(j * TILE, (j + 1) * TILE)
            scores = masked(mm(k_ref[keys, :], q_t), start, i, j, i == j)
            probs = jnp.exp(scores - log_total)
            d_probs = mm(v_ref[keys, :], d_t)
            d_scores = (probs * (d_probs - delta)).astype(BF16)
            d_query = d_query + mm(tile_of(buf_ref, 64, 64, j), d_scores)
            d_key = mm(d_scores, q_rows)
            d_value = mm(probs.astype(BF16), d_rows)
            if i == j:
                dk_ref[keys, :] = d_key
                dv_ref[keys, :] = d_value
            else:
                dk_ref[keys, :] += d_key
                dv_ref[keys, :] += d_value
        at = (i % per) * TILE
        out_ref[i // per, 0:64, at : at + TILE] = (d_query * 0.125).astype(BF16)
    for i in range(tiles):
        at = (i % per) * TILE
        rows = slice(i * TILE, (i + 1) * TILE)
        out_ref[i // per, 64:128, at : at + TILE] = dk_ref[rows, :].T.astype(BF16)
        out_ref[i // per, 128:192, at : at + TILE] = dv_ref[rows, :].T.astype(BF16)


def attend_back(buf, dctx, ctx, lse, start):
    blocks, rows, tokens = buf.shape
    heads, length = rows // 192, blocks * tokens
    return pl.pallas_call(
        attend_back_kernel,
        grid=(heads,),
        in_specs=[
            pl.BlockSpec((blocks, 192, tokens), lambda h: (0, h, 0)),
            pl.BlockSpec((blocks, 64, tokens), lambda h: (0, h, 0)),
            pl.BlockSpec((blocks, 64, tokens), lambda h: (0, h, 0)),
            pl.BlockSpec((1, 1, length), lambda h: (h, 0, 0)),
            pl.BlockSpec((1, length), lambda h: (0, 0)),
        ],
        out_specs=pl.BlockSpec((blocks, 192, tokens), lambda h: (0, h, 0)),
        out_shape=jax.ShapeDtypeStruct(buf.shape, BF16),
        scratch_shapes=[pltpu.VMEM((length, 64), BF16)] * 2
        + [pltpu.VMEM((TILE, 64), BF16)] * 2
        + [pltpu.VMEM((length, 64), F32)] * 2,
        compiler_params=params(1),
        cost_estimate=cost(40e9, 6 << 20),
        name="attend_back",
    )(buf, dctx, ctx, lse, start)


def middle_kernel(
    ctx_ref, x_ref, w_ref, misc_ref, pick_ref, routes_ref, hidden_ref, hn_ref, send_ref, gates_ref, *, experts
):
    hidden = x_ref[...].astype(F32) + mm(ctx_ref[...], w_ref[...], TN)
    hidden_ref[...] = hidden
    r2 = lax.rsqrt(jnp.mean(hidden * hidden, axis=1, keepdims=True) + EPS)
    gain = misc_ref[...].astype(F32).T[experts : experts + 1, :]
    hn = (hidden * r2 * gain).astype(BF16)
    hn_ref[...] = hn
    send_ref[...] = mm(pick_ref[...], hn).astype(BF16)
    logits = mm(hn, misc_ref[...])
    lane = lax.broadcasted_iota(jnp.int32, logits.shape, 1)
    first = jnp.sum(jnp.where(lane == routes_ref[:, 0:1], logits, 0.0), axis=1, keepdims=True)
    second = jnp.sum(jnp.where(lane == routes_ref[:, 1:2], logits, 0.0), axis=1, keepdims=True)
    top = jnp.maximum(first, second)
    first, second = jnp.exp(first - top), jnp.exp(second - top)
    total = first + second
    gates_ref[...] = jnp.where(lane == 0, first / total, jnp.where(lane == 1, second / total, 0.0))


def middle(ctx, x, w_attn, misc, pick, routes, experts):
    tokens, width = x.shape
    slots = pick.shape[0]
    return pl.pallas_call(
        functools.partial(middle_kernel, experts=experts),
        in_specs=[whole()] * 6,
        out_specs=[whole()] * 4,
        out_shape=[
            jax.ShapeDtypeStruct((tokens, width), F32),
            jax.ShapeDtypeStruct((tokens, width), BF16),
            jax.ShapeDtypeStruct((slots, width), BF16),
            jax.ShapeDtypeStruct((tokens, LANES), F32),
        ],
        compiler_params=params(),
        cost_estimate=cost(2e9, 8 << 20),
        name="middle",
    )(ctx, x, w_attn, misc, pick, routes)


def swiglu(gate, up, d_act):
    sigma = jax.nn.sigmoid(gate)
    act = (gate * sigma * up).astype(BF16)
    d_gate = (d_act * up * sigma * (1.0 + gate * (1.0 - sigma))).astype(BF16)
    d_up = (d_act * gate * sigma).astype(BF16)
    return act, d_gate, d_up


def dense_kernel(
    x_ref, dy_ref, wg_ref, wu_ref, wo_ref, y_ref, dx_ref, gg_ref, gu_ref, go_ref, xt_ref
):
    @pl.when(pl.program_id(0) == 0)
    def _():
        y_ref[...] = jnp.zeros_like(y_ref)
        dx_ref[...] = jnp.zeros_like(dx_ref)
        xt_ref[...] = flipped(x_ref[...])

    x, dy = x_ref[...], dy_ref[...]
    act, d_gate, d_up = swiglu(mm(x, wg_ref[...]), mm(x, wu_ref[...]), mm(dy, wo_ref[...], NT))
    y_ref[...] += mm(act, wo_ref[...])
    dx_ref[...] += mm(d_gate, wg_ref[...], NT) + mm(d_up, wu_ref[...], NT)
    gg_ref[...] = mm(xt_ref[...], d_gate).astype(BF16)
    gu_ref[...] = mm(xt_ref[...], d_up).astype(BF16)
    go_ref[...] = mm(act, dy, TN).astype(BF16)


def dense(x, dy, w_gate, w_up, w_out, tile=256):
    tokens, width = x.shape
    units = w_out.shape[0]
    rows = pl.BlockSpec((tokens, width), lambda j: (0, 0))
    tall = pl.BlockSpec((width, tile), lambda j: (0, j))
    wide = pl.BlockSpec((tile, width), lambda j: (j, 0))
    return pl.pallas_call(
        dense_kernel,
        grid=(units // tile,),
        in_specs=[rows, rows, tall, tall, wide],
        out_specs=[rows, rows, tall, tall, wide],
        out_shape=[
            jax.ShapeDtypeStruct((tokens, width), F32),
            jax.ShapeDtypeStruct((tokens, width), F32),
            jax.ShapeDtypeStruct((width, units), BF16),
            jax.ShapeDtypeStruct((width, units), BF16),
            jax.ShapeDtypeStruct((units, width), BF16),
        ],
        scratch_shapes=[pltpu.VMEM((width, tokens), BF16)],
        compiler_params=params(1),
        cost_estimate=cost(18 * tokens * width * units, 30 << 20),
        name="dense",
    )(x, dy, w_gate, w_up, w_out)


def expert_kernel(
    own_ref, x_ref, dy_ref, other_ref, misc_ref, wg_ref, wu_ref, wo_ref,
    y_ref, dx_ref, dgate_ref, deo_ref, act_ref, dg_ref, du_ref, y_acc, dx_acc,
):
    step = pl.program_id(0)

    @pl.when(step == 0)
    def _():
        y_acc[...] = jnp.zeros_like(y_acc)
        dx_acc[...] = jnp.zeros_like(dx_acc)
        logits = mm(x_ref[...], misc_ref[...])
        lane = lax.broadcasted_iota(jnp.int32, logits.shape, 1)
        other = other_ref[...].astype(jnp.int32)
        mine = jnp.sum(jnp.where(lane == own_ref[0], logits, 0.0), axis=1, keepdims=True)
        theirs = jnp.sum(jnp.where(lane == other, logits, 0.0), axis=1, keepdims=True)
        top = jnp.maximum(mine, theirs)
        mine, theirs = jnp.exp(mine - top), jnp.exp(theirs - top)
        deo_ref[...] = (mine / (mine + theirs) * dy_ref[...].astype(F32)).astype(BF16)

    x, deo = x_ref[...], deo_ref[...]
    wg, wu, wo = wg_ref[0], wu_ref[0], wo_ref[0]
    act, d_gate, d_up = swiglu(mm(x, wg), mm(x, wu), mm(deo, wo, NT))
    y_acc[...] += mm(act, wo)
    dx_acc[...] += mm(d_gate, wg, NT) + mm(d_up, wu, NT)
    act_ref[...] = act
    dg_ref[...] = d_gate
    du_ref[...] = d_up

    @pl.when(step == pl.num_programs(0) - 1)
    def _():
        y = y_acc[...].astype(BF16)
        y_ref[...] = y
        dx_ref[...] = dx_acc[...].astype(BF16)
        dgate_ref[...] = jnp.sum(y.astype(F32) * dy_ref[...].astype(F32), axis=1, keepdims=True)


def expert(own, x, dy, other, misc, w_in, w_out, tile=256):
    slots, width = x.shape
    units = w_out.shape[1]
    steps = units // tile
    rows = pl.BlockSpec((slots, width), lambda j, s: (0, 0))
    column = pl.BlockSpec((slots, 1), lambda j, s: (0, 0))
    saved = pl.BlockSpec((slots, tile), lambda j, s: (0, j))
    return pl.pallas_call(
        expert_kernel,
        grid_spec=pltpu.PrefetchScalarGridSpec(
            num_scalar_prefetch=1,
            grid=(steps,),
            in_specs=[
                rows,
                rows,
                column,
                pl.BlockSpec(misc.shape, lambda j, s: (0, 0)),
                pl.BlockSpec((1, width, tile), lambda j, s: (0, 0, j)),
                pl.BlockSpec((1, width, tile), lambda j, s: (0, 0, j + steps)),
                pl.BlockSpec((1, tile, width), lambda j, s: (0, j, 0)),
            ],
            out_specs=[rows, rows, column, rows, saved, saved, saved],
            scratch_shapes=[pltpu.VMEM((slots, width), F32)] * 2,
        ),
        out_shape=[
            jax.ShapeDtypeStruct((slots, width), BF16),
            jax.ShapeDtypeStruct((slots, width), BF16),
            jax.ShapeDtypeStruct((slots, 1), F32),
            jax.ShapeDtypeStruct((slots, width), BF16),
        ]
        + [jax.ShapeDtypeStruct((slots, units), BF16)] * 3,
        compiler_params=params(1),
        cost_estimate=cost(12 * slots * width * units, 40 << 20),
        name="expert",
    )(own, x, dy, other, misc, w_in, w_in, w_out)


def expert_grads_kernel(x_ref, deo_ref, act_ref, dg_ref, du_ref, gg_ref, gu_ref, go_ref, xt_ref):
    @pl.when(pl.program_id(0) == 0)
    def _():
        xt_ref[...] = flipped(x_ref[...])

    gg_ref[0] = mm(xt_ref[...], dg_ref[...]).astype(BF16)
    gu_ref[0] = mm(xt_ref[...], du_ref[...]).astype(BF16)
    go_ref[0] = mm(act_ref[...], deo_ref[...], TN).astype(BF16)


def expert_grads(x, deo, act, d_gate, d_up, copies, tile=256):
    slots, width = x.shape
    units = act.shape[1]
    rows = pl.BlockSpec((slots, width), lambda j: (0, 0))
    saved = pl.BlockSpec((slots, tile), lambda j: (0, j))
    in_part, out_part = 2 * units // copies, units // copies
    in_steps, out_steps = in_part // tile, out_part // tile
    in_spec = pl.BlockSpec((1, width, tile), lambda j: (j // in_steps, 0, j % in_steps))
    return pl.pallas_call(
        expert_grads_kernel,
        grid=(units // tile,),
        in_specs=[rows, rows, saved, saved, saved],
        out_specs=[
            in_spec,
            in_spec,
            pl.BlockSpec((1, tile, width), lambda j: (j // out_steps, j % out_steps, 0)),
        ],
        out_shape=[
            jax.ShapeDtypeStruct((copies // 2, width, in_part), BF16),
            jax.ShapeDtypeStruct((copies // 2, width, in_part), BF16),
            jax.ShapeDtypeStruct((copies, out_part, width), BF16),
        ],
        scratch_shapes=[pltpu.VMEM((width, slots), BF16)],
        compiler_params=params(1),
        cost_estimate=cost(6 * slots * width * units, 30 << 20),
        name="expert_grads",
    )(x, deo, act, d_gate, d_up)


def middle_back_kernel(
    dhn_ref, back_ref, slots_ref, routes_ref, dgate_ref, gates_ref, misc_ref, hidden_ref, hn_ref,
    dy_ref, ctx_ref, w_ref, dh_ref, dctx_ref, grad_ref, *, experts,
):
    tokens = dhn_ref.shape[0]
    slots = back_ref.shape[0]
    place = lax.broadcasted_iota(jnp.int32, (tokens, slots), 1)
    is0, is1 = place == slots_ref[:, 0:1], place == slots_ref[:, 1:2]
    came = mm(jnp.where(is0 | is1, 1.0, 0.0).astype(BF16), back_ref[...])
    dgate = dgate_ref[...]
    dg0 = jnp.sum(jnp.where(is0, dgate, 0.0), axis=1, keepdims=True)
    dg1 = jnp.sum(jnp.where(is1, dgate, 0.0), axis=1, keepdims=True)
    g0, g1 = gates_ref[:, 0:1], gates_ref[:, 1:2]
    mean = g0 * dg0 + g1 * dg1
    lane = lax.broadcasted_iota(jnp.int32, (tokens, LANES), 1)
    dlogits = (
        jnp.where(lane == routes_ref[:, 0:1], g0 * (dg0 - mean), 0.0)
        + jnp.where(lane == routes_ref[:, 1:2], g1 * (dg1 - mean), 0.0)
    ).astype(BF16)
    misc = misc_ref[...]
    dhn = dhn_ref[...] + mm(dlogits, misc, NT) + came
    hidden = hidden_ref[...]
    r2 = lax.rsqrt(jnp.mean(hidden * hidden, axis=1, keepdims=True) + EPS)
    z2 = hidden * r2
    gain = misc.astype(F32).T[experts : experts + 1, :]
    gain_grad = jnp.sum(dhn * z2, axis=0, keepdims=True)
    dz2 = dhn * gain
    dh = dy_ref[...].astype(F32) + r2 * (dz2 - z2 * jnp.mean(dz2 * z2, axis=1, keepdims=True))
    dh_ref[...] = dh
    dhb = dh.astype(BF16)
    dctx_ref[...] = mm(w_ref[...], dhb, NT).astype(BF16)
    width = w_ref.shape[0]
    grad_ref[:, :width] = mm(ctx_ref[...], dhb).astype(BF16)
    small = mm(dlogits, hn_ref[...], TN)
    row = lax.broadcasted_iota(jnp.int32, small.shape, 0)
    small = jnp.where(row == experts, gain_grad, small)
    grad_ref[:, width:] = small.T.astype(BF16)


def middle_back(dhn, back, slots, routes, dgate, gates, misc, hidden, hn, dy, ctx, w_attn, experts):
    tokens, width = hidden.shape
    return pl.pallas_call(
        functools.partial(middle_back_kernel, experts=experts),
        in_specs=[whole()] * 12,
        out_specs=[whole()] * 3,
        out_shape=[
            jax.ShapeDtypeStruct((tokens, width), F32),
            jax.ShapeDtypeStruct((width, tokens), BF16),
            jax.ShapeDtypeStruct((width, width + LANES), BF16),
        ],
        compiler_params=params(),
        cost_estimate=cost(3e9, 16 << 20),
        name="middle_back",
    )(dhn, back, slots, routes, dgate, gates, misc, hidden, hn, dy, ctx, w_attn)


def output_kernel(hidden_ref, dense_ref, came_ref, slots_ref, gates_ref, out_ref):
    tokens, slots = hidden_ref.shape[0], came_ref.shape[0]
    place = lax.broadcasted_iota(jnp.int32, (tokens, slots), 1)
    mixture = jnp.zeros(hidden_ref.shape, F32)
    for k in range(2):
        pick = jnp.where(place == slots_ref[:, k : k + 1], 1.0, 0.0).astype(BF16)
        mixture = mixture + gates_ref[:, k : k + 1] * mm(pick, came_ref[...])
    out_ref[...] = hidden_ref[...] + dense_ref[...] + mixture


def output_of(hidden, shared, came, slots, gates):
    return pl.pallas_call(
        output_kernel,
        in_specs=[whole()] * 5,
        out_specs=whole(),
        out_shape=jax.ShapeDtypeStruct(hidden.shape, F32),
        compiler_params=params(),
        cost_estimate=cost(2e9, 8 << 20),
        name="output_of",
    )(hidden, shared, came, slots, gates)


def qkv_back_kernel(
    x_ref, dqkv_ref, w1_ref, w2_ref, misc_ref, cos_ref, sin_ref, dh_ref,
    dx_ref, g1_ref, g2_ref, small_ref, xt_ref, acc_ref,
):
    step = pl.program_id(0)

    def gain_row():
        return misc_ref[...].astype(F32).T[0:1, :]

    def z_of():
        x = x_ref[...].astype(F32)
        r1 = lax.rsqrt(jnp.mean(x * x, axis=1, keepdims=True) + EPS)
        return x * r1, r1

    @pl.when(step == 0)
    def _():
        z1, _ = z_of()
        xt_ref[...] = flipped((z1 * gain_row()).astype(BF16))
        acc_ref[...] = jnp.zeros_like(acc_ref)

    cosine, sine = cos_ref[...], -sin_ref[...]
    pieces = []
    for base in range(0, dqkv_ref.shape[0], 192):
        for c in range(2):
            at = base + c * 64
            pieces.extend(turned(dqkv_ref[at : at + 64, :].astype(F32), cosine, sine))
        pieces.append(dqkv_ref[base + 128 : base + 192, :].astype(F32))
    d_rows = jnp.concatenate(pieces, axis=0).T.astype(BF16)

    def back(w_ref, g_ref):
        acc_ref[...] += mm(d_rows, w_ref[...], NT)
        g_ref[...] = mm(xt_ref[...], d_rows).astype(BF16)

    @pl.when(step < 3)
    def _():
        back(w1_ref, g1_ref)

    @pl.when(step >= 3)
    def _():
        back(w2_ref, g2_ref)

    @pl.when(step == 5)
    def _():
        z1, r1 = z_of()
        dxn = acc_ref[...]
        total = jnp.sum(dxn * z1, axis=0, keepdims=True)
        row = lax.broadcasted_iota(jnp.int32, (LANES, total.shape[1]), 0)
        small_ref[...] = jnp.where(row == 0, total, 0.0).T.astype(BF16)
        dz1 = dxn * gain_row()
        dx_ref[...] = dh_ref[...] + r1 * (dz1 - z1 * jnp.mean(dz1 * z1, axis=1, keepdims=True))


def qkv_back(x, dqkv, w1, w2, cosine, sine, dh):
    tokens, width = x.shape
    rows = pl.BlockSpec((tokens, width), lambda i: (0, 0))
    half = 3 * width // 2
    return pl.pallas_call(
        qkv_back_kernel,
        grid=(6,),
        in_specs=[
            rows,
            pl.BlockSpec((384, tokens), lambda i: (i, 0)),
            pl.BlockSpec((width, 384), lambda i: (0, jnp.minimum(i, 2))),
            pl.BlockSpec((width, 384), lambda i: (0, jnp.maximum(i - 3, 0))),
            pl.BlockSpec((width, LANES), lambda i: (0, 9)),
            pl.BlockSpec(cosine.shape, lambda i: (0, 0)),
            pl.BlockSpec(sine.shape, lambda i: (0, 0)),
            rows,
        ],
        out_specs=[
            rows,
            pl.BlockSpec((width, 384), lambda i: (0, jnp.minimum(i, 2))),
            pl.BlockSpec((width, 384), lambda i: (0, jnp.maximum(i - 3, 0))),
            pl.BlockSpec((width, LANES), lambda i: (0, 0)),
        ],
        out_shape=[
            jax.ShapeDtypeStruct((tokens, width), F32),
            jax.ShapeDtypeStruct((width, half), BF16),
            jax.ShapeDtypeStruct((width, half), BF16),
            jax.ShapeDtypeStruct((width, LANES), BF16),
        ],
        scratch_shapes=[pltpu.VMEM((width, tokens), BF16), pltpu.VMEM((tokens, width), F32)],
        compiler_params=params(1),
        cost_estimate=cost(12 * tokens * width * width, 16 << 20),
        name="qkv_back",
    )(x, dqkv, w1, w2, w2, cosine, sine, dh)


def slot_plan(routes, order, experts, capacity):
    before = (order[:, None] > order[None, :]).astype(BF16)
    ids = jnp.arange(experts, dtype=jnp.int32)
    first = (routes[:, 0:1] == ids).astype(BF16)
    second = (routes[:, 1:2] == ids).astype(BF16)
    earlier = mm(before, jnp.concatenate([first, second], axis=1))
    every = jnp.sum(first.astype(F32), axis=0, keepdims=True)
    place0 = jnp.sum(earlier[:, :experts] * first.astype(F32), axis=1)
    place1 = jnp.sum((earlier[:, experts:] + every) * second.astype(F32), axis=1)
    place = jnp.stack([place0, place1], axis=1).astype(jnp.int32)
    return jnp.where(place < capacity, routes * capacity + place, experts * capacity)


def padded(shard, columns):
    return jnp.pad(shard, ((0, 0), (0, columns - shard.shape[1])))


def on_device(
    layer_input, cotangent, segments, routes, order, norm1_gain, attn_qkv, attn_out,
    norm2_gain, router, shared_in, shared_out, expert_in, expert_out,
):
    tokens, width = layer_input.shape
    seq_devs = lax.axis_size("seq")
    experts = lax.axis_size("dp")
    capacity = max(2, (18 * tokens + 8 * experts - 1) // (8 * experts))
    slots = experts * capacity
    half = 3 * width // 2
    units = shared_in.shape[1] // 2

    w1 = gather(attn_qkv[:, :half], "zyxc")
    w2 = gather(
        jnp.concatenate([attn_qkv[:, half:], padded(norm1_gain[:, None], LANES)], axis=1), "zxyc"
    )
    gate_shard, up_shard, out_shard, w1, w2 = lax.optimization_barrier(
        (
            shared_in[:, :units],
            jnp.concatenate(
                [
                    shared_in[:, units:],
                    attn_out,
                    padded(jnp.concatenate([router, norm2_gain[:, None]], axis=1), LANES),
                ],
                axis=1,
            ),
            shared_out,
            w1,
            w2,
        )
    )
    w_up = gather(up_shard, "zxyc")
    w_gate = gather(gate_shard, "zyxc")
    w_out = gather(out_shard, "zxyc")
    w_attn = w_up[:, units : units + width]
    misc = w_up[:, units + width :]

    slot_of = slot_plan(routes, order, experts, capacity)
    every_slot = jnp.arange(slots, dtype=jnp.int32)[:, None]
    slot_rows = slot_of.T
    in0, in1 = every_slot == slot_rows[0:1], every_slot == slot_rows[1:2]
    pick = (in0 | in1).astype(BF16)
    routes_f = routes.astype(F32)
    other = jnp.sum(
        jnp.where(in0, routes_f[:, 1][None, :], 0.0) + jnp.where(in1, routes_f[:, 0][None, :], 0.0),
        axis=1,
    )
    dy_send = mm(pick, cotangent).astype(BF16)
    dy_send, other, w1 = lax.optimization_barrier((dy_send, other, w1))
    dy_rows = swap(dy_send.reshape(experts, capacity, width), "dp").reshape(slots, width)
    other = swap(other.reshape(experts, capacity), "dp").reshape(slots, 1)

    frequency = BASE ** (-(jnp.arange(32, dtype=F32) * 2.0 / 64))
    places = lax.axis_index("seq") * tokens + jnp.arange(tokens, dtype=jnp.int32)
    angles = places.astype(F32)[None, :] * frequency[:, None]
    cosine, sine = jnp.cos(angles), jnp.sin(angles)
    docs = segments[0]
    start = jnp.zeros_like(docs)
    for doc in range(1, 4):
        start = jnp.where(docs >= doc, jnp.sum((docs < doc).astype(jnp.int32)), start)
    start = start[None, :]
    qkv = qkv_project(layer_input, w1, w2, cosine, sine)
    heads = swap(qkv.reshape(seq_devs, -1, tokens), "seq")
    ctx_heads, log_totals = attend(heads, start)
    ctx = swap(ctx_heads, "seq").reshape(width, tokens)
    hidden, hn, send, gates = middle(ctx, layer_input, w_attn, misc, pick, routes, experts)

    rows = swap(send.reshape(experts, capacity, width), "dp").reshape(slots, width)
    shared, dhn, grad_gate, grad_up, grad_out = dense(hn, cotangent, w_gate, w_up, w_out)
    own = lax.axis_index("dp").astype(jnp.int32)[None]
    eo, dxe, dgate, deo, act, d_gate, d_up = expert(
        own, rows, dy_rows, other, misc, expert_in, expert_out
    )
    dgate = swap(dgate.reshape(experts, capacity), "dp").reshape(1, slots)
    back = swap(dxe.reshape(experts, capacity, width), "dp").reshape(slots, width)
    ein_gate, ein_up, ein_out = expert_grads(rows, deo, act, d_gate, d_up, seq_devs)
    dh, dctx, grad_attn = middle_back(
        dhn, back, slot_of, routes, dgate, gates, misc, hidden, hn, cotangent, ctx, w_attn, experts
    )

    dctx_heads = swap(dctx.reshape(seq_devs, -1, tokens), "seq")
    d_heads = attend_back(heads, dctx_heads, ctx_heads, log_totals, start)
    came = swap(eo.reshape(experts, capacity, width), "dp").reshape(slots, width)
    layer_output = output_of(hidden, shared, came, slot_of, gates)
    dqkv = swap(d_heads, "seq").reshape(3 * width, tokens)
    input_grad, grad_q1, grad_q2, grad_small = qkv_back(
        layer_input, dqkv, w1, w2, cosine, sine, dh
    )

    ein_part = copies_sum(jnp.concatenate([ein_gate, ein_up], axis=0))
    eout_part = copies_sum(ein_out)
    sum_gate = scatter_sum(grad_gate, "cxyz")
    sum_up = scatter_sum(grad_up, "cyxz")
    sum_out = scatter_sum(grad_out, "cxyz")
    sum_attn = scatter_sum(grad_attn, "cyxz")
    sum_q1 = scatter_sum(grad_q1, "cxyz")
    sum_q2 = scatter_sum(jnp.concatenate([grad_q2, grad_small], axis=1), "cyxz")
    return (
        layer_output,
        input_grad,
        sum_q2[:, half],
        jnp.concatenate([sum_q1, sum_q2[:, :half]], axis=1),
        sum_attn[:, :width],
        sum_attn[:, width + experts],
        sum_attn[:, width : width + experts],
        jnp.concatenate([sum_gate, sum_up], axis=1),
        sum_out,
        ein_part[None],
        eout_part[None],
    )


def solution(mesh):
    rows = P(AXES, None)
    return jax.shard_map(
        on_device,
        mesh=mesh,
        in_specs=(
            rows, rows, P("dp", None), rows, P(AXES), P(AXES), rows, rows,
            P(AXES), rows, rows, rows, P("dp", None, None), P("dp", None, None),
        ),
        out_specs=(
            rows, rows, P(AXES), rows, rows, P(AXES), rows, rows, rows,
            P("dp", None, "seq"), P("dp", "seq", None),
        ),
        check_vma=False,
    )
```

time: 1100 us -> 644 us (0.59)
  matrix products: 280 us -> 3.56 us
  blocking collectives: 188 us -> 9.66 us
  Pallas kernels: 0 us -> 166 us
  waiting for transfers between devices: 352 us -> 205 us
  starting transfers between devices: 32.8 us -> 139 us
  local copies, waits for them, and re-layouts: 105 us -> 46.6 us
  other arithmetic: 99.4 us -> 63.1 us
  loops' own time: 16.1 us -> 0 us
  between operations: 15.3 us -> 2.41 us
    dot_general x49 -> x2, matrix products: 280 us -> 3.56 us  [mm(): return lax.dot_general(left, right, dims, preferred_element_type=F32)]
    reduce_scatter x6 -> x0, waiting for transfers between devices: 249 us -> none  [the longest x1 162 us: on_device(): lax.psum_scatter(sin_grad, ('dp', 'seq'), scatter_dimension=0, tiled=True)]
    pallas_call x0 -> x10, Pallas kernels: none -> 166 us  [the longest x1 33.9 us: expert(): pl.pallas_call(expert_kernel, grid_spec=pltpu.PrefetchScalarGridSpec(num_...]
    ppermute x0 -> x70, waiting for transfers between devices: none -> 158 us  [the longest x15 61.1 us: gather(): came = lax.ppermute(block, AXES, FLIP[name])]
    ppermute x0 -> x70, starting transfers between devices: none -> 101 us  [the longest x18 44.5 us: scatter_sum(): total = total + lax.ppermute(away, AXES, turn_z(step)).astype(F32)]
    unnamed x2 -> x0, blocking collectives: 82.1 us -> none
    all_gather x1 -> x0, blocking collectives: 64.1 us -> none  [on_device(): lax.all_gather(router, ('dp', 'seq'), axis=0, tiled=True)]
    reduce_sum x12 -> x4, other arithmetic: 44.1 us -> 2.16 us  [the longest x1 1.4 us: on_device(): jnp.sum((docs < doc).astype(jnp.int32))]
  transfers between devices with their start and end apart: 17 -> 79, of which waited for: 8 -> 30; matrix products, arithmetic and copies ran while one was open for 44% -> 15% of each run, Pallas kernels for 0% -> 22%
where the time goes in v1:
time: 644 us; the launch traced here: 635 us
  waiting for transfers between devices  205 us (32%)
  Pallas kernels  166 us (26%)
  starting transfers between devices  139 us (22%)
  other arithmetic  63.1 us (10%)
  local copies, waits for them, and re-layouts  46.6 us (7%)
  blocking collectives  9.66 us (2%)
    ppermute x15, waiting for transfers between devices, gather(): came = lax.ppermute(block, AXES, FLIP[name])  61.1 us
    ppermute x18, waiting for transfers between devices, scatter_sum(): total = kept.astype(F32) + lax.ppermute(away, AXES, FLIP[name]).astype(F32)  55.7 us
    all_to_all x9, waiting for transfers between devices, swap(): return lax.all_to_all(blocks, axis, split_axis=0, concat_axis=0, tiled=True)  47.1 us
    ppermute x18, starting transfers between devices, scatter_sum(): total = total + lax.ppermute(away, AXES, turn_z(step)).astype(F32)  44.5 us
    all_to_all x9, starting transfers between devices, swap(): return lax.all_to_all(blocks, axis, split_axis=0, concat_axis=0, tiled=True)  37.5 us
    pallas_call x1, Pallas kernels, expert(): pl.pallas_call(expert_kernel, grid_spec=pltpu.PrefetchScalarGridSpec(num_...  33.9 us
    pallas_call x1, Pallas kernels, attend_back(): pl.pallas_call(attend_back_kernel, grid=(heads,), in_specs=[pl.BlockSpec(...  33.1 us
    ppermute x15, starting transfers between devices, gather(): came = lax.ppermute(block, AXES, turn_z(-step))  23.1 us
  transfers between devices with their start and end apart: 79, of which 30 were waited for; matrix products, arithmetic and copies ran while one was open for 15% of the time, Pallas kernels for 22%

profile of v1, /device:TPU:0, one launch (start us, length us, event | category | flops | bytes accessed | tf_op | source)
XLA Modules:
  0.0 635.3 jit_solution(2064367311916802701)
XLA Ops:
  1.5 5.1 collective-permute-start.1
  8.4 2.9 collective-permute-start.7
  22.7 2.4 convolution_convert_fusion
  26.2 2.6 compare_select_fusion.2.start_ref
  32.0 4.3 collective-permute-done.8
  38.7 6.5 %collective-permute-done.9 = bf16[4,24,1280]{2,1,0:T(8,128)(2,1)S(1)} collective-permute-done((bf16[4,24,1280]{2,1,0:T(8,128)(2,1)S(1)}, bf16[4,24,1280]{2,1,0:T(8,128)(2,1)S(1)}, u32[]{:S(2)}, u32[]{:S(2)}) %collective-permute-start.9) | collective-permute-done | bytes 245792 | tf_op jit(solution)/shard_map/ppermute | solution.py:88
  47.0 4.0 collective-permute-done.4
  51.6 2.6 collective-permute-done.10
  58.5 3.8 collective-permute-start.19
  62.9 3.3 collective-permute-start.25
  66.3 8.2 %qkv_project.1 = bf16[2304,512]{1,0:T(8,128)(2,1)} custom-call(bf16[512,768]{1,0:T(8,128)(2,1)} %x_ref.5, bf16[768,1152]{1,0:T(8,128)(2,1)} %bitcast.321, bf16[768,1280]{1,0:T(8,128)(2,1)} %bitcast.309, bf16[768,1280]{1,0:T(8,128)(2,1)} %bitcast.310, f32[32,512]{1,0:T(8,128)} %get-tuple-element.204.cos_ref, f32[32,512]{1,0:T(8,128)} %get-tuple-element.203.sin_ref), custom_call_target="tpu_custom_call" | custom-call | flops 1811939328 | bytes 8388608 | tf_op jit(solution)/shard_map/qkv_project/pallas_call | solution.py:177
  74.5 4.5 all-to-all-start
  80.3 6.1 collective-permute-done.24
  86.4 4.0 collective-permute-start.13
  94.0 7.1 %collective-permute-done.12 = bf16[24,2944]{1,0:T(8,128)(2,1)S(1)} collective-permute-done((bf16[24,2944]{1,0:T(8,128)(2,1)S(1)}, bf16[24,2944]{1,0:T(8,128)(2,1)S(1)}, u32[]{:S(2)}, u32[]{:S(2)}) %collective-permute-start.12) | collective-permute-done | bytes 141344 | tf_op jit(solution)/shard_map/ppermute | solution.py:80
  102.7 13.7 %collective-permute-done.27 = bf16[4,64,768]{2,1,0:T(8,128)(2,1)S(1)} collective-permute-done((bf16[4,64,768]{2,1,0:T(8,128)(2,1)S(1)}, bf16[4,64,768]{2,1,0:T(8,128)(2,1)S(1)}, u32[]{:S(2)}, u32[]{:S(2)}) %collective-permute-start.27) | collective-permute-done | bytes 393248 | tf_op jit(solution)/shard_map/ppermute | solution.py:88
  118.7 9.7 %collective-permute-done.15 = bf16[4,24,2944]{2,1,0:T(8,128)(2,1)S(1)} collective-permute-done((bf16[4,24,2944]{2,1,0:T(8,128)(2,1)S(1)}, bf16[4,24,2944]{2,1,0:T(8,128)(2,1)S(1)}, u32[]{:S(2)}, u32[]{:S(2)}) %collective-permute-start.15) | collective-permute-done | bytes 565280 | tf_op jit(solution)/shard_map/ppermute | solution.py:88
  130.8 6.2 collective-permute-done.28
  138.3 6.5 %collective-permute-done.22 = bf16[4,2,24,2048]{3,2,1,0:T(8,128)(2,1)S(1)} collective-permute-done((bf16[4,2,24,2048]{3,2,1,0:T(8,128)(2,1)S(1)}, bf16[4,2,24,2048]{3,2,1,0:T(8,128)(2,1)S(1)}, u32[]{:S(2)}, u32[]{:S(2)}) %collective-permute-start.22) | collective-permute-done | bytes 786464 | tf_op jit(solution)/shard_map/ppermute | solution.py:88
  148.2 11.2 %collective-permute-done.16 = bf16[4,2,24,2944]{3,2,1,0:T(8,128)(2,1)S(1)} collective-permute-done((bf16[4,2,24,2944]{3,2,1,0:T(8,128)(2,1)S(1)}, bf16[4,2,24,2944]{3,2,1,0:T(8,128)(2,1)S(1)}, u32[]{:S(2)}, u32[]{:S(2)}) %collective-permute-start.16) | collective-permute-done | bytes 1130528 | tf_op jit(solution)/shard_map/ppermute | solution.py:88
  161.1 17.2 %attend.1 = (bf16[4,192,512]{2,1,0:T(8,128)(2,1)}, f32[3,1,2048]{2,1,0:T(1,128)}) custom-call(bf16[4,576,512]{2,1,0:T(8,128)(2,1)} %all-to-all-done.buf_ref, s32[1,2048]{1,0:T(1,128)} %compare_select_fusion.2.start_ref), custom_call_target="tpu_custom_call" | custom-call | flops 20000000000 | bytes 4194304 | tf_op jit(solution)/shard_map/attend/pallas_call | solution.py:247
  178.3 3.7 all-to-all-start.1
  185.5 3.7 maximum_select_fusion.2
  189.2 3.6 maximum_select_fusion.1
  192.8 3.3 maximum_select_fusion
  200.3 5.9 middle.1
  206.2 20.7 %dense.1 = (f32[512,768]{1,0:T(8,128)}, f32[512,768]{1,0:T(8,128)}, bf16[768,2048]{1,0:T(8,128)(2,1)}, bf16[768,2048]{1,0:T(8,128)(2,1)}, bf16[2048,768]{1,0:T(8,128)(2,1)}) custom-call(bf16[512,768]{1,0:T(8,128)(2,1)} %get-tuple-element.53.x_ref.hn_ref, bf16[512,768]{1,0:T(8,128)(2,1)} %dy_ref.3, bf16[768,2048]{1,0:T(8,128)(2,1)} %bitcast.336, ...), custom_call_target="tpu_custom_call" | custom-call | flops 14495514624 | bytes 31457280 | tf_op jit(solution)/shard_map/dense/pallas_call | solution.py:405
  229.8 9.7 %all_to_all.59 = f32[8,1,144]{2,1,0:T(1,128)S(1)} all-to-all(f32[8,1,144]{2,1,0:T(1,128)S(1)} %all_to_all.40), channel_id=1, replica_groups=mesh['dp'=8,'seq'=4] {'dp'}, dimensions={0} | all-to-all | bytes 9216 | tf_op jit(solution)/shard_map/all_to_all | solution.py:137
  239.5 4.3 all-to-all-start.3
  243.8 3.4 constant_dynamic-slice_fusion.3
  265.2 18.9 %all-to-all-done.3 = bf16[8,144,768]{2,1,0:T(8,128)(2,1)} async-done(((bf16[8,144,768]{2,1,0:T(8,128)(2,1)}), bf16[8,144,768]{2,1,0:T(8,128)(2,1)}, u32[]{:S(2)}, u32[]{:S(2)}) %all-to-all-start.3) | async-done | bytes 1769504 | tf_op jit(solution)/shard_map/all_to_all | solution.py:137
  284.0 4.3 all-to-all-start.2
  297.0 22.4 %collective-permute-done.50 = bf16[4,24,2048]{2,1,0:T(8,128)(2,1)S(1)} collective-permute-done((bf16[4,24,2048]{2,1,0:T(8,128)(2,1)S(1)}, bf16[4,24,2048]{2,1,0:T(8,128)(2,1)S(1)}, u32[]{:S(2)}, u32[]{:S(2)}) %collective-permute-start.50) | collective-permute-done | bytes 393248 | tf_op jit(solution)/shard_map/ppermute | solution.py:115
  320.4 3.2 collective-permute-start.53
  327.7 9.7 %all-to-all-done.2 = bf16[8,144,768]{2,1,0:T(8,128)(2,1)} async-done(((bf16[8,144,768]{2,1,0:T(8,128)(2,1)}), bf16[8,144,768]{2,1,0:T(8,128)(2,1)}, u32[]{:S(2)}, u32[]{:S(2)}) %all-to-all-start.2) | async-done | bytes 1769504 | tf_op jit(solution)/shard_map/all_to_all | solution.py:137
  337.4 33.9 %expert.1 = (bf16[1152,768]{1,0:T(8,128)(2,1)}, bf16[1152,768]{1,0:T(8,128)(2,1)}, f32[1152,1]{1,0:T(8,128)}, bf16[1152,768]{1,0:T(8,128)(2,1)}, bf16[1152,2048]...) custom-call(s32[1]{0:T(128)} %bitcast.76.own_ref, bf16[1152,768]{1,0:T(8,128)(2,1)} %bitcast.78.x_ref, ...), custom_call_target="tpu_custom_call" | custom-call | flops 21743271936 | bytes 41943040 | tf_op jit(solution)/shard_map/expert/pallas_call | solution.py:467
  373.3 3.3 all-to-all-start.7
  377.4 2.8 collective-permute-start.63
  380.2 2.9 all-to-all-done.7
  383.1 3.6 all-to-all-start.6
  386.7 18.2 %expert_grads.1 = (bf16[2,768,1024]{2,1,0:T(8,128)(2,1)}, bf16[2,768,1024]{2,1,0:T(8,128)(2,1)}, bf16[4,512,768]{2,1,0:T(8,128)(2,1)}) custom-call(bf16[1152,768]{1,0:T(8,128)(2,1)} %bitcast.78.x_ref, bf16[1152,768]{1,0:T(8,128)(2,1)} %get-tuple-element.76.deo_ref, bf16[1152,2048]{1,0:T(8,128)(2,1)} %get-tuple-element.77.act_ref, ...), custom_call_target="tpu_custom_call" | custom-call | flops 10871635968 | bytes 31457280 | tf_op jit(solution)/shard_map/expert_grads/pallas_call | solution.py:515
  406.5 3.8 collective-permute-start.65
  411.5 3.8 collective-permute-start.59
  416.5 17.1 %collective-permute-start.58 = (bf16[24,2048]{1,0:T(8,128)(2,1)S(1)}, bf16[24,2048]{1,0:T(8,128)(2,1)S(1)}, u32[]{:S(2)}, u32[]{:S(2)}) collective-permute-start(bf16[24,2048]{1,0:T(8,128)(2,1)S(1)} %get-tuple-element.183), channel_id=1, source_target_pairs={{0,8},{1,9},{2,10},{3,11},{4,12},{5,13},{6,14},{7,15},{8,16},{9,17... | collective-permute-start | bytes 294920 | tf_op jit(solution)/shard_map/ppermute | solution.py:111
  444.8 9.5 %middle_back.1 = (f32[512,768]{1,0:T(8,128)}, bf16[768,512]{1,0:T(8,128)(2,1)}, bf16[768,896]{1,0:T(8,128)(2,1)}) custom-call(f32[512,768]{1,0:T(8,128)} %get-tuple-element.62.dhn_ref, bf16[1152,768]{1,0:T(8,128)(2,1)} %bitcast.355, s32[512,2]{1,0:T(8,128)} %copy-done.10, s32[512,2]{1,0:T(8,128)} %copy.222.routes_ref, f32[1,1152]{1,0:T(1,128)} %reshape.1095.dgate_ref, ...), custom_call_target="tpu_custom_call" | custom-call | flops 3000000000 | bytes 16777216 | tf_op jit(solution)/shard_map/middle_back/pallas_call | solution.py:577
  455.5 2.4 pad_maximum_fusion
  461.9 4.2 all-to-all-start.8
  466.2 2.5 fusion.11
  470.3 7.6 %all-to-all-done.8.dctx_ref = bf16[4,192,512]{2,1,0:T(8,128)(2,1)} async-done(((bf16[4,192,512]{2,1,0:T(8,128)(2,1)}), bf16[4,192,512]{2,1,0:T(8,128)(2,1)}, u32[]{:S(2)}, u32[]{:S(2)}) %all-to-all-start.8) | async-done | bytes 786464 | tf_op jit(solution)/shard_map/all_to_all | solution.py:137
  477.8 4.7 all-to-all-start.5
  482.5 33.1 %attend_back.1 = bf16[4,576,512]{2,1,0:T(8,128)(2,1)} custom-call(bf16[4,576,512]{2,1,0:T(8,128)(2,1)} %all-to-all-done.buf_ref, bf16[4,192,512]{2,1,0:T(8,128)(2,1)} %all-to-all-done.8.dctx_ref, bf16[4,192,512]{2,1,0:T(8,128)(2,1)} %get-tuple-element.50.ctx_ref, f32[3,1,2048]{2,1,0:T(1,128)} %get-tuple-element.66.lse_ref, ...), custom_call_target="tpu_custom_call" | custom-call | flops 40000000000 | bytes 6291456 | tf_op jit(solution)/shard_map/attend_back/pallas_call | solution.py:313
  515.6 8.0 %all-to-all-done.5 = bf16[8,144,768]{2,1,0:T(8,128)(2,1)} async-done(((bf16[8,144,768]{2,1,0:T(8,128)(2,1)}), bf16[8,144,768]{2,1,0:T(8,128)(2,1)}, u32[]{:S(2)}, u32[]{:S(2)}) %all-to-all-start.5) | async-done | bytes 1769504 | tf_op jit(solution)/shard_map/all_to_all | solution.py:137
  523.7 4.9 all-to-all-start.9
  528.6 6.1 output_of.1
  536.9 3.4 fusion
  540.3 20.4 %collective-permute-done.44 = bf16[4,24,896]{2,1,0:T(8,128)(2,1)S(1)} collective-permute-done((bf16[4,24,896]{2,1,0:T(8,128)(2,1)S(1)}, bf16[4,24,896]{2,1,0:T(8,128)(2,1)S(1)}, u32[]{:S(2)}, u32[]{:S(2)}) %collective-permute-start.44) | collective-permute-done | bytes 172064 | tf_op jit(solution)/shard_map/ppermute | solution.py:115
  560.8 2.3 collective-permute-start.47
  566.1 2.9 collective-permute-done.46
  571.0 13.2 %qkv_back.1 = (f32[512,768]{1,0:T(8,128)}, bf16[768,1152]{1,0:T(8,128)(2,1)}, bf16[768,1152]{1,0:T(8,128)(2,1)}, bf16[768,128]{1,0:T(8,128)(2,1)}) custom-call(bf16[512,768]{1,0:T(8,128)(2,1)} %x_ref.5, bf16[2304,512]{1,0:T(8,128)(2,1)} %bitcast.86.dqkv_ref, bf16[768,1152]{1,0:T(8,128)(2,1)} %bitcast.322, bf16[768,1280]{1,0:T(8,128)(2,1)} %bitcast.311, ...), custom_call_target="tpu_custom_call" | custom-call | flops 3623878656 | bytes 16777216 | tf_op jit(solution)/shard_map/qkv_back/pallas_call | solution.py:670
  587.8 11.4 %collective-permute-done.67 = bf16[768,1024]{1,0:T(8,128)(2,1)S(1)} collective-permute-done((bf16[768,1024]{1,0:T(8,128)(2,1)S(1)}, bf16[768,1024]{1,0:T(8,128)(2,1)S(1)}, u32[]{:S(2)}, u32[]{:S(2)}) %collective-permute-start.67) | collective-permute-done | bytes 1572896 | tf_op jit(solution)/shard_map/ppermute | solution.py:133
  603.6 8.5 %collective-permute-done.37 = bf16[4,2,24,1152]{3,2,0,1:T(8,128)(2,1)S(1)} collective-permute-done((bf16[4,2,24,1152]{3,2,0,1:T(8,128)(2,1)S(1)}, bf16[4,2,24,1152]{3,2,0,1:T(8,128)(2,1)S(1)}, u32[]{:S(2)}, u32[]{:S(2)}) %collective-permute-start.37) | collective-permute-done | bytes 442400 | tf_op jit(solution)/shard_map/ppermute | solution.py:115
  613.0 2.9 collective-permute-done.31
  624.5 2.9 collective-permute-start.35
  630.5 2.9 collective-permute-done.34
  (335 shorter events, 140.7 us)
Async XLA Ops:
  1.5 28.8 %collective-permute-start.1 = (bf16[24,1152]{1,0:T(8,128)(2,1)S(1)}, bf16[24,1152]{1,0:T(8,128)(2,1)S(1)}, u32[]{:S(2)}, u32[]{:S(2)}) collective-permute-start(bf16[24,1152]{1,0:T(8,128)(2,1)S(1)} %get-tuple-element.196), channel_id=1, source_target_pairs={{0,24},{1,25},{2,26},{3,27},{4,28},{5,29},{6,30},{7,31},{8,0},{9,1... | collective-permute-start | bytes 165896 | tf_op jit(solution)/shard_map/ppermute | solution.py:80
  6.6 23.7 %collective-permute-start = (bf16[24,1152]{1,0:T(8,128)(2,1)S(1)}, bf16[24,1152]{1,0:T(8,128)(2,1)S(1)}, u32[]{:S(2)}, u32[]{:S(2)}) collective-permute-start(bf16[24,1152]{1,0:T(8,128)(2,1)S(1)} %get-tuple-element.196), channel_id=1, source_target_pairs={{0,16},{1,17},{2,18},{3,19},{4,20},{5,21},{6,22},{7,23},{8,24},{9,... | collective-permute-start | bytes 165896 | tf_op jit(solution)/shard_map/ppermute | solution.py:80
  6.6 23.7 %collective-permute-start.2 = (bf16[24,1152]{1,0:T(8,128)(2,1)S(1)}, bf16[24,1152]{1,0:T(8,128)(2,1)S(1)}, u32[]{:S(2)}, u32[]{:S(2)}) collective-permute-start(bf16[24,1152]{1,0:T(8,128)(2,1)S(1)} %get-tuple-element.196), channel_id=1, source_target_pairs={{0,8},{1,9},{2,10},{3,11},{4,12},{5,13},{6,14},{7,15},{8,16},{9,17... | collective-permute-start | bytes 165896 | tf_op jit(solution)/shard_map/ppermute | solution.py:80
  8.4 23.6 %collective-permute-start.7 = (bf16[24,1280]{1,0:T(8,128)(2,1)S(1)}, bf16[24,1280]{1,0:T(8,128)(2,1)S(1)}, u32[]{:S(2)}, u32[]{:S(2)}) collective-permute-start(bf16[24,1280]{1,0:T(8,128)(2,1)S(1)} %fusion.44), channel_id=1, source_target_pairs={{0,24},{1,25},{2,26},{3,27},{4,28},{5,29},{6,30},{7,31},{8,0},{9,1... | collective-permute-start | bytes 184328 | tf_op jit(solution)/shard_map/ppermute | solution.py:80
  11.2 20.7 %collective-permute-start.6 = (bf16[24,1280]{1,0:T(8,128)(2,1)S(1)}, bf16[24,1280]{1,0:T(8,128)(2,1)S(1)}, u32[]{:S(2)}, u32[]{:S(2)}) collective-permute-start(bf16[24,1280]{1,0:T(8,128)(2,1)S(1)} %fusion.44), channel_id=1, source_target_pairs={{0,16},{1,17},{2,18},{3,19},{4,20},{5,21},{6,22},{7,23},{8,24},{9,... | collective-permute-start | bytes 184328 | tf_op jit(solution)/shard_map/ppermute | solution.py:80
  36.3 9.0 %collective-permute-start.9 = (bf16[4,24,1280]{2,1,0:T(8,128)(2,1)S(1)}, bf16[4,24,1280]{2,1,0:T(8,128)(2,1)S(1)}, u32[]{:S(2)}, u32[]{:S(2)}) collective-permute-start(bf16[4,24,1280]{2,1,0:T(8,128)(2,1)S(1)} %bitcast_dynamic-update-slice_fusion.12), channel_id=1, source_target_pairs={{0,2},{1,3},{2,0},{3,1},{4,6},{5,7},{6,4},{7,5},{8,10},{9,11},{10,... | collective-permute-start | bytes 737288 | tf_op jit(solution)/shard_map/ppermute | solution.py:88
  38.0 13.0 %collective-permute-start.4 = (bf16[4,2,24,1152]{3,2,1,0:T(8,128)(2,1)S(1)}, bf16[4,2,24,1152]{3,2,1,0:T(8,128)(2,1)S(1)}, u32[]{:S(2)}, u32[]{:S(2)}) collective-permute-start(bf16[4,2,24,1152]{3,2,1,0:T(8,128)(2,1)S(1)} %maximum_select_fusion.14), channel_id=1, source_target_pairs={{0,2},{1,3},{2,0},{3,1},{4,6},{5,7},{6,4},{7,5},{8,10},{9,11},{10,... | collective-permute-start | bytes 1327112 | tf_op jit(solution)/shard_map/ppermute | solution.py:88
  45.3 8.9 %collective-permute-start.10 = (bf16[4,2,24,1280]{3,2,1,0:T(8,128)(2,1)S(1)}, bf16[4,2,24,1280]{3,2,1,0:T(8,128)(2,1)S(1)}, u32[]{:S(2)}, u32[]{:S(2)}) collective-permute-start(bf16[4,2,24,1280]{3,2,1,0:T(8,128)(2,1)S(1)} %maximum_select_fusion.13), channel_id=1, source_target_pairs={{0,4},{1,5},{2,6},{3,7},{4,0},{5,1},{6,2},{7,3},{8,12},{9,13},{10,... | collective-permute-start | bytes 1474568 | tf_op jit(solution)/shard_map/ppermute | solution.py:88
  58.5 33.9 %collective-permute-start.20 = (bf16[24,2048]{1,0:T(8,128)(2,1)S(1)}, bf16[24,2048]{1,0:T(8,128)(2,1)S(1)}, u32[]{:S(2)}, u32[]{:S(2)}) collective-permute-start(bf16[24,2048]{1,0:T(8,128)(2,1)S(1)} %get-tuple-element.54), channel_id=1, source_target_pairs={{0,8},{1,9},{2,10},{3,11},{4,12},{5,13},{6,14},{7,15},{8,16},{9,17... | collective-permute-start | bytes 294920 | tf_op jit(solution)/shard_map/ppermute | solution.py:80
  58.5 32.1 %collective-permute-start.19 = (bf16[24,2048]{1,0:T(8,128)(2,1)S(1)}, bf16[24,2048]{1,0:T(8,128)(2,1)S(1)}, u32[]{:S(2)}, u32[]{:S(2)}) collective-permute-start(bf16[24,2048]{1,0:T(8,128)(2,1)S(1)} %get-tuple-element.54), channel_id=1, source_target_pairs={{0,24},{1,25},{2,26},{3,27},{4,28},{5,29},{6,30},{7,31},{8,0},{9,1... | collective-permute-start | bytes 294920 | tf_op jit(solution)/shard_map/ppermute | solution.py:80
  62.3 16.8 %collective-permute-start.18 = (bf16[24,2048]{1,0:T(8,128)(2,1)S(1)}, bf16[24,2048]{1,0:T(8,128)(2,1)S(1)}, u32[]{:S(2)}, u32[]{:S(2)}) collective-permute-start(bf16[24,2048]{1,0:T(8,128)(2,1)S(1)} %get-tuple-element.54), channel_id=1, source_target_pairs={{0,16},{1,17},{2,18},{3,19},{4,20},{5,21},{6,22},{7,23},{8,24},{9,... | collective-permute-start | bytes 294920 | tf_op jit(solution)/shard_map/ppermute | solution.py:80
  62.3 28.2 %collective-permute-start.26 = (bf16[64,768]{1,0:T(8,128)(2,1)S(1)}, bf16[64,768]{1,0:T(8,128)(2,1)S(1)}, u32[]{:S(2)}, u32[]{:S(2)}) collective-permute-start(bf16[64,768]{1,0:T(8,128)(2,1)S(1)} %copy-done.19), channel_id=1, source_target_pairs={{0,8},{1,9},{2,10},{3,11},{4,12},{5,13},{6,14},{7,15},{8,16},{9,17... | collective-permute-start | bytes 294920 | tf_op jit(solution)/shard_map/ppermute | solution.py:80
  62.9 23.5 %collective-permute-start.25 = (bf16[64,768]{1,0:T(8,128)(2,1)S(1)}, bf16[64,768]{1,0:T(8,128)(2,1)S(1)}, u32[]{:S(2)}, u32[]{:S(2)}) collective-permute-start(bf16[64,768]{1,0:T(8,128)(2,1)S(1)} %copy-done.19), channel_id=1, source_target_pairs={{0,24},{1,25},{2,26},{3,27},{4,28},{5,29},{6,30},{7,31},{8,0},{9,1... | collective-permute-start | bytes 294920 | tf_op jit(solution)/shard_map/ppermute | solution.py:80
  74.5 86.6 %all-to-all-start = ((bf16[4,576,512]{2,1,0:T(8,128)(2,1)}), bf16[4,576,512]{2,1,0:T(8,128)(2,1)}, u32[]{:S(2)}, u32[]{:S(2)}) async-start(bf16[4,576,512]{2,1,0:T(8,128)(2,1)} %bitcast.314), calls=%async_computation | async-start | bytes 4718592 | tf_op jit(solution)/shard_map/all_to_all | solution.py:137
  86.4 14.7 %collective-permute-start.14 = (bf16[24,2944]{1,0:T(8,128)(2,1)S(1)}, bf16[24,2944]{1,0:T(8,128)(2,1)S(1)}, u32[]{:S(2)}, u32[]{:S(2)}) collective-permute-start(bf16[24,2944]{1,0:T(8,128)(2,1)S(1)} %pad_maximum_fusion.24), channel_id=1, source_target_pairs={{0,8},{1,9},{2,10},{3,11},{4,12},{5,13},{6,14},{7,15},{8,16},{9,17... | collective-permute-start | bytes 423944 | tf_op jit(solution)/shard_map/ppermute | solution.py:80
  86.4 14.6 %collective-permute-start.13 = (bf16[24,2944]{1,0:T(8,128)(2,1)S(1)}, bf16[24,2944]{1,0:T(8,128)(2,1)S(1)}, u32[]{:S(2)}, u32[]{:S(2)}) collective-permute-start(bf16[24,2944]{1,0:T(8,128)(2,1)S(1)} %pad_maximum_fusion.24), channel_id=1, source_target_pairs={{0,24},{1,25},{2,26},{3,27},{4,28},{5,29},{6,30},{7,31},{8,0},{9,1... | collective-permute-start | bytes 423944 | tf_op jit(solution)/shard_map/ppermute | solution.py:80
  90.5 10.5 %collective-permute-start.12 = (bf16[24,2944]{1,0:T(8,128)(2,1)S(1)}, bf16[24,2944]{1,0:T(8,128)(2,1)S(1)}, u32[]{:S(2)}, u32[]{:S(2)}) collective-permute-start(bf16[24,2944]{1,0:T(8,128)(2,1)S(1)} %pad_maximum_fusion.24), channel_id=1, source_target_pairs={{0,16},{1,17},{2,18},{3,19},{4,20},{5,21},{6,22},{7,23},{8,24},{9,... | collective-permute-start | bytes 423944 | tf_op jit(solution)/shard_map/ppermute | solution.py:80
  90.6 25.7 %collective-permute-start.27 = (bf16[4,64,768]{2,1,0:T(8,128)(2,1)S(1)}, bf16[4,64,768]{2,1,0:T(8,128)(2,1)S(1)}, u32[]{:S(2)}, u32[]{:S(2)}) collective-permute-start(bf16[4,64,768]{2,1,0:T(8,128)(2,1)S(1)} %bitcast_dynamic-update-slice_fusion.4), channel_id=1, source_target_pairs={{0,2},{1,3},{2,0},{3,1},{4,6},{5,7},{6,4},{7,5},{8,10},{9,11},{10,... | collective-permute-start | bytes 1179656 | tf_op jit(solution)/shard_map/ppermute | solution.py:88
  92.4 25.6 %collective-permute-start.21 = (bf16[4,24,2048]{2,1,0:T(8,128)(2,1)S(1)}, bf16[4,24,2048]{2,1,0:T(8,128)(2,1)S(1)}, u32[]{:S(2)}, u32[]{:S(2)}) collective-permute-start(bf16[4,24,2048]{2,1,0:T(8,128)(2,1)S(1)} %bitcast_dynamic-update-slice_fusion.8), channel_id=1, source_target_pairs={{0,4},{1,5},{2,6},{3,7},{4,0},{5,1},{6,2},{7,3},{8,12},{9,13},{10,... | collective-permute-start | bytes 1179656 | tf_op jit(solution)/shard_map/ppermute | solution.py:88
  101.1 27.3 %collective-permute-start.15 = (bf16[4,24,2944]{2,1,0:T(8,128)(2,1)S(1)}, bf16[4,24,2944]{2,1,0:T(8,128)(2,1)S(1)}, u32[]{:S(2)}, u32[]{:S(2)}) collective-permute-start(bf16[4,24,2944]{2,1,0:T(8,128)(2,1)S(1)} %bitcast_dynamic-update-slice_fusion), channel_id=1, source_target_pairs={{0,2},{1,3},{2,0},{3,1},{4,6},{5,7},{6,4},{7,5},{8,10},{9,11},{10,... | collective-permute-start | bytes 1695752 | tf_op jit(solution)/shard_map/ppermute | solution.py:88
  116.4 20.5 %collective-permute-start.28 = (bf16[4,2,64,768]{3,2,1,0:T(8,128)(2,1)S(1)}, bf16[4,2,64,768]{3,2,1,0:T(8,128)(2,1)S(1)}, u32[]{:S(2)}, u32[]{:S(2)}) collective-permute-start(bf16[4,2,64,768]{3,2,1,0:T(8,128)(2,1)S(1)} %maximum_select_fusion.12), channel_id=1, source_target_pairs={{0,4},{1,5},{2,6},{3,7},{4,0},{5,1},{6,2},{7,3},{8,12},{9,13},{10,... | collective-permute-start | bytes 2359304 | tf_op jit(solution)/shard_map/ppermute | solution.py:88
  118.1 26.7 %collective-permute-start.22 = (bf16[4,2,24,2048]{3,2,1,0:T(8,128)(2,1)S(1)}, bf16[4,2,24,2048]{3,2,1,0:T(8,128)(2,1)S(1)}, u32[]{:S(2)}, u32[]{:S(2)}) collective-permute-start(bf16[4,2,24,2048]{3,2,1,0:T(8,128)(2,1)S(1)} %maximum_select_fusion.11), channel_id=1, source_target_pairs={{0,2},{1,3},{2,0},{3,1},{4,6},{5,7},{6,4},{7,5},{8,10},{9,11},{10,... | collective-permute-start | bytes 2359304 | tf_op jit(solution)/shard_map/ppermute | solution.py:88
  128.8 30.5 %collective-permute-start.16 = (bf16[4,2,24,2944]{3,2,1,0:T(8,128)(2,1)S(1)}, bf16[4,2,24,2944]{3,2,1,0:T(8,128)(2,1)S(1)}, u32[]{:S(2)}, u32[]{:S(2)}) collective-permute-start(bf16[4,2,24,2944]{3,2,1,0:T(8,128)(2,1)S(1)} %maximum_select_fusion.8), channel_id=1, source_target_pairs={{0,4},{1,5},{2,6},{3,7},{4,0},{5,1},{6,2},{7,3},{8,12},{9,13},{10,... | collective-permute-start | bytes 3391496 | tf_op jit(solution)/shard_map/ppermute | solution.py:88
  138.3 46.0 %collective-permute-start.29 = (bf16[4,2,2,64,768]{4,3,2,1,0:T(8,128)(2,1)}, bf16[4,2,2,64,768]{4,3,2,1,0:T(8,128)(2,1)}, u32[]{:S(2)}, u32[]{:S(2)}) collective-permute-start(bf16[4,2,2,64,768]{4,3,2,1,0:T(8,128)(2,1)} %maximum_select_fusion.7), channel_id=1, source_target_pairs={{0,1},{1,0},{2,3},{3,2},{4,5},{5,4},{6,7},{7,6},{8,9},{9,8},{10,11... | collective-permute-start | bytes 4718600 | tf_op jit(solution)/shard_map/ppermute | solution.py:88
  146.1 43.0 %collective-permute-start.23 = (bf16[4,2,2,24,2048]{4,3,2,1,0:T(8,128)(2,1)}, bf16[4,2,2,24,2048]{4,3,2,1,0:T(8,128)(2,1)}, u32[]{:S(2)}, u32[]{:S(2)}) collective-permute-start(bf16[4,2,2,24,2048]{4,3,2,1,0:T(8,128)(2,1)} %maximum_select_fusion.6), channel_id=1, source_target_pairs={{0,1},{1,0},{2,3},{3,2},{4,5},{5,4},{6,7},{7,6},{8,9},{9,8},{10,11... | collective-permute-start | bytes 4718600 | tf_op jit(solution)/shard_map/ppermute | solution.py:88
  161.1 31.7 %collective-permute-start.17 = (bf16[4,2,2,24,2944]{4,3,2,1,0:T(8,128)(2,1)}, bf16[4,2,2,24,2944]{4,3,2,1,0:T(8,128)(2,1)}, u32[]{:S(2)}, u32[]{:S(2)}) collective-permute-start(bf16[4,2,2,24,2944]{4,3,2,1,0:T(8,128)(2,1)} %maximum_select_fusion.3), channel_id=1, source_target_pairs={{0,1},{1,0},{2,3},{3,2},{4,5},{5,4},{6,7},{7,6},{8,9},{9,8},{10,11... | collective-permute-start | bytes 6782984 | tf_op jit(solution)/shard_map/ppermute | solution.py:88
  178.3 21.1 %all-to-all-start.1 = ((bf16[4,192,512]{2,1,0:T(8,128)(2,1)}), bf16[4,192,512]{2,1,0:T(8,128)(2,1)S(1)}, u32[]{:S(2)}, u32[]{:S(2)}) async-start(bf16[4,192,512]{2,1,0:T(8,128)(2,1)} %get-tuple-element.50.ctx_ref), calls=%async_computation.1 | async-start | bytes 1572864 | tf_op jit(solution)/shard_map/all_to_all | solution.py:137
  229.2 23.2 %collective-permute-start.48 = (bf16[4,2,2,24,2048]{4,3,0,1,2:T(8,128)(2,1)S(1)}, bf16[4,2,2,24,2048]{4,3,0,1,2:T(8,128)(2,1)}, u32[]{:S(2)}, u32[]{:S(2)}) collective-permute-start(bf16[4,2,2,24,2048]{4,3,0,1,2:T(8,128)(2,1)S(1)} %bitcast.359), channel_id=1, source_target_pairs={{0,1},{1,0},{2,3},{3,2},{4,5},{5,4},{6,7},{7,6},{8,9},{9,8},{10,11... | collective-permute-start | bytes 4718600 | tf_op jit(solution)/shard_map/ppermute | solution.py:115
  239.5 44.6 %all-to-all-start.3 = ((bf16[8,144,768]{2,1,0:T(8,128)(2,1)}), bf16[8,144,768]{2,1,0:T(8,128)(2,1)}, u32[]{:S(2)}, u32[]{:S(2)}) async-start(bf16[8,144,768]{2,1,0:T(8,128)(2,1)} %bitcast.79), calls=%async_computation.3 | async-start | bytes 3538944 | tf_op jit(solution)/shard_map/all_to_all | solution.py:137
  248.5 8.5 %collective-permute-start.54 = (bf16[4,2,2,24,2048]{4,3,0,2,1:T(8,128)(2,1)}, bf16[4,2,2,24,2048]{4,3,0,2,1:T(8,128)(2,1)}, u32[]{:S(2)}, u32[]{:S(2)}) collective-permute-start(bf16[4,2,2,24,2048]{4,3,0,2,1:T(8,128)(2,1)} %bitcast.301), channel_id=1, source_target_pairs={{0,1},{1,0},{2,3},{3,2},{4,5},{5,4},{6,7},{7,6},{8,9},{9,8},{10,11... | collective-permute-start | bytes 4718600 | tf_op jit(solution)/shard_map/ppermute | solution.py:115
  251.8 10.1 %collective-permute-start.60 = (bf16[4,2,2,64,768]{4,3,0,1,2:T(8,128)(2,1)S(1)}, bf16[4,2,2,64,768]{4,3,0,1,2:T(8,128)(2,1)S(1)}, u32[]{:S(2)}, u32[]{:S(2)}) collective-permute-start(bf16[4,2,2,64,768]{4,3,0,1,2:T(8,128)(2,1)S(1)} %bitcast.360), channel_id=1, source_target_pairs={{0,1},{1,0},{2,3},{3,2},{4,5},{5,4},{6,7},{7,6},{8,9},{9,8},{10,11... | collective-permute-start | bytes 4718600 | tf_op jit(solution)/shard_map/ppermute | solution.py:115
  255.4 33.0 %collective-permute-start.49 = (bf16[4,2,24,2048]{3,2,0,1:T(8,128)(2,1)}, bf16[4,2,24,2048]{3,2,0,1:T(8,128)(2,1)}, u32[]{:S(2)}, u32[]{:S(2)}) collective-permute-start(bf16[4,2,24,2048]{3,2,0,1:T(8,128)(2,1)} %dynamic-slice_bitcast_fusion.6), channel_id=1, source_target_pairs={{0,2},{1,3},{2,0},{3,1},{4,6},{5,7},{6,4},{7,5},{8,10},{9,11},{10,... | collective-permute-start | bytes 2359304 | tf_op jit(solution)/shard_map/ppermute | solution.py:115
  260.0 31.8 %collective-permute-start.55 = (bf16[4,2,24,2048]{3,2,0,1:T(8,128)(2,1)}, bf16[4,2,24,2048]{3,2,0,1:T(8,128)(2,1)}, u32[]{:S(2)}, u32[]{:S(2)}) collective-permute-start(bf16[4,2,24,2048]{3,2,0,1:T(8,128)(2,1)} %dynamic-slice_bitcast_fusion.5), channel_id=1, source_target_pairs={{0,4},{1,5},{2,6},{3,7},{4,0},{5,1},{6,2},{7,3},{8,12},{9,13},{10,... | collective-permute-start | bytes 2359304 | tf_op jit(solution)/shard_map/ppermute | solution.py:115
  264.5 30.8 %collective-permute-start.61 = (bf16[4,2,64,768]{3,2,0,1:T(8,128)(2,1)}, bf16[4,2,64,768]{3,2,0,1:T(8,128)(2,1)}, u32[]{:S(2)}, u32[]{:S(2)}) collective-permute-start(bf16[4,2,64,768]{3,2,0,1:T(8,128)(2,1)} %dynamic-slice_bitcast_fusion.4), channel_id=1, source_target_pairs={{0,2},{1,3},{2,0},{3,1},{4,6},{5,7},{6,4},{7,5},{8,10},{9,11},{10,... | collective-permute-start | bytes 2359304 | tf_op jit(solution)/shard_map/ppermute | solution.py:115
  284.0 53.4 %all-to-all-start.2 = ((bf16[8,144,768]{2,1,0:T(8,128)(2,1)}), bf16[8,144,768]{2,1,0:T(8,128)(2,1)}, u32[]{:S(2)}, u32[]{:S(2)}) async-start(bf16[8,144,768]{2,1,0:T(8,128)(2,1)} %bitcast.353), calls=%async_computation.2 | async-start | bytes 3538944 | tf_op jit(solution)/shard_map/all_to_all | solution.py:137
  289.8 29.6 %collective-permute-start.50 = (bf16[4,24,2048]{2,1,0:T(8,128)(2,1)S(1)}, bf16[4,24,2048]{2,1,0:T(8,128)(2,1)S(1)}, u32[]{:S(2)}, u32[]{:S(2)}) collective-permute-start(bf16[4,24,2048]{2,1,0:T(8,128)(2,1)S(1)} %dynamic-slice_bitcast_fusion.12), channel_id=1, source_target_pairs={{0,4},{1,5},{2,6},{3,7},{4,0},{5,1},{6,2},{7,3},{8,12},{9,13},{10,... | collective-permute-start | bytes 1179656 | tf_op jit(solution)/shard_map/ppermute | solution.py:115
  293.2 31.3 %collective-permute-start.56 = (bf16[4,24,2048]{2,1,0:T(8,128)(2,1)S(1)}, bf16[4,24,2048]{2,1,0:T(8,128)(2,1)S(1)}, u32[]{:S(2)}, u32[]{:S(2)}) collective-permute-start(bf16[4,24,2048]{2,1,0:T(8,128)(2,1)S(1)} %dynamic-slice_bitcast_fusion.11), channel_id=1, source_target_pairs={{0,2},{1,3},{2,0},{3,1},{4,6},{5,7},{6,4},{7,5},{8,10},{9,11},{10,... | collective-permute-start | bytes 1179656 | tf_op jit(solution)/shard_map/ppermute | solution.py:115
  296.7 30.9 %collective-permute-start.62 = (bf16[4,64,768]{2,1,0:T(8,128)(2,1)S(1)}, bf16[4,64,768]{2,1,0:T(8,128)(2,1)S(1)}, u32[]{:S(2)}, u32[]{:S(2)}) collective-permute-start(bf16[4,64,768]{2,1,0:T(8,128)(2,1)S(1)} %dynamic-slice_bitcast_fusion.10), channel_id=1, source_target_pairs={{0,4},{1,5},{2,6},{3,7},{4,0},{5,1},{6,2},{7,3},{8,12},{9,13},{10,... | collective-permute-start | bytes 1179656 | tf_op jit(solution)/shard_map/ppermute | solution.py:115
  320.4 86.1 %collective-permute-start.51 = (bf16[24,2048]{1,0:T(8,128)(2,1)}, bf16[24,2048]{1,0:T(8,128)(2,1)}, u32[]{:S(2)}, u32[]{:S(2)}) collective-permute-start(bf16[24,2048]{1,0:T(8,128)(2,1)} %get-tuple-element.178), channel_id=1, source_target_pairs={{0,16},{1,17},{2,18},{3,19},{4,20},{5,21},{6,22},{7,23},{8,24},{9,... | collective-permute-start | bytes 294920 | tf_op jit(solution)/shard_map/ppermute | solution.py:111
  320.4 89.9 %collective-permute-start.53 = (bf16[24,2048]{1,0:T(8,128)(2,1)}, bf16[24,2048]{1,0:T(8,128)(2,1)}, u32[]{:S(2)}, u32[]{:S(2)}) collective-permute-start(bf16[24,2048]{1,0:T(8,128)(2,1)} %get-tuple-element.179), channel_id=1, source_target_pairs={{0,24},{1,25},{2,26},{3,27},{4,28},{5,29},{6,30},{7,31},{8,0},{9,1... | collective-permute-start | bytes 294920 | tf_op jit(solution)/shard_map/ppermute | solution.py:111
  323.6 86.7 %collective-permute-start.52 = (bf16[24,2048]{1,0:T(8,128)(2,1)}, bf16[24,2048]{1,0:T(8,128)(2,1)}, u32[]{:S(2)}, u32[]{:S(2)}) collective-permute-start(bf16[24,2048]{1,0:T(8,128)(2,1)} %get-tuple-element.180), channel_id=1, source_target_pairs={{0,8},{1,9},{2,10},{3,11},{4,12},{5,13},{6,14},{7,15},{8,16},{9,17... | collective-permute-start | bytes 294920 | tf_op jit(solution)/shard_map/ppermute | solution.py:111
  326.1 109.2 %collective-permute-start.57 = (bf16[24,2048]{1,0:T(8,128)(2,1)}, bf16[24,2048]{1,0:T(8,128)(2,1)S(1)}, u32[]{:S(2)}, u32[]{:S(2)}) collective-permute-start(bf16[24,2048]{1,0:T(8,128)(2,1)} %get-tuple-element.181), channel_id=1, source_target_pairs={{0,16},{1,17},{2,18},{3,19},{4,20},{5,21},{6,22},{7,23},{8,24},{9,... | collective-permute-start | bytes 294920 | tf_op jit(solution)/shard_map/ppermute | solution.py:111
  373.3 9.8 %all-to-all-start.7 = ((f32[8,1,144]{2,1,0:T(1,128)}), f32[8,1,144]{2,1,0:T(1,128)S(1)}, u32[]{:S(2)}, u32[]{:S(2)}) async-start(f32[8,1,144]{2,1,0:T(1,128)} %all_to_all.48), calls=%async_computation.7 | async-start | bytes 16384 | tf_op jit(solution)/shard_map/all_to_all | solution.py:137
  377.4 34.1 %collective-permute-start.63 = (bf16[64,768]{1,0:T(8,128)(2,1)}, bf16[64,768]{1,0:T(8,128)(2,1)}, u32[]{:S(2)}, u32[]{:S(2)}) collective-permute-start(bf16[64,768]{1,0:T(8,128)(2,1)} %get-tuple-element.175), channel_id=1, source_target_pairs={{0,16},{1,17},{2,18},{3,19},{4,20},{5,21},{6,22},{7,23},{8,24},{9,... | collective-permute-start | bytes 294920 | tf_op jit(solution)/shard_map/ppermute | solution.py:111
  383.1 60.5 %all-to-all-start.6 = ((bf16[8,144,768]{2,1,0:T(8,128)(2,1)}), bf16[8,144,768]{2,1,0:T(8,128)(2,1)S(1)}, u32[]{:S(2)}, u32[]{:S(2)}) async-start(bf16[8,144,768]{2,1,0:T(8,128)(2,1)} %bitcast.354), calls=%async_computation.6 | async-start | bytes 3538944 | tf_op jit(solution)/shard_map/all_to_all | solution.py:137
  406.5 10.0 %collective-permute-start.65 = (bf16[64,768]{1,0:T(8,128)(2,1)S(1)}, bf16[64,768]{1,0:T(8,128)(2,1)S(1)}, u32[]{:S(2)}, u32[]{:S(2)}) collective-permute-start(bf16[64,768]{1,0:T(8,128)(2,1)S(1)} %copy-done.22), channel_id=1, source_target_pairs={{0,24},{1,25},{2,26},{3,27},{4,28},{5,29},{6,30},{7,31},{8,0},{9,1... | collective-permute-start | bytes 294920 | tf_op jit(solution)/shard_map/ppermute | solution.py:111
  410.3 23.4 %collective-permute-start.64 = (bf16[64,768]{1,0:T(8,128)(2,1)S(1)}, bf16[64,768]{1,0:T(8,128)(2,1)S(1)}, u32[]{:S(2)}, u32[]{:S(2)}) collective-permute-start(bf16[64,768]{1,0:T(8,128)(2,1)S(1)} %copy-done.21), channel_id=1, source_target_pairs={{0,8},{1,9},{2,10},{3,11},{4,12},{5,13},{6,14},{7,15},{8,16},{9,17... | collective-permute-start | bytes 294920 | tf_op jit(solution)/shard_map/ppermute | solution.py:111
  410.3 28.0 %collective-permute-start.68 = (bf16[2,512,768]{2,1,0:T(8,128)(2,1)S(1)}, bf16[2,512,768]{2,1,0:T(8,128)(2,1)}, u32[]{:S(2)}, u32[]{:S(2)}) collective-permute-start(bf16[2,512,768]{2,1,0:T(8,128)(2,1)S(1)} %dynamic-slice_bitcast_fusion.1), channel_id=1, source_target_pairs={{0,1},{1,0},{2,3},{3,2},{4,5},{5,4},{6,7},{7,6},{8,9},{9,8},{10,11... | collective-permute-start | bytes 4718600 | tf_op jit(solution)/shard_map/ppermute | solution.py:130
  411.5 23.8 %collective-permute-start.59 = (bf16[24,2048]{1,0:T(8,128)(2,1)S(1)}, bf16[24,2048]{1,0:T(8,128)(2,1)S(1)}, u32[]{:S(2)}, u32[]{:S(2)}) collective-permute-start(bf16[24,2048]{1,0:T(8,128)(2,1)S(1)} %copy-done.20), channel_id=1, source_target_pairs={{0,24},{1,25},{2,26},{3,27},{4,28},{5,29},{6,30},{7,31},{8,0},{9,1... | collective-permute-start | bytes 294920 | tf_op jit(solution)/shard_map/ppermute | solution.py:111
  416.5 19.4 %collective-permute-start.58 = (bf16[24,2048]{1,0:T(8,128)(2,1)S(1)}, bf16[24,2048]{1,0:T(8,128)(2,1)S(1)}, u32[]{:S(2)}, u32[]{:S(2)}) collective-permute-start(bf16[24,2048]{1,0:T(8,128)(2,1)S(1)} %get-tuple-element.183), channel_id=1, source_target_pairs={{0,8},{1,9},{2,10},{3,11},{4,12},{5,13},{6,14},{7,15},{8,16},{9,17... | collective-permute-start | bytes 294920 | tf_op jit(solution)/shard_map/ppermute | solution.py:111
  441.5 24.6 %collective-permute-start.69 = (bf16[512,768]{1,0:T(8,128)(2,1)}, bf16[512,768]{1,0:T(8,128)(2,1)}, u32[]{:S(2)}, u32[]{:S(2)}) collective-permute-start(bf16[512,768]{1,0:T(8,128)(2,1)} %dynamic-slice_bitcast_fusion.3), channel_id=1, source_target_pairs={{0,2},{1,3},{2,0},{3,1},{4,6},{5,7},{6,4},{7,5},{8,10},{9,11},{10,... | collective-permute-start | bytes 2359304 | tf_op jit(solution)/shard_map/ppermute | solution.py:133
  455.4 13.3 %collective-permute-start.42 = (bf16[4,2,2,24,896]{4,3,2,1,0:T(8,128)(2,1)S(1)}, bf16[4,2,2,24,896]{4,3,2,1,0:T(8,128)(2,1)S(1)}, u32[]{:S(2)}, u32[]{:S(2)}) collective-permute-start(bf16[4,2,2,24,896]{4,3,2,1,0:T(8,128)(2,1)S(1)} %dynamic-slice_bitcast_fusion.7), channel_id=1, source_target_pairs={{0,1},{1,0},{2,3},{3,2},{4,5},{5,4},{6,7},{7,6},{8,9},{9,8},{10,11... | collective-permute-start | bytes 2064392 | tf_op jit(solution)/shard_map/ppermute | solution.py:115
  461.4 75.4 %collective-permute-start.66 = (bf16[2,768,1024]{2,1,0:T(8,128)(2,1)}, bf16[2,768,1024]{2,1,0:T(8,128)(2,1)}, u32[]{:S(2)}, u32[]{:S(2)}) collective-permute-start(bf16[2,768,1024]{2,1,0:T(8,128)(2,1)} %dynamic-slice_bitcast_fusion), channel_id=1, source_target_pairs={{0,1},{1,0},{2,3},{3,2},{4,5},{5,4},{6,7},{7,6},{8,9},{9,8},{10,11... | collective-permute-start | bytes 9437192 | tf_op jit(solution)/shard_map/ppermute | solution.py:130
  461.9 15.9 %all-to-all-start.8 = ((bf16[4,192,512]{2,1,0:T(8,128)(2,1)}), bf16[4,192,512]{2,1,0:T(8,128)(2,1)}, u32[]{:S(2)}, u32[]{:S(2)}) async-start(bf16[4,192,512]{2,1,0:T(8,128)(2,1)} %bitcast.85), calls=%async_computation.8 | async-start | bytes 1572864 | tf_op jit(solution)/shard_map/all_to_all | solution.py:137
  468.9 65.7 %collective-permute-start.43 = (bf16[4,2,24,896]{3,2,1,0:T(8,128)(2,1)S(1)}, bf16[4,2,24,896]{3,2,1,0:T(8,128)(2,1)S(1)}, u32[]{:S(2)}, u32[]{:S(2)}) collective-permute-start(bf16[4,2,24,896]{3,2,1,0:T(8,128)(2,1)S(1)} %dynamic-slice_bitcast_fusion.13), channel_id=1, source_target_pairs={{0,4},{1,5},{2,6},{3,7},{4,0},{5,1},{6,2},{7,3},{8,12},{9,13},{10,... | collective-permute-start | bytes 1032200 | tf_op jit(solution)/shard_map/ppermute | solution.py:115
  477.8 45.8 %all-to-all-start.5 = ((bf16[8,144,768]{2,1,0:T(8,128)(2,1)}), bf16[8,144,768]{2,1,0:T(8,128)(2,1)}, u32[]{:S(2)}, u32[]{:S(2)}) async-start(bf16[8,144,768]{2,1,0:T(8,128)(2,1)} %bitcast.81), calls=%async_computation.5 | async-start | bytes 3538944 | tf_op jit(solution)/shard_map/all_to_all | solution.py:137
  523.7 47.4 %all-to-all-start.9 = ((bf16[4,576,512]{2,1,0:T(8,128)(2,1)}), bf16[4,576,512]{2,1,0:T(8,128)(2,1)}, u32[]{:S(2)}, u32[]{:S(2)}) async-start(bf16[4,576,512]{2,1,0:T(8,128)(2,1)} %attend_back.1), calls=%async_computation.9 | async-start | bytes 4718592 | tf_op jit(solution)/shard_map/all_to_all | solution.py:137
  534.8 25.9 %collective-permute-start.44 = (bf16[4,24,896]{2,1,0:T(8,128)(2,1)S(1)}, bf16[4,24,896]{2,1,0:T(8,128)(2,1)S(1)}, u32[]{:S(2)}, u32[]{:S(2)}) collective-permute-start(bf16[4,24,896]{2,1,0:T(8,128)(2,1)S(1)} %dynamic-slice_bitcast_fusion.16), channel_id=1, source_target_pairs={{0,2},{1,3},{2,0},{3,1},{4,6},{5,7},{6,4},{7,5},{8,10},{9,11},{10,... | collective-permute-start | bytes 516104 | tf_op jit(solution)/shard_map/ppermute | solution.py:115
  563.8 35.4 %collective-permute-start.67 = (bf16[768,1024]{1,0:T(8,128)(2,1)S(1)}, bf16[768,1024]{1,0:T(8,128)(2,1)S(1)}, u32[]{:S(2)}, u32[]{:S(2)}) collective-permute-start(bf16[768,1024]{1,0:T(8,128)(2,1)S(1)} %dynamic-slice_bitcast_fusion.2), channel_id=1, source_target_pairs={{0,2},{1,3},{2,0},{3,1},{4,6},{5,7},{6,4},{7,5},{8,10},{9,11},{10,... | collective-permute-start | bytes 4718600 | tf_op jit(solution)/shard_map/ppermute | solution.py:133
  585.9 15.6 %collective-permute-start.36 = (bf16[4,2,2,24,1152]{4,3,0,1,2:T(8,128)(2,1)S(1)}, bf16[4,2,2,24,1152]{4,3,0,1,2:T(8,128)(2,1)S(1)}, u32[]{:S(2)}, u32[]{:S(2)}) collective-permute-start(bf16[4,2,2,24,1152]{4,3,0,1,2:T(8,128)(2,1)S(1)} %bitcast.371), channel_id=1, source_target_pairs={{0,1},{1,0},{2,3},{3,2},{4,5},{5,4},{6,7},{7,6},{8,9},{9,8},{10,11... | collective-permute-start | bytes 2654216 | tf_op jit(solution)/shard_map/ppermute | solution.py:115
  587.7 14.8 %collective-permute-start.30 = (bf16[4,2,2,24,1280]{4,3,0,2,1:T(8,128)(2,1)S(1)}, bf16[4,2,2,24,1280]{4,3,0,2,1:T(8,128)(2,1)S(1)}, u32[]{:S(2)}, u32[]{:S(2)}) collective-permute-start(bf16[4,2,2,24,1280]{4,3,0,2,1:T(8,128)(2,1)S(1)} %bitcast.367), channel_id=1, source_target_pairs={{0,1},{1,0},{2,3},{3,2},{4,5},{5,4},{6,7},{7,6},{8,9},{9,8},{10,11... | collective-permute-start | bytes 2949128 | tf_op jit(solution)/shard_map/ppermute | solution.py:115
  601.8 10.3 %collective-permute-start.37 = (bf16[4,2,24,1152]{3,2,0,1:T(8,128)(2,1)S(1)}, bf16[4,2,24,1152]{3,2,0,1:T(8,128)(2,1)S(1)}, u32[]{:S(2)}, u32[]{:S(2)}) collective-permute-start(bf16[4,2,24,1152]{3,2,0,1:T(8,128)(2,1)S(1)} %dynamic-slice_bitcast_fusion.9), channel_id=1, source_target_pairs={{0,2},{1,3},{2,0},{3,1},{4,6},{5,7},{6,4},{7,5},{8,10},{9,11},{10,... | collective-permute-start | bytes 1327112 | tf_op jit(solution)/shard_map/ppermute | solution.py:115
  602.8 13.2 %collective-permute-start.31 = (bf16[4,2,24,1280]{3,2,0,1:T(8,128)(2,1)S(1)}, bf16[4,2,24,1280]{3,2,0,1:T(8,128)(2,1)S(1)}, u32[]{:S(2)}, u32[]{:S(2)}) collective-permute-start(bf16[4,2,24,1280]{3,2,0,1:T(8,128)(2,1)S(1)} %dynamic-slice_bitcast_fusion.8), channel_id=1, source_target_pairs={{0,4},{1,5},{2,6},{3,7},{4,0},{5,1},{6,2},{7,3},{8,12},{9,13},{10,... | collective-permute-start | bytes 1474568 | tf_op jit(solution)/shard_map/ppermute | solution.py:115
  618.9 8.5 %collective-permute-start.39 = (bf16[24,1152]{1,0:T(8,128)(2,1)S(1)}, bf16[24,1152]{1,0:T(8,128)(2,1)S(1)}, u32[]{:S(2)}, u32[]{:S(2)}) collective-permute-start(bf16[24,1152]{1,0:T(8,128)(2,1)S(1)} %get-tuple-element.187), channel_id=1, source_target_pairs={{0,16},{1,17},{2,18},{3,19},{4,20},{5,21},{6,22},{7,23},{8,24},{9,... | collective-permute-start | bytes 165896 | tf_op jit(solution)/shard_map/ppermute | solution.py:111
  (44 other events, 280.6 us)

commit v2 on v1

v2 whole, which is shorter than its diff:
```python
import functools

import jax
import jax.numpy as jnp
from jax import lax
from jax.experimental import pallas as pl
from jax.experimental.pallas import tpu as pltpu
from jax.sharding import PartitionSpec as P

HEADS = 12
EPS = 1e-06
BASE = 10000.0
MASKED = -1e30
AXES = ("dp", "seq")
LANES = 128
F32 = jnp.float32
BF16 = jnp.bfloat16
NN = (((1,), (0,)), ((), ()))
NT = (((1,), (1,)), ((), ()))
TN = (((0,), (0,)), ((), ()))


def mm(left, right, dims=NN):
    return lax.dot_general(left, right, dims, preferred_element_type=F32)


def params(steps=0, mib=56):
    semantics = ("arbitrary",) * steps if steps else None
    return pltpu.CompilerParams(dimension_semantics=semantics, vmem_limit_bytes=mib << 20)


def cost(flops, moved):
    return pl.CostEstimate(flops=int(flops), bytes_accessed=int(moved), transcendentals=0)


def whole():
    return pl.BlockSpec(memory_space=pltpu.VMEM)


def pairs(place):
    found = []
    for device in range(32):
        z, y, x, c = device // 8, (device // 4) % 2, (device // 2) % 2, device % 2
        z, y, x, c = place(z, y, x, c)
        found.append((device, ((z * 2 + y) * 2 + x) * 2 + c))
    return found


FLIP = {
    "y": pairs(lambda z, y, x, c: (z, 1 - y, x, c)),
    "x": pairs(lambda z, y, x, c: (z, y, 1 - x, c)),
    "c": pairs(lambda z, y, x, c: (z, y, x, 1 - c)),
    "z1": pairs(lambda z, y, x, c: (z ^ 1, y, x, c)),
    "z2": pairs(lambda z, y, x, c: (z ^ 2, y, x, c)),
    "z3": pairs(lambda z, y, x, c: (z ^ 3, y, x, c)),
    "xc": pairs(lambda z, y, x, c: (z, y, 1 - x, 1 - c)),
}


def coordinates():
    dp, seq = lax.axis_index("dp"), lax.axis_index("seq")
    return {"z": dp // 2, "y": dp % 2, "x": seq // 2, "c": seq % 2}


def small_torus():
    return lax.axis_size("dp") == 8 and lax.axis_size("seq") == 4


def after(value, *others):
    return lax.optimization_barrier((value,) + others)[0]


def together(values, *others):
    return lax.optimization_barrier(tuple(values) + others)[: len(values)]


def ordered(own, came, mine, axis):
    return jnp.where(mine == 0, jnp.stack([own, came], axis), jnp.stack([came, own], axis))


def flip(block, name):
    return lax.ppermute(block, AXES, FLIP[name])


def join(block, name, axis):
    return ordered(block, flip(block, name), coordinates()[name], axis)


def half_sum(part, name, axis):
    me = coordinates()[name]
    away = lax.dynamic_index_in_dim(part, 1 - me, axis, False)
    kept = lax.dynamic_index_in_dim(part, me, axis, False)
    return kept.astype(F32) + flip(away, name).astype(F32)


def z_gather(shard):
    return jnp.stack([shard] + [flip(shard, name) for name in ("z1", "z2", "z3")])


def z_sum(parts):
    groups = [[0, 2, 4, 6], [1, 3, 5, 7]]
    came = lax.all_to_all(parts, "dp", 0, 0, axis_index_groups=groups, tiled=True)
    return jnp.sum(came.astype(F32), axis=0)


def seq_send(blocks):
    if not small_torus():
        came = relative(swap(relative(blocks), "seq"))
        return [came[k : k + 1] for k in range(blocks.shape[0])]
    return [blocks] + [flip(blocks[k : k + 1], name) for k, name in ((1, "c"), (2, "x"), (3, "xc"))]


def seq_send_twice(blocks):
    if not small_torus():
        return seq_send(blocks)
    far = flip(blocks[2:], "x")
    near = flip(jnp.concatenate([blocks[1:2], far[1:]]), "c")
    return [blocks, near[:1], far[:1], near[1:]]


def relative(blocks):
    places = jnp.arange(blocks.shape[0], dtype=jnp.int32) ^ lax.axis_index("seq").astype(jnp.int32)
    return blocks[places]


def copies_sum(kept, away):
    if not small_torus():
        blocks = relative(jnp.stack([kept[0], away[0], kept[1], away[1]]))
        return [lax.psum_scatter(blocks, "seq", scatter_dimension=0, tiled=False)], kept
    far = (kept[1].astype(F32) + away[1].astype(F32)).astype(BF16)
    return [kept[0], away[0], flip(far, "x")], far


def add_up(terms):
    return sum((term.astype(F32) for term in terms[1:]), terms[0].astype(F32))


def swap(blocks, axis):
    return lax.all_to_all(blocks, axis, split_axis=0, concat_axis=0, tiled=True)


def turned(rows, cosine, sine):
    a, b = rows[:32], rows[32:]
    return a * cosine - b * sine, b * cosine + a * sine


def first_norm(x):
    x = x.astype(F32)
    r1 = lax.rsqrt(jnp.mean(x * x, axis=1, keepdims=True) + EPS)
    return x * r1, r1


def gain_row(w_ref):
    last = w_ref.shape[1] - LANES
    return w_ref[:, last:].astype(F32).T[LANES // 2 : LANES // 2 + 1, :]


def assemble(parts, width_ref, place):
    first = 0
    for part in parts:
        for k in range(part.shape[0]):
            rows = part.shape[1]
            at = pl.multiple_of(place(first + k) * rows, 8)
            width_ref[pl.ds(at, rows), :] = part[k]
        first += part.shape[0]


def qkv_kernel(seq_ref, dp_ref, *refs, sources):
    x_refs, part_refs = refs[:sources], refs[sources:-5]
    cos_ref, sin_ref, out_ref, w_ref, xn_ref = refs[-5:]
    step = pl.program_id(0)

    @pl.when(step == 0)
    def _():
        if len(part_refs) == 1:
            assemble(part_refs, w_ref, lambda r: r)
        else:
            assemble(part_refs, w_ref, lambda r: dp_ref[0] ^ ((r & 3) << 1 | r >> 2))

    for k, x_ref in enumerate(x_refs):

        @pl.when(step == k)
        def _(x_ref=x_ref):
            z1, _ = first_norm(x_ref[...])
            xn_ref[...] = (z1 * gain_row(w_ref)).astype(BF16)

    rows = mm(xn_ref[...], w_ref[...]).T
    cosine, sine = cos_ref[...], sin_ref[...]
    for base in range(0, out_ref.shape[1], 192):
        for c in range(2):
            at = base + c * 64
            a, b = turned(rows[at : at + 64], cosine, sine)
            out_ref[0, at : at + 32, :] = a.astype(BF16)
            out_ref[0, at + 32 : at + 64, :] = b.astype(BF16)
        out_ref[0, base + 128 : base + 192, :] = rows[base + 128 : base + 192].astype(BF16)


def qkv_project(seq, dp, xs, w_parts, cosine, sine):
    tokens, width = xs[0].shape
    across = w_parts[0].shape[2]
    columns = across - 64
    angles = pl.BlockSpec((32, tokens), lambda i, s, d: (0, i ^ s[0]))
    return pl.pallas_call(
        functools.partial(qkv_kernel, sources=len(xs)),
        grid_spec=pltpu.PrefetchScalarGridSpec(
            num_scalar_prefetch=2,
            grid=(len(xs),),
            in_specs=[pl.BlockSpec((tokens, width), lambda i, s, d: (0, 0))] * len(xs)
            + [pl.BlockSpec(part.shape, lambda i, s, d: (0, 0, 0)) for part in w_parts]
            + [angles, angles],
            out_specs=[
                pl.BlockSpec((1, columns, tokens), lambda i, s, d: (i ^ s[0], 0, 0)),
                pl.BlockSpec((width, across), lambda i, s, d: (0, 0)),
            ],
            scratch_shapes=[pltpu.VMEM((tokens, width), BF16)],
        ),
        out_shape=[
            jax.ShapeDtypeStruct((len(xs), columns, tokens), BF16),
            jax.ShapeDtypeStruct((width, across), BF16),
        ],
        compiler_params=params(1),
        cost_estimate=cost(1e9, 1 << 20),
        name="qkv_project",
    )(seq, dp, *xs, *w_parts, cosine, sine)


TILE = 256


def tile_of(ref, row, rows, index):
    per = ref.shape[2] // TILE
    at = (index % per) * TILE
    return ref[index // per, row : row + rows, at : at + TILE]


def flipped(block):
    return block.astype(F32).T.astype(BF16)


def masked(scores, start, i, j, diagonal):
    key = lax.broadcasted_iota(jnp.int32, scores.shape, 0)
    allowed = key >= start - j * TILE
    if diagonal:
        query = lax.broadcasted_iota(jnp.int32, scores.shape, 1)
        allowed = allowed & (key <= query)
    return jnp.where(allowed, scores, MASKED)


def start_of(docs):
    start = jnp.zeros_like(docs)
    for doc in range(1, 4):
        before = jnp.sum(jnp.where(docs < doc, 1, 0), axis=1, keepdims=True)
        start = jnp.where(docs >= doc, before, start)
    return start


def attend_kernel(seq_ref, buf_ref, docs_ref, ctx_ref, lse_ref, k_ref, s_ref, start_ref):
    start_ref[...] = start_of(docs_ref[...])
    tiles = buf_ref.shape[0] * buf_ref.shape[2] // TILE
    per = buf_ref.shape[2] // TILE
    for i in range(tiles):
        rows = slice(i * TILE, (i + 1) * TILE)
        k_ref[rows, :] = flipped(tile_of(buf_ref, 64, 64, i))
        q = (tile_of(buf_ref, 0, 64, i).astype(F32) * 0.125).astype(BF16)
        start = start_ref[0:1, rows]
        top = jnp.full((1, TILE), MASKED, F32)
        for j in range(i + 1):
            keys = slice(j * TILE, (j + 1) * TILE)
            scores = masked(mm(k_ref[keys, :], q), start, i, j, i == j)
            s_ref[keys, :] = scores
            top = jnp.maximum(top, jnp.max(scores, axis=0, keepdims=True))
        total = jnp.zeros((1, TILE), F32)
        context = jnp.zeros((64, TILE), F32)
        for j in range(i + 1):
            probs = jnp.exp(s_ref[j * TILE : (j + 1) * TILE, :] - top)
            total = total + jnp.sum(probs, axis=0, keepdims=True)
            context = context + mm(tile_of(buf_ref, 128, 64, j), probs.astype(BF16))
        at = (i % per) * TILE
        ctx_ref[(i // per) ^ seq_ref[0], :, at : at + TILE] = (context / total).astype(BF16)
        lse_ref[0, 0:1, rows] = top + jnp.log(total)


def attend(seq, buf, docs):
    blocks, rows, tokens = buf.shape
    heads, length = rows // 192, blocks * tokens
    return pl.pallas_call(
        attend_kernel,
        grid_spec=pltpu.PrefetchScalarGridSpec(
            num_scalar_prefetch=1,
            grid=(heads,),
            in_specs=[
                pl.BlockSpec((blocks, 192, tokens), lambda h, s: (0, h, 0)),
                pl.BlockSpec((1, length), lambda h, s: (0, 0)),
            ],
            out_specs=[
                pl.BlockSpec((blocks, 64, tokens), lambda h, s: (0, h, 0)),
                pl.BlockSpec((1, 1, length), lambda h, s: (h, 0, 0)),
            ],
            scratch_shapes=[
                pltpu.VMEM((length, 64), BF16),
                pltpu.VMEM((length, TILE), F32),
                pltpu.VMEM((1, length), jnp.int32),
            ],
        ),
        out_shape=[
            jax.ShapeDtypeStruct((blocks, heads * 64, tokens), BF16),
            jax.ShapeDtypeStruct((heads, 1, length), F32),
        ],
        compiler_params=params(1),
        cost_estimate=cost(3e9, 1 << 20),
        name="attend",
    )(seq, buf, docs)


def attend_back_kernel(
    seq_ref, buf_ref, d0_ref, d1_ref, d2_ref, d3_ref, ctx_ref, lse_ref, docs_ref, out_ref,
    k_ref, v_ref, dk_ref, dv_ref, start_ref, dctx_ref,
):
    for k, block_ref in enumerate((d0_ref, d1_ref, d2_ref, d3_ref)):
        dctx_ref[k ^ seq_ref[0]] = block_ref[0]
    start_ref[...] = start_of(docs_ref[...])
    tiles = buf_ref.shape[0] * buf_ref.shape[2] // TILE
    per = buf_ref.shape[2] // TILE
    for i in range(tiles):
        rows = slice(i * TILE, (i + 1) * TILE)
        k_ref[rows, :] = flipped(tile_of(buf_ref, 64, 64, i))
        v_ref[rows, :] = flipped(tile_of(buf_ref, 128, 64, i))
        q_t = (tile_of(buf_ref, 0, 64, i).astype(F32) * 0.125).astype(BF16)
        d_t = tile_of(dctx_ref, 0, 64, i)
        q_rows, d_rows = flipped(q_t), flipped(d_t)
        at = (i % per) * TILE
        context = ctx_ref[(i // per) ^ seq_ref[0], :, at : at + TILE].astype(F32)
        delta = jnp.sum(d_t.astype(F32) * context, axis=0, keepdims=True)
        start, log_total = start_ref[0:1, rows], lse_ref[0, 0:1, rows]
        d_query = jnp.zeros((64, TILE), F32)
        for j in range(i + 1):
            keys = slice(j * TILE, (j + 1) * TILE)
            scores = masked(mm(k_ref[keys, :], q_t), start, i, j, i == j)
            probs = jnp.exp(scores - log_total)
            d_probs = mm(v_ref[keys, :], d_t)
            d_scores = (probs * (d_probs - delta)).astype(BF16)
            d_query = d_query + mm(tile_of(buf_ref, 64, 64, j), d_scores)
            d_key = mm(d_scores, q_rows)
            d_value = mm(probs.astype(BF16), d_rows)
            if i == j:
                dk_ref[keys, :] = d_key
                dv_ref[keys, :] = d_value
            else:
                dk_ref[keys, :] += d_key
                dv_ref[keys, :] += d_value
        at = (i % per) * TILE
        out_ref[i // per, 0:64, at : at + TILE] = (d_query * 0.125).astype(BF16)
    for i in range(tiles):
        at = (i % per) * TILE
        rows = slice(i * TILE, (i + 1) * TILE)
        out_ref[i // per, 64:128, at : at + TILE] = dk_ref[rows, :].T.astype(BF16)
        out_ref[i // per, 128:192, at : at + TILE] = dv_ref[rows, :].T.astype(BF16)


def attend_back(seq, buf, dctxs, ctx, lse, docs, head):
    blocks, rows, tokens = buf.shape
    length = blocks * tokens
    one = pl.BlockSpec((blocks, 64, tokens), lambda i, s: (0, head, 0))
    return pl.pallas_call(
        attend_back_kernel,
        grid_spec=pltpu.PrefetchScalarGridSpec(
            num_scalar_prefetch=1,
            grid=(1,),
            in_specs=[
                pl.BlockSpec((blocks, 192, tokens), lambda i, s: (0, head, 0)),
                *[pl.BlockSpec((1, 64, tokens), lambda i, s: (0, head, 0))] * 4,
                one,
                pl.BlockSpec((1, 1, length), lambda i, s: (head, 0, 0)),
                pl.BlockSpec((1, length), lambda i, s: (0, 0)),
            ],
            out_specs=pl.BlockSpec((blocks, 192, tokens), lambda i, s: (0, 0, 0)),
            scratch_shapes=[pltpu.VMEM((length, 64), BF16)] * 2
            + [pltpu.VMEM((length, 64), F32)] * 2
            + [pltpu.VMEM((1, length), jnp.int32), pltpu.VMEM((blocks, 64, tokens), BF16)],
        ),
        out_shape=jax.ShapeDtypeStruct((blocks, 192, tokens), BF16),
        compiler_params=params(1),
        cost_estimate=cost(4e9, 1 << 20),
        name="attend_back",
    )(seq, buf, *dctxs, ctx, lse, docs)


def zyx_of(r):
    return (r & 3) << 2 | (r >> 2 & 1) << 1 | r >> 3


def middle_kernel(me_ref, seq_ref, *refs, experts, sources, parts):
    ctx_refs, w_refs = refs[:sources], refs[sources : -9 - parts]
    x_ref, pick_ref, routes_ref = refs[-9 - parts : -6 - parts]
    hidden_ref, hn_ref, gates_ref, attn_ref, misc_ref, ctx_ref = refs[-6 - parts : -parts]
    send_refs = refs[-parts:]
    width = x_ref.shape[1]
    first = 0
    for w_ref in w_refs:
        blocks, rows = w_ref.shape[0], w_ref.shape[1]
        for k in range(blocks):
            place = me_ref[0] ^ zyx_of(first + k)
            at = pl.ds(pl.multiple_of(place * rows, 16), rows)
            attn_ref[at, :] = w_ref[k, :, :width]
            misc_ref[at, :] = w_ref[k, :, width:]
        first += blocks
    for k, block_ref in enumerate(ctx_refs):
        rows = block_ref.shape[1]
        at = pl.ds(pl.multiple_of((seq_ref[0] ^ k) * rows, 16), rows)
        ctx_ref[at, :] = block_ref[0]
    hidden = x_ref[...].astype(F32) + mm(ctx_ref[...], attn_ref[...], TN)
    hidden_ref[...] = hidden
    r2 = lax.rsqrt(jnp.mean(hidden * hidden, axis=1, keepdims=True) + EPS)
    gain = misc_ref[...].astype(F32).T[experts : experts + 1, :]
    hn = (hidden * r2 * gain).astype(BF16)
    hn_ref[...] = hn
    first = 0
    for send_ref in send_refs:
        slots = send_ref.shape[0]
        send_ref[...] = mm(pick_ref[first : first + slots, :], hn).astype(BF16)
        first += slots
    logits = mm(hn, misc_ref[...])
    lane = lax.broadcasted_iota(jnp.int32, logits.shape, 1)
    first = jnp.sum(jnp.where(lane == routes_ref[:, 0:1], logits, 0.0), axis=1, keepdims=True)
    second = jnp.sum(jnp.where(lane == routes_ref[:, 1:2], logits, 0.0), axis=1, keepdims=True)
    top = jnp.maximum(first, second)
    first, second = jnp.exp(first - top), jnp.exp(second - top)
    total = first + second
    gates_ref[...] = jnp.where(lane == 0, first / total, jnp.where(lane == 1, second / total, 0.0))


def middle(me, seq, ctxs, x, w_parts, pick, routes, experts, parts):
    tokens, width = x.shape
    first = pl.BlockSpec((1,) + ctxs[0].shape[1:], lambda i, m, s: (0, 0, 0))

    def full(array):
        return pl.BlockSpec(array.shape, lambda i, m, s: (0,) * len(array.shape))

    out_shape = [
        jax.ShapeDtypeStruct((tokens, width), F32),
        jax.ShapeDtypeStruct((tokens, width), BF16),
        jax.ShapeDtypeStruct((tokens, LANES), F32),
        jax.ShapeDtypeStruct((width, width), BF16),
        jax.ShapeDtypeStruct((width, LANES), BF16),
        jax.ShapeDtypeStruct((width, tokens), BF16),
    ] + [jax.ShapeDtypeStruct((experts * part, width), BF16) for part in parts]
    return pl.pallas_call(
        functools.partial(middle_kernel, experts=experts, sources=len(ctxs), parts=len(parts)),
        grid_spec=pltpu.PrefetchScalarGridSpec(
            num_scalar_prefetch=2,
            grid=(1,),
            in_specs=[first] * len(ctxs) + [full(array) for array in (*w_parts, x, pick, routes)],
            out_specs=[full(array) for array in out_shape],
        ),
        out_shape=out_shape,
        compiler_params=params(1),
        cost_estimate=cost(5e8, 1 << 20),
        name="middle",
    )(me, seq, *ctxs, *w_parts, x, pick, routes)


def swiglu(gate, up, d_act):
    sigma = jax.nn.sigmoid(gate)
    act = (gate * sigma * up).astype(BF16)
    d_gate = (d_act * up * sigma * (1.0 + gate * (1.0 - sigma))).astype(BF16)
    d_up = (d_act * gate * sigma).astype(BF16)
    return act, d_gate, d_up


def dense_kernel(
    x_ref, dy_ref, wg_ref, wu_ref, wo_ref, y_ref, dx_ref, gg_ref, gu_ref, go_ref, xt_ref
):
    @pl.when(pl.program_id(0) == 0)
    def _():
        y_ref[...] = jnp.zeros_like(y_ref)
        dx_ref[...] = jnp.zeros_like(dx_ref)
        xt_ref[...] = flipped(x_ref[...])

    x, dy = x_ref[...], dy_ref[...]
    act, d_gate, d_up = swiglu(mm(x, wg_ref[...]), mm(x, wu_ref[...]), mm(dy, wo_ref[...], NT))
    y_ref[...] += mm(act, wo_ref[...])
    dx_ref[...] += mm(d_gate, wg_ref[...], NT) + mm(d_up, wu_ref[...], NT)
    gg_ref[...] = mm(xt_ref[...], d_gate).astype(BF16)
    gu_ref[...] = mm(xt_ref[...], d_up).astype(BF16)
    go_ref[...] = mm(act, dy, TN).astype(BF16)


def dense(x, dy, w_gate, w_up, w_out, tile=256):
    tokens, width = x.shape
    units = w_out.shape[0]
    rows = pl.BlockSpec((tokens, width), lambda j: (0, 0))
    tall = pl.BlockSpec((width, tile), lambda j: (0, j))
    wide = pl.BlockSpec((tile, width), lambda j: (j, 0))
    return pl.pallas_call(
        dense_kernel,
        grid=(units // tile,),
        in_specs=[rows, rows, tall, tall, wide],
        out_specs=[rows, rows, tall, tall, wide],
        out_shape=[
            jax.ShapeDtypeStruct((tokens, width), F32),
            jax.ShapeDtypeStruct((tokens, width), F32),
            jax.ShapeDtypeStruct((width, units), BF16),
            jax.ShapeDtypeStruct((width, units), BF16),
            jax.ShapeDtypeStruct((units, width), BF16),
        ],
        scratch_shapes=[pltpu.VMEM((width, tokens), BF16)],
        compiler_params=params(1),
        cost_estimate=cost(18 * tokens * width * units, 30 << 20),
        name="dense",
    )(x, dy, w_gate, w_up, w_out)


def paired_kernel(me_ref, x_ref, dy_ref, *refs):
    parts_a, parts_b = refs[0:3], refs[3:6]
    y_ref, dx_ref, share_ref, ka_ref, wa_ref, kb_ref, wb_ref = refs[6:13]
    xt_ref, y_acc, dx_acc, all_a, all_b, sum_a, sum_b = refs[13:]
    step = pl.program_id(0)
    tokens, width = y_ref.shape
    me = me_ref[0]

    def place_a(r):
        return me ^ zyx_of(r)

    def place_b(r):
        return me ^ ((r & 3) << 2 | (r >> 3) << 1 | (r >> 2 & 1))

    def z_kept(place):
        return lambda r: place(r) ^ (me & 12)

    @pl.when(step == 0)
    def _():
        y_acc[...] = jnp.zeros_like(y_acc)
        dx_acc[...] = jnp.zeros_like(dx_acc)
        xt_ref[...] = flipped(x_ref[...])
        for parts, every, place in ((parts_a, all_a, place_a), (parts_b, all_b, place_b)):
            first = 0
            for part in parts:
                for k in range(part.shape[0]):
                    every[place(first + k)] = part[k]
                first += part.shape[0]

    at = pl.ds(pl.multiple_of(step * 48, 16), 48)
    four = pl.ds(step * 4, 4)
    wg, wu = all_a[:, at, :].reshape(width, 256), all_b[:, at, :].reshape(width, 256)
    wo = jnp.concatenate(
        [
            jnp.concatenate(
                [half[four, 192 + k * 32 : 224 + k * 32, :] for half in (all_a, all_b)], axis=1
            ).reshape(256, 256)
            for k in range(width // 256)
        ],
        axis=1,
    )
    x, dy = x_ref[...], dy_ref[...]
    act, d_gate, d_up = swiglu(mm(x, wg), mm(x, wu), mm(dy, wo, NT))
    y_acc[...] += mm(act, wo)
    dx_acc[...] += mm(d_gate, wg, NT) + mm(d_up, wu, NT)
    sum_a[:, at, :] = mm(xt_ref[...], d_gate).astype(BF16).reshape(16, 48, 256)
    sum_b[:, at, :] = mm(xt_ref[...], d_up).astype(BF16).reshape(16, 48, 256)
    go = mm(act, dy, TN).astype(BF16).reshape(4, 64, width)
    for k in range(width // 256):
        block = go[:, :, k * 256 : k * 256 + 256]
        sum_a[four, 192 + k * 32 : 224 + k * 32, :] = block[:, :32]
        sum_b[four, 192 + k * 32 : 224 + k * 32, :] = block[:, 32:]

    @pl.when(step == pl.num_programs(0) - 1)
    def _():
        y_ref[...] = y_acc[:tokens, :]
        dx_ref[...] = dx_acc[:tokens, :]
        share_ref[:tokens, :] = y_acc[tokens:, :].astype(BF16)
        share_ref[tokens:, :] = dx_acc[tokens:, :].astype(BF16)
        for kept, away, total, place in (
            (ka_ref, wa_ref, sum_a, z_kept(place_a)),
            (kb_ref, wb_ref, sum_b, z_kept(place_b)),
        ):
            for r in range(8):
                kept[r] = total[place(r)]
                away[r] = total[place(r + 8)]


def paired(me, x, dy, parts_a, parts_b):
    every, width = x.shape
    tokens = every // 2
    block = parts_a[0].shape[1:]
    rows = pl.BlockSpec((every, width), lambda j, s: (0, 0))
    part = pl.BlockSpec((tokens, width), lambda j, s: (0, 0))

    def blocks(count):
        return pl.BlockSpec((count,) + block, lambda j, s: (0, 0, 0))

    return pl.pallas_call(
        paired_kernel,
        grid_spec=pltpu.PrefetchScalarGridSpec(
            num_scalar_prefetch=1,
            grid=(4,),
            in_specs=[rows, rows] + [blocks(4), blocks(4), blocks(8)] * 2,
            out_specs=[part, part, rows] + [blocks(8)] * 4,
            scratch_shapes=[pltpu.VMEM((width, every), BF16)]
            + [pltpu.VMEM((every, width), F32)] * 2
            + [pltpu.VMEM((16,) + block, BF16)] * 4,
        ),
        out_shape=[
            jax.ShapeDtypeStruct((tokens, width), F32),
            jax.ShapeDtypeStruct((tokens, width), F32),
            jax.ShapeDtypeStruct((every, width), BF16),
        ]
        + [jax.ShapeDtypeStruct((8,) + block, BF16)] * 4,
        compiler_params=params(1, 60),
        cost_estimate=cost(18 * every * width * 1024, 30 << 20),
        name="dense_pair",
    )(me, x, dy, *parts_a, *parts_b)


def lane_row(column):
    shape = (column.shape[0], LANES)
    here = lax.broadcasted_iota(jnp.int32, shape, 0) == lax.broadcasted_iota(jnp.int32, shape, 1)
    return jnp.sum(jnp.where(here, column, 0.0), axis=0, keepdims=True)


def noted(columns):
    row = lax.broadcasted_iota(jnp.int32, (16, LANES), 0)
    tile = jnp.zeros((16, LANES), F32)
    for k, column in enumerate(columns):
        values = lane_row(column)
        high = values.astype(BF16).astype(F32)
        tile = jnp.where(row == 2 * k, high, jnp.where(row == 2 * k + 1, values - high, tile))
    return tile.astype(BF16)


def expert_kernel(own_ref, x_ref, dy_ref, other_ref, misc_ref, wg_ref, wu_ref, wo_ref, *refs, low):
    y_ref, dx_ref, dgate_ref, deo_ref, act_ref, dg_ref, du_ref, y_acc, dx_acc = refs[-9:]
    earlier_refs = refs[:-9]
    step = pl.program_id(0)

    def dy_rows():
        if len(dy_ref.shape) == 2:
            return dy_ref[...]
        part = x_ref.shape[0] // dy_ref.shape[0]
        return dy_ref[:, low : low + part, :].reshape(x_ref.shape)

    @pl.when(step == 0)
    def _():
        y_acc[...] = jnp.zeros_like(y_acc)
        dx_acc[...] = jnp.zeros_like(dx_acc)
        logits = mm(x_ref[...], misc_ref[...])
        lane = lax.broadcasted_iota(jnp.int32, logits.shape, 1)
        other = other_ref[...].astype(jnp.int32)
        mine = jnp.sum(jnp.where(lane == own_ref[0], logits, 0.0), axis=1, keepdims=True)
        theirs = jnp.sum(jnp.where(lane == other, logits, 0.0), axis=1, keepdims=True)
        top = jnp.maximum(mine, theirs)
        mine, theirs = jnp.exp(mine - top), jnp.exp(theirs - top)
        deo_ref[...] = (mine / (mine + theirs) * dy_rows().astype(F32)).astype(BF16)

    x, deo = x_ref[...], deo_ref[...]
    wg, wu, wo = wg_ref[0], wu_ref[0], wo_ref[0]
    act, d_gate, d_up = swiglu(mm(x, wg), mm(x, wu), mm(deo, wo, NT))
    y_acc[...] += mm(act, wo)
    dx_acc[...] += mm(d_gate, wg, NT) + mm(d_up, wu, NT)
    act_ref[...] = act
    dg_ref[...] = d_gate
    du_ref[...] = d_up

    @pl.when(step == pl.num_programs(0) - 1)
    def _():
        y = y_acc[...].astype(BF16)
        y_ref[...] = y
        dgate = jnp.sum(y.astype(F32) * dy_rows().astype(F32), axis=1, keepdims=True)
        dgate_ref[...] = dgate
        if not earlier_refs:
            dx_ref[...] = dx_acc[...].astype(BF16)
        else:
            sources = dx_ref.shape[0]
            part, before = dgate.shape[0] // sources, earlier_refs[0].shape[0] // sources
            dx_ref[:, :part, :] = dx_acc[...].astype(BF16).reshape(sources, part, dx_ref.shape[2])
            dx_ref[:, part:, LANES:] = jnp.zeros((sources, 16, dx_ref.shape[2] - LANES), BF16)
            for k in range(sources):
                dx_ref[k, part:, :LANES] = noted(
                    [
                        dgate[k * part : (k + 1) * part],
                        earlier_refs[0][k * before : (k + 1) * before, :],
                    ]
                )


def expert(own, x, dy, low, other, misc, w_in, w_out, earlier=None, tile=256):
    slots, width = x.shape
    units = w_out.shape[1]
    steps = units // tile
    rows = pl.BlockSpec((slots, width), lambda j, s: (0, 0))
    column = pl.BlockSpec((slots, 1), lambda j, s: (0, 0))
    saved = pl.BlockSpec((slots, tile), lambda j, s: (0, j))
    every = pl.BlockSpec(dy.shape, lambda j, s: (0,) * len(dy.shape))
    dx_shape, more = (slots, width), []
    if earlier is not None:
        dx_shape, more = (dy.shape[0], slots // dy.shape[0] + 16, width), [earlier]
    dx_spec = pl.BlockSpec(dx_shape, lambda j, s: (0,) * len(dx_shape))
    return pl.pallas_call(
        functools.partial(expert_kernel, low=low),
        grid_spec=pltpu.PrefetchScalarGridSpec(
            num_scalar_prefetch=1,
            grid=(steps,),
            in_specs=[
                rows,
                every,
                column,
                pl.BlockSpec(misc.shape, lambda j, s: (0, 0)),
                pl.BlockSpec((1, width, tile), lambda j, s: (0, 0, j)),
                pl.BlockSpec((1, width, tile), lambda j, s: (0, 0, j + steps)),
                pl.BlockSpec((1, tile, width), lambda j, s: (0, j, 0)),
                *[pl.BlockSpec(array.shape, lambda j, s: (0, 0)) for array in more],
            ],
            out_specs=[rows, dx_spec, column, rows, saved, saved, saved],
            scratch_shapes=[pltpu.VMEM((slots, width), F32)] * 2,
        ),
        out_shape=[
            jax.ShapeDtypeStruct((slots, width), BF16),
            jax.ShapeDtypeStruct(dx_shape, BF16),
            jax.ShapeDtypeStruct((slots, 1), F32),
            jax.ShapeDtypeStruct((slots, width), BF16),
        ]
        + [jax.ShapeDtypeStruct((slots, units), BF16)] * 3,
        compiler_params=params(1),
        cost_estimate=cost(12 * slots * width * units, 40 << 20),
        name="expert",
    )(own, x, dy, other, misc, w_in, w_in, w_out, *more)


def expert_grads_kernel(seq_ref, *refs):
    count = (len(refs) - 4) // 6
    sets = [refs[k * 5 : k * 5 + 5] for k in range(count)]
    in_kept, in_away, out_kept, out_away = refs[5 * count : 5 * count + 4]
    turned_x = refs[5 * count + 4 :]
    step, half = pl.program_id(0), pl.num_programs(0) // 2

    @pl.when(step == 0)
    def _():
        for xt_ref, one in zip(turned_x, sets, strict=True):
            xt_ref[...] = flipped(one[0][...])

    def total(of):
        return sum((of(k) for k in range(1, count)), of(0)).astype(BF16)

    gate = total(lambda k: mm(turned_x[k][...], sets[k][3][...]))
    up = total(lambda k: mm(turned_x[k][...], sets[k][4][...]))
    down = total(lambda k: mm(sets[k][2][...], sets[k][1][...], TN))
    across = seq_ref[0] // 2

    def put(in_ref, out_ref):
        in_ref[across] = gate
        in_ref[1 - across] = up
        out_ref[0] = down

    @pl.when(step < half)
    def _():
        put(in_away, out_away)

    @pl.when(step >= half)
    def _():
        put(in_kept, out_kept)


def expert_grads(seq, sets, tile=256):
    width, units = sets[0][0].shape[1], sets[0][2].shape[1]
    steps = units // tile
    half = steps // 2
    part = units // 4

    def core_of(j, s):
        return jnp.where(j < half, 1 - s[0] % 2, s[0] % 2)

    def inner(j, s):
        return core_of(j, s) * half + j % half

    def outer(j, s):
        owner = 2 * ((s[0] // 2) ^ (j % half // (half // 2))) + core_of(j, s)
        return owner * (half // 2) + j % (half // 2)

    in_specs = []
    for x, *_ in sets:
        rows = pl.BlockSpec(x.shape, lambda j, s: (0, 0))
        saved = pl.BlockSpec((x.shape[0], tile), lambda j, s: (0, inner(j, s)))
        acts = pl.BlockSpec((x.shape[0], tile), lambda j, s: (0, outer(j, s)))
        in_specs += [rows, rows, acts, saved, saved]

    def kept(j):
        return jnp.maximum(j - half, 0)

    def away(j):
        return jnp.minimum(j, half - 1)

    def places(of):
        return [
            pl.BlockSpec((2, width, tile), lambda j, s: (0, 0, of(j))),
            pl.BlockSpec(
                (1, tile, width), lambda j, s: (of(j) // (half // 2), of(j) % (half // 2), 0)
            ),
        ]

    keeps, aways = places(kept), places(away)
    in_shape = jax.ShapeDtypeStruct((2, width, 2 * part), BF16)
    out_shape = jax.ShapeDtypeStruct((2, part, width), BF16)
    slots = sum(one[0].shape[0] for one in sets)
    return pl.pallas_call(
        expert_grads_kernel,
        grid_spec=pltpu.PrefetchScalarGridSpec(
            num_scalar_prefetch=1,
            grid=(steps,),
            in_specs=in_specs,
            out_specs=[keeps[0], aways[0], keeps[1], aways[1]],
            scratch_shapes=[pltpu.VMEM((width, one[0].shape[0]), BF16) for one in sets],
        ),
        out_shape=[in_shape, in_shape, out_shape, out_shape],
        compiler_params=params(1),
        cost_estimate=cost(2 * slots * width * units, 4 << 20),
        name="expert_grads",
    )(seq, *[array for one in sets for array in one])


def share_block(tokens, width, index):
    return pl.BlockSpec((tokens, width), lambda i: (index, 0))


def middle_back_kernel(
    dhn_ref, share_ref, slots_ref, routes_ref, gates_ref, misc_ref, hidden_ref, hn_ref,
    dy_ref, ctx_ref, w_ref, seq_ref, *refs, experts, parts,
):
    back_refs, (dh_ref, dctx_ref, grad_ref) = refs[:-3], refs[-3:]
    tokens = dhn_ref.shape[0]
    slots = experts * sum(parts)
    place = lax.broadcasted_iota(jnp.int32, (tokens, slots), 1)
    is0, is1 = place == slots_ref[:, 0:1], place == slots_ref[:, 1:2]
    pick = jnp.where(is0 | is1, 1.0, 0.0).astype(BF16)
    came = jnp.zeros(hidden_ref.shape, F32)
    first = 0
    for part, back_ref in zip(parts, back_refs, strict=False):
        rows = experts * part
        back = back_ref[...]
        if len(back.shape) == 3:
            back = back[:, :part, :].reshape(rows, back.shape[2])
        came = came + mm(pick[:, first : first + rows], back)
        first += rows
    if len(parts) == 1:
        dgate = back_refs[1][...]
        dg0 = jnp.sum(jnp.where(is0, dgate, 0.0), axis=1, keepdims=True)
        dg1 = jnp.sum(jnp.where(is1, dgate, 0.0), axis=1, keepdims=True)
    else:
        notes = back_refs[1][:, parts[1] :, :LANES].astype(F32)
        tables = [notes[:, 2, :] + notes[:, 3, :], notes[:, 0, :] + notes[:, 1, :]]
        spot = lax.broadcasted_iota(jnp.int32, (tokens, LANES), 1)
        found = []
        for k in range(2):
            route, slot = routes_ref[:, k : k + 1], slots_ref[:, k : k + 1]
            value, first = jnp.zeros((tokens, 1), F32), 0
            for part, table in zip(parts, tables, strict=True):
                line = jnp.zeros((tokens, LANES), F32)
                for e in range(experts):
                    line = jnp.where(route == e, table[e : e + 1, :], line)
                inside = (slot >= first) & (slot < first + experts * part)
                here = inside & (spot == slot - first - route * part)
                value = value + jnp.sum(jnp.where(here, line, 0.0), axis=1, keepdims=True)
                first += experts * part
            found.append(value)
        dg0, dg1 = found
    g0, g1 = gates_ref[:, 0:1], gates_ref[:, 1:2]
    mean = g0 * dg0 + g1 * dg1
    lane = lax.broadcasted_iota(jnp.int32, (tokens, LANES), 1)
    dlogits = (
        jnp.where(lane == routes_ref[:, 0:1], g0 * (dg0 - mean), 0.0)
        + jnp.where(lane == routes_ref[:, 1:2], g1 * (dg1 - mean), 0.0)
    ).astype(BF16)
    misc = misc_ref[...]
    dhn = dhn_ref[...] + share_ref[...].astype(F32) + mm(dlogits, misc, NT) + came
    hidden = hidden_ref[...]
    r2 = lax.rsqrt(jnp.mean(hidden * hidden, axis=1, keepdims=True) + EPS)
    z2 = hidden * r2
    gain = misc.astype(F32).T[experts : experts + 1, :]
    gain_grad = jnp.sum(dhn * z2, axis=0, keepdims=True)
    dz2 = dhn * gain
    dh = dy_ref[...].astype(F32) + r2 * (dz2 - z2 * jnp.mean(dz2 * z2, axis=1, keepdims=True))
    dh_ref[...] = dh
    dhb = dh.astype(BF16)
    for k in range(dctx_ref.shape[0]):
        rows = dctx_ref.shape[1]
        at = pl.ds(pl.multiple_of((seq_ref[0] ^ k) * rows, 16), rows)
        dctx_ref[k] = mm(w_ref[at, :], dhb, NT).astype(BF16)
    width = w_ref.shape[0]
    grad_ref[:, :width] = mm(ctx_ref[...], dhb).astype(BF16)
    small = mm(dlogits, hn_ref[...], TN)
    row = lax.broadcasted_iota(jnp.int32, small.shape, 0)
    small = jnp.where(row == experts, gain_grad, small)
    grad_ref[:, width:] = small.T.astype(BF16)


def middle_back(dhn, share, backs, slots, routes, gates, misc, hidden, hn, dy, ctx, w_attn, seq, seq_devs, experts, parts):
    tokens, width = hidden.shape
    return pl.pallas_call(
        functools.partial(middle_back_kernel, experts=experts, parts=parts),
        grid=(1,),
        in_specs=[whole(), share_block(tokens, width, 1)]
        + [whole()] * 9
        + [pl.BlockSpec(memory_space=pltpu.SMEM)]
        + [whole()] * len(backs),
        out_specs=[whole()] * 3,
        out_shape=[
            jax.ShapeDtypeStruct((tokens, width), F32),
            jax.ShapeDtypeStruct((seq_devs, width // seq_devs, tokens), BF16),
            jax.ShapeDtypeStruct((width, width + LANES), BF16),
        ],
        compiler_params=params(),
        cost_estimate=cost(3e9, 16 << 20),
        name="middle_back",
    )(dhn, share, slots, routes, gates, misc, hidden, hn, dy, ctx, w_attn, seq, *backs)


def output_kernel(hidden_ref, dense_ref, share_ref, slots_ref, gates_ref, *refs):
    came_refs, out_ref = refs[:-1], refs[-1]
    mixture = jnp.zeros(hidden_ref.shape, F32)
    first = 0
    for came_ref in came_refs:
        tokens, slots = hidden_ref.shape[0], came_ref.shape[0]
        place = first + lax.broadcasted_iota(jnp.int32, (tokens, slots), 1)
        for k in range(2):
            pick = jnp.where(place == slots_ref[:, k : k + 1], 1.0, 0.0).astype(BF16)
            mixture = mixture + gates_ref[:, k : k + 1] * mm(pick, came_ref[...])
        first += slots
    out_ref[...] = hidden_ref[...] + dense_ref[...] + share_ref[...].astype(F32) + mixture


def output_of(hidden, shared, share, cames, slots, gates):
    return pl.pallas_call(
        output_kernel,
        grid=(1,),
        in_specs=[whole(), whole(), share_block(*hidden.shape, 0)] + [whole()] * (2 + len(cames)),
        out_specs=whole(),
        out_shape=jax.ShapeDtypeStruct(hidden.shape, F32),
        compiler_params=params(),
        cost_estimate=cost(2e9, 8 << 20),
        name="output_of",
    )(hidden, shared, share, slots, gates, *cames)


def qkv_back_kernel(seq_ref, *refs):
    count = len(ORDER)
    x_refs, d_refs, refs = refs[:count], refs[count:-9], refs[-9:]
    w_ref, cos_ref, sin_ref, kept_ref, away_ref, g_ref, acc_ref, gain_ref, z_ref = refs
    step = pl.program_id(0)
    columns = w_ref.shape[1] - 64

    @pl.when(step == 0)
    def _():
        acc_ref[...] = jnp.zeros_like(acc_ref)
        gain_ref[...] = jnp.zeros_like(gain_ref)

    for at_step, k in enumerate(ORDER):

        @pl.when(step == at_step)
        def _(x_ref=x_refs[k]):
            z_ref[...], _ = first_norm(x_ref[...])

    z1 = z_ref[...]
    xn_t = (z1 * gain_row(w_ref)).T.astype(BF16)
    cosine, sine = cos_ref[...], -sin_ref[...]
    pieces = []
    for d_ref in d_refs:
        for c in range(2):
            pieces.extend(turned(d_ref[0, c * 64 : c * 64 + 64, :].astype(F32), cosine, sine))
        pieces.append(d_ref[0, 128:192, :].astype(F32))
    pieces.append(jnp.zeros((64, z1.shape[0]), F32))
    d_rows = jnp.concatenate(pieces, axis=0).T.astype(BF16)
    dxn = mm(d_rows, w_ref[...], NT)
    acc_ref[...] += mm(xn_t, d_rows)
    gain_ref[0:1, :] += jnp.sum(dxn * z1, axis=0, keepdims=True)

    @pl.when(step < count // 2)
    def _():
        away_ref[0] = dxn.astype(BF16)

    @pl.when(step >= count // 2)
    def _():
        kept_ref[0] = dxn.astype(BF16)

    @pl.when(step == pl.num_programs(0) - 1)
    def _():
        split = columns + 64 - LANES
        g_ref[:, :split] = acc_ref[:, :split].astype(BF16)
        row = lax.broadcasted_iota(jnp.int32, (LANES, gain_ref.shape[1]), 0)
        gain = jnp.where(row == LANES // 2, gain_ref[0:1, :], 0.0).T
        g_ref[:, split:] = (acc_ref[:, split:] + gain).astype(BF16)


ORDER = (1, 3, 0, 2)


def qkv_back(seq, xs, d_heads, w, cosine, sine):
    tokens, width = xs[0].shape

    def place(i, s):
        k = jnp.where(i < 2, 2 * i + 1, 2 * i - 4)
        return k ^ s[0]

    angles = pl.BlockSpec((32, tokens), lambda i, s: (0, place(i, s)))
    rows = pl.BlockSpec((tokens, width), lambda i, s: (0, 0))
    grads = pl.BlockSpec((1, 192, tokens), lambda i, s: (place(i, s), 0, 0))
    pair = jax.ShapeDtypeStruct((2, tokens, width), BF16)
    return pl.pallas_call(
        qkv_back_kernel,
        grid_spec=pltpu.PrefetchScalarGridSpec(
            num_scalar_prefetch=1,
            grid=(len(ORDER),),
            in_specs=[rows] * len(xs)
            + [grads] * len(d_heads)
            + [pl.BlockSpec(w.shape, lambda i, s: (0, 0)), angles, angles],
            out_specs=[
                pl.BlockSpec((1, tokens, width), lambda i, s: (jnp.maximum(i - 2, 0), 0, 0)),
                pl.BlockSpec((1, tokens, width), lambda i, s: (jnp.minimum(i, 1), 0, 0)),
                pl.BlockSpec(w.shape, lambda i, s: (0, 0)),
            ],
            scratch_shapes=[
                pltpu.VMEM(w.shape, F32),
                pltpu.VMEM((8, width), F32),
                pltpu.VMEM((tokens, width), F32),
            ],
        ),
        out_shape=[pair, pair, jax.ShapeDtypeStruct(w.shape, BF16)],
        compiler_params=params(1),
        cost_estimate=cost(12e9, 12 << 20),
        name="qkv_back",
    )(seq, *xs, *d_heads, w, cosine, sine)


def input_back_kernel(x_ref, dh_ref, w_ref, *refs):
    dxn_refs, out_ref = refs[:-1], refs[-1]
    z1, r1 = first_norm(x_ref[...])
    dz1 = add_up([ref[...] for ref in dxn_refs]) * gain_row(w_ref)
    out_ref[...] = dh_ref[...] + r1 * (dz1 - z1 * jnp.mean(dz1 * z1, axis=1, keepdims=True))


def input_back(x, dh, w, dxns):
    return pl.pallas_call(
        input_back_kernel,
        in_specs=[whole()] * (3 + len(dxns)),
        out_specs=whole(),
        out_shape=jax.ShapeDtypeStruct(dh.shape, F32),
        compiler_params=params(),
        cost_estimate=cost(1e8, 6 << 20),
        name="input_back",
    )(x, dh, w, *dxns)


def slot_plan(routes, order, experts, parts):
    before = (order[:, None] > order[None, :]).astype(BF16)
    ids = jnp.arange(experts, dtype=jnp.int32)
    first = (routes[:, 0:1] == ids).astype(BF16)
    second = (routes[:, 1:2] == ids).astype(BF16)
    earlier = mm(before, jnp.concatenate([first, second], axis=1))
    every = jnp.sum(first.astype(F32), axis=0, keepdims=True)
    place0 = jnp.sum(earlier[:, :experts] * first.astype(F32), axis=1)
    place1 = jnp.sum((earlier[:, experts:] + every) * second.astype(F32), axis=1)
    place = jnp.stack([place0, place1], axis=1).astype(jnp.int32)
    capacity = sum(parts)
    every = jnp.where(place < capacity, routes * capacity + place, experts * capacity)
    slot = jnp.full(place.shape, experts * capacity, jnp.int32)
    low = 0
    for part in parts:
        inside = (place >= low) & (place < low + part)
        slot = jnp.where(inside, experts * low + routes * part + place - low, slot)
        low += part
    return slot, every


def padded(shard, columns):
    return jnp.pad(shard, ((0, 0), (0, columns - shard.shape[1])))


def by_core(columns):
    rows, count = columns.shape
    tiles = count // 512
    return columns.reshape(rows, tiles, 4, 2, 64).transpose(3, 1, 0, 2, 4).reshape(2, tiles, rows, 256)


def paired_shards(shared_in, shared_out):
    units, width = shared_in.shape[1] // 2, shared_out.shape[1]
    shard = jnp.stack([by_core(shared_in[:, :units]), by_core(shared_in[:, units:])], axis=1)
    me = coordinates()["c"]
    away = lax.dynamic_index_in_dim(shard, 1 - me, 0, False)
    kept = lax.dynamic_index_in_dim(shard, me, 0, False)
    inner = ordered(kept, flip(away, "c"), me, 2).reshape(2, -1, 256)
    down = shared_out.reshape(2, 32, width // 256, 256).transpose(0, 2, 1, 3).reshape(2, -1, 256)
    return jnp.concatenate([inner, down], axis=1)


def paired_grads(sum_a, sum_b):
    me = coordinates()["c"]
    inner = jnp.stack([sum_a[:192], sum_b[:192]]).reshape(2, 4, 2, 24, 256)
    away = lax.dynamic_index_in_dim(inner, 1 - me, 2, False)
    kept = lax.dynamic_index_in_dim(inner, me, 2, False)
    both = ordered(kept, flip(away, "c"), me, 0).reshape(2, 2, 4, 24, 4, 64)
    inner = both.transpose(3, 1, 2, 4, 0, 5).reshape(24, -1)
    down = jnp.stack([sum_a[192:], sum_b[192:]]).reshape(2, 3, 32, 256)
    return inner, down.transpose(0, 2, 1, 3).reshape(64, -1)


def scalar(value):
    return value.astype(jnp.int32).reshape(1)


def split_parts(array, sizes):
    found, low = [], 0
    for size in sizes:
        found.append(array[low : low + size])
        low += size
    return found


def on_device(
    layer_input, cotangent, segments, routes, order, norm1_gain, attn_qkv, attn_out,
    norm2_gain, router, shared_in, shared_out, expert_in, expert_out,
):
    tokens, width = layer_input.shape
    seq_devs = lax.axis_size("seq")
    experts = lax.axis_size("dp")
    capacity = max(2, (18 * tokens + 8 * experts - 1) // (8 * experts))
    small = small_torus()
    parts = (80, capacity - 80) if small and capacity == 144 else (capacity,)
    sizes = [experts * part for part in parts]
    slots = experts * capacity
    units = shared_in.shape[1] // 2
    columns = 3 * width // seq_devs
    seq = scalar(lax.axis_index("seq"))

    shard_rows = norm1_gain.shape[0]
    head_shard = jnp.concatenate(
        [
            attn_qkv.reshape(-1, seq_devs, columns).transpose(1, 0, 2),
            jnp.broadcast_to(norm1_gain[None, :, None], (seq_devs, shard_rows, 1)),
            jnp.zeros((seq_devs, shard_rows, 63), BF16),
        ],
        axis=2,
    )
    head_shard = swap(head_shard, "seq").reshape(-1, columns + 64)
    misc_shard = jnp.concatenate(
        [attn_out, padded(jnp.concatenate([router, norm2_gain[:, None]], axis=1), LANES)], axis=1
    )
    slot_of, expert_slot = slot_plan(routes, order, experts, parts)
    every_slot = jnp.arange(slots, dtype=jnp.int32)[:, None]

    def pick_of(rows):
        return ((every_slot == rows[0:1]) | (every_slot == rows[1:2])).astype(BF16)

    rows = expert_slot.T
    pick_dy = pick_of(rows)
    routes_f = routes.astype(F32)
    other = jnp.sum(
        jnp.where(every_slot == rows[0:1], routes_f[:, 1][None, :], 0.0)
        + jnp.where(every_slot == rows[1:2], routes_f[:, 0][None, :], 0.0),
        axis=1,
    ).reshape(experts, capacity)
    pick = pick_of(slot_of.T)
    dy_send = mm(pick_dy, cotangent).astype(BF16).reshape(experts, capacity, width)
    frequency = BASE ** (-(jnp.arange(32, dtype=F32) * 2.0 / 64))
    places = jnp.arange(tokens * seq_devs, dtype=jnp.int32)
    angles = places.astype(F32)[None, :] * frequency[:, None]
    cosine, sine = jnp.cos(angles), jnp.sin(angles)

    block_rows = head_shard.shape[0]
    extra = -(-capacity // block_rows)
    notes = jnp.pad(other.astype(BF16), ((0, 0), (0, extra * block_rows - capacity)))
    notes = notes.reshape(experts, block_rows, extra)
    packed = jnp.concatenate(
        [
            jnp.broadcast_to(head_shard[None, :, : columns + 1], (experts, block_rows, columns + 1)),
            notes,
            jnp.zeros((experts, block_rows, 63 - extra), BF16),
        ],
        axis=2,
    )
    packed = swap(packed, "dp")
    w_parts = [packed.reshape(1, -1, columns + 64)]
    notes = packed[:, :, columns + 1 : columns + 1 + extra].reshape(experts, -1)[:, :capacity]
    others, low = [], 0
    for part in parts:
        others.append(notes[:, low : low + part].astype(F32).reshape(-1, 1))
        low += part
    if small:
        here = coordinates()
        me = scalar(here["z"] * 4 + here["y"] * 2 + here["x"])
        along_x = flip(after(layer_input, head_shard), "x")
        token_blocks = [layer_input, flip(layer_input, "c"), along_x, flip(along_x, "c")]
        misc_z = z_gather(after(join(misc_shard, "c", 0).reshape(48, -1), *w_parts))
        misc_parts = [misc_z, flip(after(misc_z, *w_parts), "y")]
    else:
        me = jnp.zeros((1,), jnp.int32)
        gathered = relative(lax.all_gather(layer_input, "seq", axis=0, tiled=False))
        token_blocks = [gathered[k] for k in range(seq_devs)]
        misc_parts = [lax.all_gather(misc_shard, AXES, axis=0, tiled=True)[None]]
    w_parts, pick, routes = (lambda v: (v[:-2], *v[-2:]))(together([*w_parts, pick, routes]))
    dy_rows = swap(after(dy_send, *w_parts, misc_z) if small else dy_send, "dp")

    heads, w_heads = qkv_project(
        seq, scalar(lax.axis_index("dp")), token_blocks, w_parts, cosine, sine
    )
    if small:
        heads = after(heads, misc_z)
        misc_parts.append(flip(jnp.concatenate(misc_parts), "x"))
        shards = z_gather(after(paired_shards(shared_in, shared_out), w_heads))
    ctx_heads, log_totals = attend(seq, heads, segments)
    ctxs = seq_send_twice(ctx_heads)
    hidden, hn, gates, w_attn, misc, ctx, *sends = middle(
        me, seq, ctxs, layer_input, misc_parts, pick, routes, experts, parts
    )

    sends[0] = after(sends[0], dy_rows, shards) if small else sends[0]

    row_parts = [
        swap(send.reshape(experts, part, width), "dp").reshape(-1, width)
        for part, send in zip(parts, sends, strict=True)
    ]
    if small:
        shards = after(shards, hn)
        a0, b0 = shards[:, 0], shards[:, 1]
        a1, b1 = flip(a0, "y"), flip(b0, "x")
        a2, b2 = flip(jnp.concatenate([a0, a1]), "x"), flip(jnp.concatenate([b0, b1]), "y")
        hn_pair = jnp.concatenate([hn, flip(hn, "c")], axis=0)
        dy_pair = jnp.concatenate([cotangent, flip(cotangent, "c")], axis=0)
        row_parts[0] = after(row_parts[0], a1, b1, hn_pair, dy_pair)
    else:
        w_gate = lax.all_gather(shared_in[:, :units], AXES, axis=0, tiled=True)
        w_up = lax.all_gather(shared_in[:, units:], AXES, axis=0, tiled=True)
        w_out = lax.all_gather(shared_out, AXES, axis=0, tiled=True)

    own = scalar(lax.axis_index("dp"))
    sets, eos, dxes, dgates, low = [], [], [], [], 0
    for k, (part, rows, other) in enumerate(zip(parts, row_parts, others, strict=True)):
        if k == 1:
            hn_pair = after(hn_pair, dxes[0])
            shared, dhn, share, *grads = paired(me, hn_pair, dy_pair, (a0, a1, a2), (b0, b1, b2))
            rows = after(rows, dhn)
        eo, dxe, dgate, deo, act, d_gate, d_up = expert(
            own, rows, dy_rows if small else dy_rows.reshape(-1, width), low, other, misc, expert_in,
            expert_out, dgates[0] if k == 1 else None,
        )
        low += part
        sets.append((rows, deo, act, d_gate, d_up))
        eos.append(eo.reshape(experts, part, width))
        dxes.append(dxe.reshape(experts, -1, width))
        dgates.append(dgate)
    backs = []
    for k, dxe in enumerate(dxes):
        back = swap(after(dxe, *backs), "dp")
        backs.append(back if k else back.reshape(-1, width))
    if not small:
        backs.append(swap(dgates[0].reshape(experts, capacity), "dp").reshape(1, slots))
    held = backs[:1]
    if small:
        share = flip(share, "c")
        ka, wa, kb, wb = grads
        ca, cb = flip(wa, "x"), flip(wb, "y")
        held += [share, ca, cb]
    else:
        shared, dhn, grad_gate, grad_up, grad_out = dense(hn, cotangent, w_gate, w_up, w_out)
        share = jnp.zeros((2 * tokens, width), BF16)
    sets = [(after(one[0], *held),) + one[1:] for one in sets]
    in_kept, in_away, out_kept, out_away = expert_grads(seq, sets)
    if small:
        ca, cb = together((ca, cb), in_kept)
        wa, wb = add_up([ka[4:], ca[4:]]).astype(BF16), add_up([kb[4:], cb[4:]]).astype(BF16)
        ea, eb = flip(wa, "y"), flip(wb, "x")
        in_away, out_away = flip(in_away, "c"), flip(out_away, "c")
        backs = [after(back, in_kept) for back in backs]
    dh, dctx, grad_attn = middle_back(
        dhn, share, backs, slot_of, routes, gates, misc, hidden, hn, cotangent, ctx, w_attn,
        seq, seq_devs, experts, parts,
    )

    dctxs = seq_send_twice(dctx)
    in_terms, in_far = copies_sum(in_kept, in_away)
    out_terms, out_far = copies_sum(out_kept, out_away)
    if small:
        dctxs[0] = after(dctxs[0], in_far, out_far)
    came = swap(after(jnp.concatenate(eos, axis=1), backs[-1]), "dp").reshape(-1, width)
    d_heads = []
    for head in range(columns // 192):
        held = after(heads, *d_heads) if d_heads else heads
        if small and head == 1:
            grad_attn = after(grad_attn, d_heads[0])
            part = half_sum(grad_attn.reshape(8, 2, 2, -1, width + LANES), "c", 2).astype(BF16)
            held = after(held, grad_attn)
        if small and head == 2:
            part = after(part, d_heads[1])
            part_kept = lax.dynamic_index_in_dim(part, here["x"], 1, False)
            part_came = flip(lax.dynamic_index_in_dim(part, 1 - here["x"], 1, False), "x")
        d_heads.append(attend_back(seq, held, dctxs, ctx_heads, log_totals, segments, head))
    if small:
        ea, eb = together((ea, eb), d_heads[0])
        wa, wb = add_up([ka[:4], ca[:4], ea]).astype(BF16), add_up([kb[:4], cb[:4], eb]).astype(BF16)
        sums = z_sum(after(jnp.stack([wa, wb], axis=1), came))
        d_heads[0] = after(d_heads[0], sums)
    dxn_kept, dxn_away, grad_heads = qkv_back(seq, token_blocks, d_heads, w_heads, cosine, sine)
    if small:
        dxn_away = after(flip(dxn_away, "c"), in_terms[2], out_terms[2])
    dxn_terms, dxn_far = copies_sum(dxn_kept, dxn_away)
    input_grad = input_back(layer_input, dh, w_heads, dxn_terms)
    layer_output = output_of(
        hidden, shared, share, [after(came, dxn_far)], expert_slot, gates
    )

    grad_heads = grad_heads.reshape(experts * seq_devs, -1, columns + 64)
    grad_heads = swap(grad_heads, AXES)
    grad_heads = grad_heads.reshape((experts, seq_devs) + grad_heads.shape[1:])
    if small:
        sum_in, sum_out = paired_grads(*together((sums[0], sums[1]), dxn_far))
        part = add_up([part_kept, after(part_came, dxn_far)]).astype(BF16)
        sum_attn = jnp.sum(swap(after(part, grad_heads), "dp").astype(F32), axis=0)
        in_terms, out_terms = together((*in_terms, *out_terms), dxn_far), ()
        in_terms, out_terms = in_terms[:3], in_terms[3:]
    else:
        total = functools.partial(lax.psum_scatter, scatter_dimension=0, tiled=True)
        sum_attn = total(grad_attn, AXES).astype(F32)
        sum_out = total(grad_out, AXES).astype(F32)
        sum_in = jnp.concatenate([total(grad_gate, AXES), total(grad_up, AXES)], axis=1).astype(F32)
    sum_heads = jnp.sum(grad_heads.astype(F32), axis=0)
    return (
        layer_output,
        input_grad,
        jnp.sum(sum_heads[:, :, columns], axis=0),
        sum_heads[:, :, :columns].transpose(1, 0, 2).reshape(-1, seq_devs * columns),
        sum_attn[:, :width],
        sum_attn[:, width + experts],
        sum_attn[:, width : width + experts],
        sum_in,
        sum_out,
        add_up(in_terms)[None],
        add_up(out_terms)[None],
    )


def solution(mesh):
    rows = P(AXES, None)
    return jax.shard_map(
        on_device,
        mesh=mesh,
        in_specs=(
            rows, rows, P("dp", None), rows, P(AXES), P(AXES), rows, rows,
            P(AXES), rows, rows, rows, P("dp", None, None), P("dp", None, None),
        ),
        out_specs=(
            rows, rows, P(AXES), rows, rows, P(AXES), rows, rows, rows,
            P("dp", None, "seq"), P("dp", "seq", None),
        ),
        check_vma=False,
    )
```

time: 644 us -> 489 us (0.76)
  waiting for transfers between devices: 205 us -> 89.1 us
  starting transfers between devices: 139 us -> 101 us
  Pallas kernels: 166 us -> 192 us
  other arithmetic: 63.1 us -> 41.8 us
  blocking collectives: 9.66 us -> 0 us
  local copies, waits for them, and re-layouts: 46.6 us -> 54 us
    ppermute x70 -> x37, waiting for transfers between devices: 158 us -> 71 us  [flip(): return lax.ppermute(block, AXES, FLIP[name])]
    ppermute x70 -> x37, starting transfers between devices: 101 us -> 37 us  [flip(): return lax.ppermute(block, AXES, FLIP[name])]
    all_to_all x9 -> x10, waiting for transfers between devices: 47.1 us -> 18 us  [swap(): return lax.all_to_all(blocks, axis, split_axis=0, concat_axis=0, tiled=True)]
    pallas_call x10 -> x14, Pallas kernels: 166 us -> 192 us  [the longest x2 38.6 us: expert(): pl.pallas_call(functools.partial(expert_kernel, low=low), grid_spec=pltpu...]
    select_n x27 -> x3, other arithmetic: 24 us -> 1.16 us  [the longest x2 1.03 us: ordered(): jnp.where(mine == 0, jnp.stack([own, came], axis), jnp.stack([came, own],...]
    all_to_all x9 -> x10, starting transfers between devices: 37.5 us -> 59.2 us  [swap(): return lax.all_to_all(blocks, axis, split_axis=0, concat_axis=0, tiled=True)]
    all_to_all x1 -> x0, blocking collectives: 9.66 us -> none  [swap(): return lax.all_to_all(blocks, axis, split_axis=0, concat_axis=0, tiled=True)]
    dynamic_slice x10 -> x2, local copies, waits for them, and re-layouts: 11.1 us -> 2.02 us  [the longest x1 1.04 us: half_sum(): kept = lax.dynamic_index_in_dim(part, me, axis, False)]
  transfers between devices with their start and end apart: 79 -> 48, of which waited for: 30 -> 13; matrix products, arithmetic and copies ran while one was open for 15% -> 19% of each run, Pallas kernels for 22% -> 40%
where the time goes in v2:
time: 489 us; the launch traced here: 482 us
  Pallas kernels  192 us (39%)
  starting transfers between devices  101 us (21%)
  waiting for transfers between devices  89.1 us (18%)
  local copies, waits for them, and re-layouts  54 us (11%)
  other arithmetic  41.8 us (9%)
    ppermute x37, waiting for transfers between devices, flip(): return lax.ppermute(block, AXES, FLIP[name])  71 us
    all_to_all x10, starting transfers between devices, swap(): return lax.all_to_all(blocks, axis, split_axis=0, concat_axis=0, tiled=True)  59.2 us
    pallas_call x2, Pallas kernels, expert(): pl.pallas_call(functools.partial(expert_kernel, low=low), grid_spec=pltpu...  38.6 us
    pallas_call x3, Pallas kernels, attend_back(): pl.pallas_call(attend_back_kernel, grid_spec=pltpu.PrefetchScalarGridSpec...  37.8 us
    ppermute x37, starting transfers between devices, flip(): return lax.ppermute(block, AXES, FLIP[name])  37 us
    pallas_call x1, Pallas kernels, paired(): pl.pallas_call(paired_kernel, grid_spec=pltpu.PrefetchScalarGridSpec(num_...  25 us
    pallas_call x1, Pallas kernels, expert_grads(): pl.pallas_call(expert_grads_kernel, grid_spec=pltpu.PrefetchScalarGridSpe...  21.4 us
    all_to_all x10, waiting for transfers between devices, swap(): return lax.all_to_all(blocks, axis, split_axis=0, concat_axis=0, tiled=True)  18 us
  transfers between devices with their start and end apart: 48, of which 13 were waited for; matrix products, arithmetic and copies ran while one was open for 19% of the time, Pallas kernels for 40%

profile of v2, /device:TPU:0, one launch (start us, length us, event | category | flops | bytes accessed | tf_op | source)
XLA Modules:
  0.0 482.0 jit_solution(6401351901623872192)
XLA Ops:
  3.8 3.9 all-to-all-start
  16.0 6.3 %all-to-all-start.1 = ((bf16[8,96,640]{2,1,0:T(8,128)(2,1)}), bf16[8,96,640]{2,1,0:T(8,128)(2,1)S(1)}, u32[]{:S(2)}, u32[]{:S(2)}) async-start(bf16[8,96,640]{2,1,0:T(8,128)(2,1)} %maximum_maximum_fusion), calls=%async_computation.1 | async-start | bytes 1966080 | tf_op jit(solution)/shard_map/all_to_all | solution.py:139
  24.2 2.4 convolution_convert_fusion
  26.6 1.7 collective-permute-start.1
  28.3 1.6 fusion.3.refs_8_
  30.0 16.8 %all-to-all-done.1 = bf16[8,96,640]{2,1,0:T(8,128)(2,1)S(1)} async-done(((bf16[8,96,640]{2,1,0:T(8,128)(2,1)}), bf16[8,96,640]{2,1,0:T(8,128)(2,1)S(1)}, u32[]{:S(2)}, u32[]{:S(2)}) %all-to-all-start.1) | async-done | bytes 983072 | tf_op jit(solution)/shard_map/all_to_all | solution.py:139
  48.2 3.0 collective-permute-start.4
  51.3 2.4 collective-permute-done.6
  53.7 2.4 collective-permute-done.5
  56.7 4.5 all-to-all-start.2
  61.3 1.8 multiply_sine_fusion
  65.2 8.5 %qkv_project.1 = (bf16[4,576,512]{2,1,0:T(8,128)(2,1)}, bf16[768,640]{1,0:T(8,128)(2,1)}) custom-call(s32[1]{0:T(128)} %bitcast.1.seq_ref, s32[1]{0:T(128)} %bitcast.2.dp_ref.own_ref, bf16[512,768]{1,0:T(8,128)(2,1)} %x_ref.1, bf16[512,768]{1,0:T(8,128)(2,1)} %collective-permute-done.refs_1_, bf16[512,768]{1,0:T(8,128)(2,1)} %collective-permute-done.1.refs_2_, ...), custom_call_target="tpu_custom_call" | custom-call | flops 1000000000 | bytes 1048576 | tf_op jit(solution)/shard_map/qkv_project/pallas_call | solution.py:203
  73.6 3.8 collective-permute-start.15
  78.7 17.6 %attend.1 = (bf16[4,192,512]{2,1,0:T(8,128)(2,1)}, f32[3,1,2048]{2,1,0:T(1,128)}) custom-call(s32[1]{0:T(128)} %bitcast.1.seq_ref, bf16[4,576,512]{2,1,0:T(8,128)(2,1)} %get-tuple-element.165.buf_ref, s32[1,2048]{1,0:T(1,128)} %docs_ref.7), custom_call_target="tpu_custom_call" | custom-call | flops 3000000000 | bytes 1048576 | tf_op jit(solution)/shard_map/attend/pallas_call | solution.py:286
  97.3 2.1 collective-permute-start.7
  99.4 2.0 collective-permute-start.9
  104.2 6.6 %collective-permute-done.9.refs_5_ = bf16[4,48,896]{2,1,0:T(8,128)(2,1)S(1)} collective-permute-done((bf16[4,48,896]{2,1,0:T(8,128)(2,1)S(1)}, bf16[4,48,896]{2,1,0:T(8,128)(2,1)S(1)}, u32[]{:S(2)}, u32[]{:S(2)}) %collective-permute-start.9) | collective-permute-done | bytes 344096 | tf_op jit(solution)/shard_map/ppermute | solution.py:82
  114.0 13.9 %collective-permute-done.14 = bf16[2,288,256]{2,1,0:T(8,128)(2,1)S(1)} collective-permute-done((bf16[2,288,256]{2,1,0:T(8,128)(2,1)S(1)}, bf16[2,288,256]{2,1,0:T(8,128)(2,1)S(1)}, u32[]{:S(2)}, u32[]{:S(2)}) %collective-permute-start.14) | collective-permute-done | bytes 294944 | tf_op jit(solution)/shard_map/ppermute | solution.py:82
  129.9 1.8 fusion.37
  132.6 5.9 %middle.1 = (f32[512,768]{1,0:T(8,128)}, bf16[512,768]{1,0:T(8,128)(2,1)}, f32[512,128]{1,0:T(8,128)}, bf16[768,768]{1,0:T(8,128)(2,1)}, bf16[768,128]{1,0:T(8,1...) custom-call(s32[1]{0:T(128)} %bitcast.me_ref, s32[1]{0:T(128)} %bitcast.1.seq_ref, ...), custom_call_target="tpu_custom_call" | custom-call | flops 500000000 | bytes 1048576 | tf_op jit(solution)/shard_map/middle/pallas_call | solution.py:447
  138.5 4.1 all-to-all-start.3
  143.6 2.0 collective-permute-start.16
  145.8 2.0 collective-permute-start.17
  151.8 2.1 constant_dynamic-update-slice_fusion.6
  153.9 14.4 %collective-permute-done.16.refs_1_ = bf16[4,288,256]{2,1,0:T(8,128)(2,1)S(1)} collective-permute-done((bf16[4,288,256]{2,1,0:T(8,128)(2,1)}, bf16[4,288,256]{2,1,0:T(8,128)(2,1)S(1)}, u32[]{:S(2)}, u32[]{:S(2)}) %collective-permute-start.16) | collective-permute-done | bytes 589856 | tf_op jit(solution)/shard_map/ppermute | solution.py:82
  168.3 2.4 pad_maximum_fusion.2
  170.7 2.0 collective-permute-start.19
  172.7 4.5 all-to-all-start.4
  177.3 2.2 pad_maximum_fusion.3
  179.5 2.0 collective-permute-start.20
  181.5 2.1 constant_dynamic-update-slice_fusion.5.x_ref
  183.5 20.8 %expert.2 = (bf16[640,768]{1,0:T(8,128)(2,1)}, bf16[640,768]{1,0:T(8,128)(2,1)}, f32[640,1]{1,0:T(8,128)}, bf16[640,768]{1,0:T(8,128)(2,1)}, bf16[640,2048]{1,0:...) custom-call(s32[1]{0:T(128)} %bitcast.2.dp_ref.own_ref, bf16[640,768]{1,0:T(8,128)(2,1)} %bitcast.138, ...), custom_call_target="tpu_custom_call" | custom-call | flops 12079595520 | bytes 41943040 | tf_op jit(solution)/shard_map/expert/pallas_call | solution.py:697
  204.3 4.6 all-to-all-start.5
  208.9 8.9 %collective-permute-done.20.refs_5_ = bf16[8,288,256]{2,1,0:T(8,128)(2,1)} collective-permute-done((bf16[8,288,256]{2,1,0:T(8,128)(2,1)}, bf16[8,288,256]{2,1,0:T(8,128)(2,1)}, u32[]{:S(2)}, u32[]{:S(2)}) %collective-permute-start.20) | collective-permute-done | bytes 1179680 | tf_op jit(solution)/shard_map/ppermute | solution.py:82
  217.8 25.0 %dense_pair.1 = (f32[512,768]{1,0:T(8,128)}, f32[512,768]{1,0:T(8,128)}, bf16[1024,768]{1,0:T(8,128)(2,1)}, bf16[8,288,256]{2,1,0:T(8,128)(2,1)}, bf16[8,288,256...) custom-call(s32[1]{0:T(128)} %bitcast.me_ref, ...), custom_call_target="tpu_custom_call" | custom-call | flops 14495514624 | bytes 31457280 | tf_op jit(solution)/shard_map/dense_pair/pallas_call | solution.py:591
  244.7 17.9 %expert.3 = (bf16[512,768]{1,0:T(8,128)(2,1)}, bf16[8,80,768]{2,1,0:T(8,128)(2,1)}, f32[512,1]{1,0:T(8,128)}, bf16[512,768]{1,0:T(8,128)(2,1)}, bf16[512,2048]{1...) custom-call(s32[1]{0:T(128)} %bitcast.2.dp_ref.own_ref, bf16[512,768]{1,0:T(8,128)(2,1)} %bitcast.141, ...), custom_call_target="tpu_custom_call" | custom-call | flops 9663676416 | bytes 41943040 | tf_op jit(solution)/shard_map/expert/pallas_call | solution.py:697
  262.6 5.9 %all-to-all-start.6 = ((bf16[8,80,768]{2,1,0:T(8,128)(2,1)}), bf16[8,80,768]{2,1,0:T(8,128)(2,1)}, u32[]{:S(2)}, u32[]{:S(2)}) async-start(bf16[8,80,768]{2,1,0:T(8,128)(2,1)} %get-tuple-element.128), calls=%async_computation.6 | async-start | bytes 1966080 | tf_op jit(solution)/shard_map/all_to_all | solution.py:139
  268.5 3.0 collective-permute-done.22
  271.8 21.4 %expert_grads.1 = (bf16[2,768,1024]{2,1,0:T(8,128)(2,1)}, bf16[2,768,1024]{2,1,0:T(8,128)(2,1)}, bf16[2,512,768]{2,1,0:T(8,128)(2,1)}, bf16[2,512,768]{2,1,0:T(8,128)(2,1)}) custom-call(s32[1]{0:T(128)} %bitcast.1.seq_ref, bf16[640,768]{1,0:T(8,128)(2,1)} %bitcast.139, bf16[640,768]{1,0:T(8,128)(2,1)} %get-tuple-element.132.refs_1_, ...), custom_call_target="tpu_custom_call" | custom-call | flops 3623878656 | bytes 4194304 | tf_op jit(solution)/shard_map/expert_grads/pallas_call | solution.py:803
  295.2 11.8 %all-to-all-start.7 = ((bf16[8,144,768]{2,1,0:T(8,128)(2,1)}), bf16[8,144,768]{2,1,0:T(8,128)(2,1)S(1)}, u32[]{:S(2)}, u32[]{:S(2)}) async-start(bf16[8,144,768]{2,1,0:T(8,128)(2,1)} %pad_maximum_fusion), calls=%async_computation.7 | async-start | bytes 3538944 | tf_op jit(solution)/shard_map/all_to_all | solution.py:139
  307.1 13.7 %middle_back.1 = (f32[512,768]{1,0:T(8,128)}, bf16[4,192,512]{2,1,0:T(8,128)(2,1)}, bf16[768,896]{1,0:T(8,128)(2,1)}) custom-call(f32[512,768]{1,0:T(8,128)} %get-tuple-element.123.dhn_ref, bf16[1024,768]{1,0:T(8,128)(2,1)} %copy-done.2, s32[512,2]{1,0:T(8,128)} %copy-done.5, s32[512,2]{1,0:T(8,128)} %copy.225.refs_9_.routes_ref, ...), custom_call_target="tpu_custom_call" | custom-call | flops 3000000000 | bytes 16777216 | tf_op jit(solution)/shard_map/middle_back/pallas_call | solution.py:896
  321.8 1.9 collective-permute-start.26
  325.0 2.1 collective-permute-start.28
  328.0 4.7 collective-permute-done.26
  334.8 1.8 collective-permute-start.29
  339.5 3.2 fusion.4
  342.7 12.8 %attend_back.3.refs_4_ = bf16[4,192,512]{2,1,0:T(8,128)(2,1)} custom-call(s32[1]{0:T(128)} %bitcast.1.seq_ref, bf16[4,576,512]{2,1,0:T(8,128)(2,1)} %get-tuple-element.165.buf_ref, bf16[4,192,512]{2,1,0:T(8,128)(2,1)} %get-tuple-element.151.d0_ref, bf16[1,192,512]{2,1,0:T(8,128)(2,1)} %get-tuple-element.286.d1_ref, ...), custom_call_target="tpu_custom_call" | custom-call | flops 4000000000 | bytes 1048576 | tf_op jit(solution)/shard_map/attend_back/pallas_call | solution.py:364
  360.0 4.8 all-to-all-start.8
  366.7 12.5 %attend_back.4.refs_5_ = bf16[4,192,512]{2,1,0:T(8,128)(2,1)} custom-call(s32[1]{0:T(128)} %bitcast.1.seq_ref, bf16[4,576,512]{2,1,0:T(8,128)(2,1)} %get-tuple-element.165.buf_ref, bf16[4,192,512]{2,1,0:T(8,128)(2,1)} %get-tuple-element.151.d0_ref, bf16[1,192,512]{2,1,0:T(8,128)(2,1)} %get-tuple-element.286.d1_ref, ...), custom_call_target="tpu_custom_call" | custom-call | flops 4000000000 | bytes 1048576 | tf_op jit(solution)/shard_map/attend_back/pallas_call | solution.py:364
  381.2 12.6 %attend_back.5.refs_6_ = bf16[4,192,512]{2,1,0:T(8,128)(2,1)} custom-call(s32[1]{0:T(128)} %bitcast.1.seq_ref, bf16[4,576,512]{2,1,0:T(8,128)(2,1)} %get-tuple-element.165.buf_ref, bf16[4,192,512]{2,1,0:T(8,128)(2,1)} %get-tuple-element.151.d0_ref, bf16[1,192,512]{2,1,0:T(8,128)(2,1)} %get-tuple-element.286.d1_ref, ...), custom_call_target="tpu_custom_call" | custom-call | flops 4000000000 | bytes 1048576 | tf_op jit(solution)/shard_map/attend_back/pallas_call | solution.py:364
  393.9 12.2 %qkv_back.1 = (bf16[2,512,768]{2,1,0:T(8,128)(2,1)}, bf16[2,512,768]{2,1,0:T(8,128)(2,1)}, bf16[768,640]{1,0:T(8,128)(2,1)}) custom-call(s32[1]{0:T(128)} %bitcast.1.seq_ref, bf16[512,768]{1,0:T(8,128)(2,1)} %x_ref.1, bf16[512,768]{1,0:T(8,128)(2,1)} %collective-permute-done.refs_1_, bf16[512,768]{1,0:T(8,128)(2,1)} %collective-permute-done.1.refs_2_, ...), custom_call_target="tpu_custom_call" | custom-call | flops 12000000000 | bytes 12582912 | tf_op jit(solution)/shard_map/qkv_back/pallas_call | solution.py:1005
  407.6 1.7 collective-permute-start.32
  416.2 6.6 %all-to-all-start.9 = ((bf16[32,24,640]{2,1,0:T(8,128)(2,1)}), bf16[32,24,640]{2,1,0:T(8,128)(2,1)}, u32[]{:S(2)}, u32[]{:S(2)}) async-start(bf16[32,24,640]{2,1,0:T(8,128)(2,1)} %bitcast.147), calls=%async_computation.9 | async-start | bytes 1966080 | tf_op jit(solution)/shard_map/all_to_all | solution.py:139
  422.7 8.4 %collective-permute-done.32 = bf16[512,768]{1,0:T(8,128)(2,1)} collective-permute-done((bf16[512,768]{1,0:T(8,128)(2,1)}, bf16[512,768]{1,0:T(8,128)(2,1)}, u32[]{:S(2)}, u32[]{:S(2)}) %collective-permute-start.32) | collective-permute-done | bytes 786464 | tf_op jit(solution)/shard_map/ppermute | solution.py:82
  431.2 2.5 fusion.11
  433.6 2.6 collective-permute-start.33
  436.3 6.0 %collective-permute-done.35 = bf16[8,24,896]{2,1,0:T(8,128)(2,1)} collective-permute-done((bf16[8,24,896]{2,1,0:T(8,128)(2,1)}, bf16[8,24,896]{2,1,0:T(8,128)(2,1)}, u32[]{:S(2)}, u32[]{:S(2)}) %collective-permute-start.35) | collective-permute-done | bytes 344096 | tf_op jit(solution)/shard_map/ppermute | solution.py:82
  442.4 1.9 fusion.13
  444.3 2.1 slice_bitcast_fusion.4.refs_1_
  446.4 2.6 add_bitcast_fusion.1
  449.0 4.1 add_bitcast_fusion
  454.2 6.3 %output_of.1 = f32[512,768]{1,0:T(8,128)} custom-call(f32[512,768]{1,0:T(8,128)} %get-tuple-element.106.hidden_ref, f32[512,768]{1,0:T(8,128)} %get-tuple-element.118.dense_ref, bf16[1024,768]{1,0:T(8,128)(2,1)} %copy-done.2, s32[512,2]{1,0:T(8,128)} %copy-done.4, f32[512,128]{1,0:T(8,128)} %get-tuple-element.120.gates_ref, bf16[1152,768]{1,0:T(8,128)(2,1)} %bitcast.134), custom_call_target="tpu_custom_call" | custom-call | flops 2000000000 | bytes 8388608 | tf_op jit(solution)/shard_map/output_of/pallas_call | solution.py:930
  461.6 7.0 %all-to-all-start.10 = ((bf16[8,24,896]{2,1,0:T(8,128)(2,1)}), bf16[8,24,896]{2,1,0:T(8,128)(2,1)S(1)}, u32[]{:S(2)}, u32[]{:S(2)}) async-start(bf16[8,24,896]{2,1,0:T(8,128)(2,1)} %fusion.13), calls=%async_computation.10 | async-start | bytes 688128 | tf_op jit(solution)/shard_map/all_to_all | solution.py:139
  473.9 4.6 input_back.1
  (264 shorter events, 73.6 us)
Async XLA Ops:
  0.7 63.6 %collective-permute-start = (bf16[512,768]{1,0:T(8,128)(2,1)}, bf16[512,768]{1,0:T(8,128)(2,1)}, u32[]{:S(2)}, u32[]{:S(2)}) collective-permute-start(bf16[512,768]{1,0:T(8,128)(2,1)} %x_ref.1), channel_id=1, source_target_pairs={{0,1},{1,0},{2,3},{3,2},{4,5},{5,4},{6,7},{7,6},{8,9},{9,8},{10,11... | collective-permute-start | bytes 2359304 | tf_op jit(solution)/shard_map/ppermute | solution.py:82
  3.8 10.8 %all-to-all-start = ((bf16[4,24,640]{2,1,0:T(8,128)(2,1)}), bf16[4,24,640]{2,1,0:T(8,128)(2,1)S(1)}, u32[]{:S(2)}, u32[]{:S(2)}) async-start(bf16[4,24,640]{2,1,0:T(8,128)(2,1)} %copy.215), calls=%async_computation | async-start | bytes 245760 | tf_op jit(solution)/shard_map/all_to_all | solution.py:139
  9.3 20.7 %collective-permute-start.3 = (bf16[24,896]{1,0:T(8,128)(2,1)S(1)}, bf16[24,896]{1,0:T(8,128)(2,1)S(1)}, u32[]{:S(2)}, u32[]{:S(2)}) collective-permute-start(bf16[24,896]{1,0:T(8,128)(2,1)S(1)} %get-tuple-element.300), channel_id=1, source_target_pairs={{0,1},{1,0},{2,3},{3,2},{4,5},{5,4},{6,7},{7,6},{8,9},{9,8},{10,11... | collective-permute-start | bytes 129032 | tf_op jit(solution)/shard_map/ppermute | solution.py:82
  12.7 11.2 %copy-start.5 = (s32[512,2]{1,0:T(8,128)}, s32[512,2]{1,0:T(8,128)S(1)}, u32[]{:S(2)}) copy-start(s32[512,2]{1,0:T(8,128)S(1)} %get-tuple-element.293.slots_ref) | copy-start | bytes 12292
  16.0 30.8 %all-to-all-start.1 = ((bf16[8,96,640]{2,1,0:T(8,128)(2,1)}), bf16[8,96,640]{2,1,0:T(8,128)(2,1)S(1)}, u32[]{:S(2)}, u32[]{:S(2)}) async-start(bf16[8,96,640]{2,1,0:T(8,128)(2,1)} %maximum_maximum_fusion), calls=%async_computation.1 | async-start | bytes 1966080 | tf_op jit(solution)/shard_map/all_to_all | solution.py:139
  26.6 24.6 %collective-permute-start.1 = (bf16[512,768]{1,0:T(8,128)(2,1)S(1)}, bf16[512,768]{1,0:T(8,128)(2,1)}, u32[]{:S(2)}, u32[]{:S(2)}) collective-permute-start(bf16[512,768]{1,0:T(8,128)(2,1)S(1)} %copy-done.1), channel_id=1, source_target_pairs={{0,2},{1,3},{2,0},{3,1},{4,6},{5,7},{6,4},{7,5},{8,10},{9,11},{10,... | collective-permute-start | bytes 2359304 | tf_op jit(solution)/shard_map/ppermute | solution.py:82
  46.8 6.9 %collective-permute-start.6 = (bf16[48,896]{1,0:T(8,128)(2,1)S(1)}, bf16[48,896]{1,0:T(8,128)(2,1)S(1)}, u32[]{:S(2)}, u32[]{:S(2)}) collective-permute-start(bf16[48,896]{1,0:T(8,128)(2,1)S(1)} %bitcast.157), channel_id=1, source_target_pairs={{0,24},{1,25},{2,26},{3,27},{4,28},{5,29},{6,30},{7,31},{8,16},{9,... | collective-permute-start | bytes 258056 | tf_op jit(solution)/shard_map/ppermute | solution.py:82
  48.2 7.9 %collective-permute-start.5 = (bf16[48,896]{1,0:T(8,128)(2,1)S(1)}, bf16[48,896]{1,0:T(8,128)(2,1)S(1)}, u32[]{:S(2)}, u32[]{:S(2)}) collective-permute-start(bf16[48,896]{1,0:T(8,128)(2,1)S(1)} %bitcast.158), channel_id=1, source_target_pairs={{0,16},{1,17},{2,18},{3,19},{4,20},{5,21},{6,22},{7,23},{8,24},{9,... | collective-permute-start | bytes 258056 | tf_op jit(solution)/shard_map/ppermute | solution.py:82
  48.2 7.9 %collective-permute-start.4 = (bf16[48,896]{1,0:T(8,128)(2,1)S(1)}, bf16[48,896]{1,0:T(8,128)(2,1)S(1)}, u32[]{:S(2)}, u32[]{:S(2)}) collective-permute-start(bf16[48,896]{1,0:T(8,128)(2,1)S(1)} %bitcast.159), channel_id=1, source_target_pairs={{0,8},{1,9},{2,10},{3,11},{4,12},{5,13},{6,14},{7,15},{8,0},{9,1},... | collective-permute-start | bytes 258056 | tf_op jit(solution)/shard_map/ppermute | solution.py:82
  51.2 11.9 %collective-permute-start.12 = (bf16[2,4,24,256]{3,2,1,0:T(8,128)(2,1)}, bf16[2,4,24,256]{3,2,1,0:T(8,128)(2,1)}, u32[]{:S(2)}, u32[]{:S(2)}) collective-permute-start(bf16[2,4,24,256]{3,2,1,0:T(8,128)(2,1)} %get-tuple-element.296), channel_id=1, source_target_pairs={{0,1},{1,0},{2,3},{3,2},{4,5},{5,4},{6,7},{7,6},{8,9},{9,8},{10,11... | collective-permute-start | bytes 294920 | tf_op jit(solution)/shard_map/ppermute | solution.py:82
  53.7 10.5 %collective-permute-start.2 = (bf16[512,768]{1,0:T(8,128)(2,1)}, bf16[512,768]{1,0:T(8,128)(2,1)S(1)}, u32[]{:S(2)}, u32[]{:S(2)}) collective-permute-start(bf16[512,768]{1,0:T(8,128)(2,1)} %collective-permute-done.1.refs_2_), channel_id=1, source_target_pairs={{0,1},{1,0},{2,3},{3,2},{4,5},{5,4},{6,7},{7,6},{8,9},{9,8},{10,11... | collective-permute-start | bytes 2359304 | tf_op jit(solution)/shard_map/ppermute | solution.py:82
  56.2 43.2 %copy-start.23 = (bf16[4,48,896]{2,1,0:T(8,128)(2,1)}, bf16[4,48,896]{2,1,0:T(8,128)(2,1)S(1)}, u32[]{:S(2)}) copy-start(bf16[4,48,896]{2,1,0:T(8,128)(2,1)S(1)} %pad_maximum_fusion.7.refs_4_) | copy-start | bytes 1032196
  56.7 81.7 %all-to-all-start.2 = ((bf16[8,144,768]{2,1,0:T(8,128)(2,1)}), bf16[8,144,768]{2,1,0:T(8,128)(2,1)}, u32[]{:S(2)}, u32[]{:S(2)}) async-start(bf16[8,144,768]{2,1,0:T(8,128)(2,1)} %bitcast.143), calls=%async_computation.2 | async-start | bytes 3538944 | tf_op jit(solution)/shard_map/all_to_all | solution.py:139
  73.6 40.4 %collective-permute-start.15 = (bf16[2,288,256]{2,1,0:T(8,128)(2,1)S(1)}, bf16[2,288,256]{2,1,0:T(8,128)(2,1)S(1)}, u32[]{:S(2)}, u32[]{:S(2)}) collective-permute-start(bf16[2,288,256]{2,1,0:T(8,128)(2,1)S(1)} %pad_maximum_fusion.8), channel_id=1, source_target_pairs={{0,24},{1,25},{2,26},{3,27},{4,28},{5,29},{6,30},{7,31},{8,16},{9,... | collective-permute-start | bytes 884744 | tf_op jit(solution)/shard_map/ppermute | solution.py:82
  77.5 50.4 %collective-permute-start.14 = (bf16[2,288,256]{2,1,0:T(8,128)(2,1)S(1)}, bf16[2,288,256]{2,1,0:T(8,128)(2,1)S(1)}, u32[]{:S(2)}, u32[]{:S(2)}) collective-permute-start(bf16[2,288,256]{2,1,0:T(8,128)(2,1)S(1)} %pad_maximum_fusion.8), channel_id=1, source_target_pairs={{0,16},{1,17},{2,18},{3,19},{4,20},{5,21},{6,22},{7,23},{8,24},{9,... | collective-permute-start | bytes 884744 | tf_op jit(solution)/shard_map/ppermute | solution.py:82
  77.5 50.4 %collective-permute-start.13 = (bf16[2,288,256]{2,1,0:T(8,128)(2,1)S(1)}, bf16[2,288,256]{2,1,0:T(8,128)(2,1)}, u32[]{:S(2)}, u32[]{:S(2)}) collective-permute-start(bf16[2,288,256]{2,1,0:T(8,128)(2,1)S(1)} %pad_maximum_fusion.8), channel_id=1, source_target_pairs={{0,8},{1,9},{2,10},{3,11},{4,12},{5,13},{6,14},{7,15},{8,0},{9,1},... | collective-permute-start | bytes 884744 | tf_op jit(solution)/shard_map/ppermute | solution.py:82
  78.7 22.6 %copy-start.35 = (bf16[48,896]{1,0:T(8,128)(2,1)S(1)}, bf16[48,896]{1,0:T(8,128)(2,1)}, u32[]{:S(2)}) copy-start(bf16[48,896]{1,0:T(8,128)(2,1)} %copy-done.34) | copy-start | bytes 258052
  97.3 14.3 %collective-permute-start.7 = (bf16[2,192,512]{2,1,0:T(8,128)(2,1)S(1)}, bf16[2,192,512]{2,1,0:T(8,128)(2,1)S(1)}, u32[]{:S(2)}, u32[]{:S(2)}) collective-permute-start(bf16[2,192,512]{2,1,0:T(8,128)(2,1)S(1)} %slice.200), channel_id=1, source_target_pairs={{0,2},{1,3},{2,0},{3,1},{4,6},{5,7},{6,4},{7,5},{8,10},{9,11},{10,... | collective-permute-start | bytes 1179656 | tf_op jit(solution)/shard_map/ppermute | solution.py:82
  99.4 11.5 %collective-permute-start.9 = (bf16[4,48,896]{2,1,0:T(8,128)(2,1)S(1)}, bf16[4,48,896]{2,1,0:T(8,128)(2,1)S(1)}, u32[]{:S(2)}, u32[]{:S(2)}) collective-permute-start(bf16[4,48,896]{2,1,0:T(8,128)(2,1)S(1)} %pad_maximum_fusion.7.refs_4_), channel_id=1, source_target_pairs={{0,4},{1,5},{2,6},{3,7},{4,0},{5,1},{6,2},{7,3},{8,12},{9,13},{10,... | collective-permute-start | bytes 1032200 | tf_op jit(solution)/shard_map/ppermute | solution.py:82
  102.0 11.2 %copy-start.40 = (s32[512,2]{0,1:T(2,128)S(1)}, s32[512,2]{0,1:T(2,128)}, u32[]{:S(2)}) copy-start(s32[512,2]{0,1:T(2,128)} %param.17) | copy-start | bytes 12292
  110.9 19.1 %copy-start.24 = (bf16[4,48,896]{2,1,0:T(8,128)(2,1)}, bf16[4,48,896]{2,1,0:T(8,128)(2,1)S(1)}, u32[]{:S(2)}) copy-start(bf16[4,48,896]{2,1,0:T(8,128)(2,1)S(1)} %collective-permute-done.9.refs_5_) | copy-start | bytes 1032196
  111.7 20.1 %collective-permute-start.10 = (bf16[8,48,896]{2,1,0:T(8,128)(2,1)}, bf16[8,48,896]{2,1,0:T(8,128)(2,1)S(1)}, u32[]{:S(2)}, u32[]{:S(2)}) collective-permute-start(bf16[8,48,896]{2,1,0:T(8,128)(2,1)} %constant_dynamic-update-slice_fusion), channel_id=1, source_target_pairs={{0,2},{1,3},{2,0},{3,1},{4,6},{5,7},{6,4},{7,5},{8,10},{9,11},{10,... | collective-permute-start | bytes 2064392 | tf_op jit(solution)/shard_map/ppermute | solution.py:82
  113.2 16.8 %collective-permute-start.8 = (bf16[2,192,512]{2,1,0:T(8,128)(2,1)}, bf16[2,192,512]{2,1,0:T(8,128)(2,1)}, u32[]{:S(2)}, u32[]{:S(2)}) collective-permute-start(bf16[2,192,512]{2,1,0:T(8,128)(2,1)} %pad_maximum_fusion.5), channel_id=1, source_target_pairs={{0,1},{1,0},{2,3},{3,2},{4,5},{5,4},{6,7},{7,6},{8,9},{9,8},{10,11... | collective-permute-start | bytes 1179656 | tf_op jit(solution)/shard_map/ppermute | solution.py:82
  114.0 13.9 %copy-start.36 = (bf16[2,288,256]{2,1,0:T(8,128)(2,1)}, bf16[2,288,256]{2,1,0:T(8,128)(2,1)S(1)}, u32[]{:S(2)}) copy-start(bf16[2,288,256]{2,1,0:T(8,128)(2,1)S(1)} %collective-permute-done.15) | copy-start | bytes 884740
  138.5 34.2 %all-to-all-start.3 = ((bf16[8,80,768]{2,1,0:T(8,128)(2,1)}), bf16[8,80,768]{2,1,0:T(8,128)(2,1)S(1)}, u32[]{:S(2)}, u32[]{:S(2)}) async-start(bf16[8,80,768]{2,1,0:T(8,128)(2,1)} %bitcast.150), calls=%async_computation.3 | async-start | bytes 1966080 | tf_op jit(solution)/shard_map/all_to_all | solution.py:139
  142.6 5.3 %collective-permute-start.18 = (bf16[512,768]{1,0:T(8,128)(2,1)S(1)}, bf16[512,768]{1,0:T(8,128)(2,1)S(1)}, u32[]{:S(2)}, u32[]{:S(2)}) collective-permute-start(bf16[512,768]{1,0:T(8,128)(2,1)S(1)} %copy-done.9), channel_id=1, source_target_pairs={{0,1},{1,0},{2,3},{3,2},{4,5},{5,4},{6,7},{7,6},{8,9},{9,8},{10,11... | collective-permute-start | bytes 2359304 | tf_op jit(solution)/shard_map/ppermute | solution.py:82
  143.6 33.7 %copy-start.16 = (bf16[4,288,256]{2,1,0:T(8,128)(2,1)}, bf16[4,288,256]{2,1,0:T(8,128)(2,1)S(1)}, u32[]{:S(2)}) copy-start(bf16[4,288,256]{2,1,0:T(8,128)(2,1)S(1)} %get-tuple-element.279.refs_3_) | copy-start | bytes 1769476
  143.6 24.7 %collective-permute-start.16 = (bf16[4,288,256]{2,1,0:T(8,128)(2,1)}, bf16[4,288,256]{2,1,0:T(8,128)(2,1)S(1)}, u32[]{:S(2)}, u32[]{:S(2)}) collective-permute-start(bf16[4,288,256]{2,1,0:T(8,128)(2,1)} %get-tuple-element.280.refs_0_), channel_id=1, source_target_pairs={{0,4},{1,5},{2,6},{3,7},{4,0},{5,1},{6,2},{7,3},{8,12},{9,13},{10,... | collective-permute-start | bytes 1769480 | tf_op jit(solution)/shard_map/ppermute | solution.py:82
  145.6 35.9 %collective-permute-start.11 = (bf16[512,768]{1,0:T(8,128)(2,1)}, bf16[512,768]{1,0:T(8,128)(2,1)}, u32[]{:S(2)}, u32[]{:S(2)}) collective-permute-start(bf16[512,768]{1,0:T(8,128)(2,1)} %get-tuple-element.107.hn_ref), channel_id=1, source_target_pairs={{0,1},{1,0},{2,3},{3,2},{4,5},{5,4},{6,7},{7,6},{8,9},{9,8},{10,11... | collective-permute-start | bytes 2359304 | tf_op jit(solution)/shard_map/ppermute | solution.py:82
  145.8 31.4 %collective-permute-start.17 = (bf16[4,288,256]{2,1,0:T(8,128)(2,1)S(1)}, bf16[4,288,256]{2,1,0:T(8,128)(2,1)}, u32[]{:S(2)}, u32[]{:S(2)}) collective-permute-start(bf16[4,288,256]{2,1,0:T(8,128)(2,1)S(1)} %get-tuple-element.279.refs_3_), channel_id=1, source_target_pairs={{0,2},{1,3},{2,0},{3,1},{4,6},{5,7},{6,4},{7,5},{8,10},{9,11},{10,... | collective-permute-start | bytes 1769480 | tf_op jit(solution)/shard_map/ppermute | solution.py:82
  170.7 38.2 %collective-permute-start.19 = (bf16[8,288,256]{2,1,0:T(8,128)(2,1)}, bf16[8,288,256]{2,1,0:T(8,128)(2,1)}, u32[]{:S(2)}, u32[]{:S(2)}) collective-permute-start(bf16[8,288,256]{2,1,0:T(8,128)(2,1)} %pad_maximum_fusion.2), channel_id=1, source_target_pairs={{0,2},{1,3},{2,0},{3,1},{4,6},{5,7},{6,4},{7,5},{8,10},{9,11},{10,... | collective-permute-start | bytes 3538952 | tf_op jit(solution)/shard_map/ppermute | solution.py:82
  172.7 31.6 %all-to-all-start.4 = ((bf16[8,64,768]{2,1,0:T(8,128)(2,1)}), bf16[8,64,768]{2,1,0:T(8,128)(2,1)S(1)}, u32[]{:S(2)}, u32[]{:S(2)}) async-start(bf16[8,64,768]{2,1,0:T(8,128)(2,1)} %bitcast.46), calls=%async_computation.4 | async-start | bytes 1572864 | tf_op jit(solution)/shard_map/all_to_all | solution.py:139
  179.5 38.3 %collective-permute-start.20 = (bf16[8,288,256]{2,1,0:T(8,128)(2,1)}, bf16[8,288,256]{2,1,0:T(8,128)(2,1)}, u32[]{:S(2)}, u32[]{:S(2)}) collective-permute-start(bf16[8,288,256]{2,1,0:T(8,128)(2,1)} %pad_maximum_fusion.3), channel_id=1, source_target_pairs={{0,4},{1,5},{2,6},{3,7},{4,0},{5,1},{6,2},{7,3},{8,12},{9,13},{10,... | collective-permute-start | bytes 3538952 | tf_op jit(solution)/shard_map/ppermute | solution.py:82
  204.3 38.5 %copy-start.8 = (bf16[8,64,768]{2,1,0:T(8,128)(2,1)}, bf16[8,64,768]{2,1,0:T(8,128)(2,1)S(1)}, u32[]{:S(2)}) copy-start(bf16[8,64,768]{2,1,0:T(8,128)(2,1)S(1)} %all-to-all-done.4) | copy-start | bytes 2359300
  204.3 58.3 %all-to-all-start.5 = ((bf16[8,80,768]{2,1,0:T(8,128)(2,1)}), bf16[8,80,768]{2,1,0:T(8,128)(2,1)S(1)}, u32[]{:S(2)}, u32[]{:S(2)}) async-start(bf16[8,80,768]{2,1,0:T(8,128)(2,1)} %bitcast.149), calls=%async_computation.5 | async-start | bytes 1966080 | tf_op jit(solution)/shard_map/all_to_all | solution.py:139
  242.8 29.0 %collective-permute-start.21 = (bf16[1024,768]{1,0:T(8,128)(2,1)}, bf16[1024,768]{1,0:T(8,128)(2,1)S(1)}, u32[]{:S(2)}, u32[]{:S(2)}) collective-permute-start(bf16[1024,768]{1,0:T(8,128)(2,1)} %get-tuple-element.119), channel_id=1, source_target_pairs={{0,1},{1,0},{2,3},{3,2},{4,5},{5,4},{6,7},{7,6},{8,9},{9,8},{10,11... | collective-permute-start | bytes 4718600 | tf_op jit(solution)/shard_map/ppermute | solution.py:82
  242.8 28.7 %collective-permute-start.22 = (bf16[8,288,256]{2,1,0:T(8,128)(2,1)}, bf16[8,288,256]{2,1,0:T(8,128)(2,1)}, u32[]{:S(2)}, u32[]{:S(2)}) collective-permute-start(bf16[8,288,256]{2,1,0:T(8,128)(2,1)} %get-tuple-element.129), channel_id=1, source_target_pairs={{0,2},{1,3},{2,0},{3,1},{4,6},{5,7},{6,4},{7,5},{8,10},{9,11},{10,... | collective-permute-start | bytes 3538952 | tf_op jit(solution)/shard_map/ppermute | solution.py:82
  242.9 28.9 %collective-permute-start.23 = (bf16[8,288,256]{2,1,0:T(8,128)(2,1)}, bf16[8,288,256]{2,1,0:T(8,128)(2,1)}, u32[]{:S(2)}, u32[]{:S(2)}) collective-permute-start(bf16[8,288,256]{2,1,0:T(8,128)(2,1)} %get-tuple-element.130), channel_id=1, source_target_pairs={{0,4},{1,5},{2,6},{3,7},{4,0},{5,1},{6,2},{7,3},{8,12},{9,13},{10,... | collective-permute-start | bytes 3538952 | tf_op jit(solution)/shard_map/ppermute | solution.py:82
  262.6 30.6 %copy-start.7 = (bf16[8,80,768]{2,1,0:T(8,128)(2,1)}, bf16[8,80,768]{2,1,0:T(8,128)(2,1)S(1)}, u32[]{:S(2)}) copy-start(bf16[8,80,768]{2,1,0:T(8,128)(2,1)S(1)} %all-to-all-done.5) | copy-start | bytes 2949124
  262.6 32.6 %all-to-all-start.6 = ((bf16[8,80,768]{2,1,0:T(8,128)(2,1)}), bf16[8,80,768]{2,1,0:T(8,128)(2,1)}, u32[]{:S(2)}, u32[]{:S(2)}) async-start(bf16[8,80,768]{2,1,0:T(8,128)(2,1)} %get-tuple-element.128), calls=%async_computation.6 | async-start | bytes 1966080 | tf_op jit(solution)/shard_map/all_to_all | solution.py:139
  271.8 21.4 %copy-start.2 = (bf16[1024,768]{1,0:T(8,128)(2,1)}, bf16[1024,768]{1,0:T(8,128)(2,1)S(1)}, u32[]{:S(2)}) copy-start(bf16[1024,768]{1,0:T(8,128)(2,1)S(1)} %collective-permute-done.21.share_ref) | copy-start | bytes 4718596
  271.8 22.0 %copy-start.28 = (bf16[640,768]{1,0:T(8,128)(2,1)S(1)}, bf16[640,768]{1,0:T(8,128)(2,1)}, u32[]{:S(2)}) copy-start(bf16[640,768]{1,0:T(8,128)(2,1)} %get-tuple-element.121) | copy-start | bytes 2949124
  271.8 22.0 %copy-start.30 = (bf16[512,768]{1,0:T(8,128)(2,1)S(1)}, bf16[512,768]{1,0:T(8,128)(2,1)}, u32[]{:S(2)}) copy-start(bf16[512,768]{1,0:T(8,128)(2,1)} %get-tuple-element.126) | copy-start | bytes 2359300
  293.3 45.2 %collective-permute-start.24 = (bf16[2,768,1024]{2,1,0:T(8,128)(2,1)}, bf16[2,768,1024]{2,1,0:T(8,128)(2,1)}, u32[]{:S(2)}, u32[]{:S(2)}) collective-permute-start(bf16[2,768,1024]{2,1,0:T(8,128)(2,1)} %get-tuple-element.148), channel_id=1, source_target_pairs={{0,1},{1,0},{2,3},{3,2},{4,5},{5,4},{6,7},{7,6},{8,9},{9,8},{10,11... | collective-permute-start | bytes 9437192 | tf_op jit(solution)/shard_map/ppermute | solution.py:82
  293.3 43.3 %collective-permute-start.25 = (bf16[2,512,768]{2,1,0:T(8,128)(2,1)}, bf16[2,512,768]{2,1,0:T(8,128)(2,1)S(1)}, u32[]{:S(2)}, u32[]{:S(2)}) collective-permute-start(bf16[2,512,768]{2,1,0:T(8,128)(2,1)} %get-tuple-element.150), channel_id=1, source_target_pairs={{0,1},{1,0},{2,3},{3,2},{4,5},{5,4},{6,7},{7,6},{8,9},{9,8},{10,11... | collective-permute-start | bytes 4718600 | tf_op jit(solution)/shard_map/ppermute | solution.py:82
  295.2 63.1 %all-to-all-start.7 = ((bf16[8,144,768]{2,1,0:T(8,128)(2,1)}), bf16[8,144,768]{2,1,0:T(8,128)(2,1)S(1)}, u32[]{:S(2)}, u32[]{:S(2)}) async-start(bf16[8,144,768]{2,1,0:T(8,128)(2,1)} %pad_maximum_fusion), calls=%async_computation.7 | async-start | bytes 3538944 | tf_op jit(solution)/shard_map/all_to_all | solution.py:139
  307.1 16.6 %copy-start.25 = (bf16[8,288,256]{2,1,0:T(8,128)(2,1)S(1)}, bf16[8,288,256]{2,1,0:T(8,128)(2,1)}, u32[]{:S(2)}) copy-start(bf16[8,288,256]{2,1,0:T(8,128)(2,1)} %get-tuple-element.153) | copy-start | bytes 3538948
  321.8 11.0 %collective-permute-start.26 = (bf16[2,192,512]{2,1,0:T(8,128)(2,1)S(1)}, bf16[2,192,512]{2,1,0:T(8,128)(2,1)S(1)}, u32[]{:S(2)}, u32[]{:S(2)}) collective-permute-start(bf16[2,192,512]{2,1,0:T(8,128)(2,1)S(1)} %slice.217), channel_id=1, source_target_pairs={{0,2},{1,3},{2,0},{3,1},{4,6},{5,7},{6,4},{7,5},{8,10},{9,11},{10,... | collective-permute-start | bytes 1179656 | tf_op jit(solution)/shard_map/ppermute | solution.py:82
  325.0 30.5 %collective-permute-start.28 = (bf16[4,288,256]{2,1,0:T(8,128)(2,1)S(1)}, bf16[4,288,256]{2,1,0:T(8,128)(2,1)S(1)}, u32[]{:S(2)}, u32[]{:S(2)}) collective-permute-start(bf16[4,288,256]{2,1,0:T(8,128)(2,1)S(1)} %add_convert_fusion.6), channel_id=1, source_target_pairs={{0,4},{1,5},{2,6},{3,7},{4,0},{5,1},{6,2},{7,3},{8,12},{9,13},{10,... | collective-permute-start | bytes 1769480 | tf_op jit(solution)/shard_map/ppermute | solution.py:82
  333.5 4.2 collective-permute-start.27
  334.8 20.7 %collective-permute-start.29 = (bf16[4,288,256]{2,1,0:T(8,128)(2,1)S(1)}, bf16[4,288,256]{2,1,0:T(8,128)(2,1)}, u32[]{:S(2)}, u32[]{:S(2)}) collective-permute-start(bf16[4,288,256]{2,1,0:T(8,128)(2,1)S(1)} %add_convert_fusion.5), channel_id=1, source_target_pairs={{0,2},{1,3},{2,0},{3,1},{4,6},{5,7},{6,4},{7,5},{8,10},{9,11},{10,... | collective-permute-start | bytes 1769480 | tf_op jit(solution)/shard_map/ppermute | solution.py:82
  360.0 33.8 %all-to-all-start.8 = ((bf16[4,2,288,256]{3,2,1,0:T(8,128)(2,1)}), bf16[4,2,288,256]{3,2,1,0:T(8,128)(2,1)S(1)}, u32[]{:S(2)}, u32[]{:S(2)}) async-start(bf16[4,2,288,256]{3,2,1,0:T(8,128)(2,1)} %copy.238), calls=%async_computation.8 | async-start | bytes 2359296 | tf_op jit(solution)/shard_map/all_to_all | solution.py:102
  366.3 64.8 %collective-permute-start.31 = (bf16[768,1024]{1,0:T(8,128)(2,1)}, bf16[768,1024]{1,0:T(8,128)(2,1)}, u32[]{:S(2)}, u32[]{:S(2)}) collective-permute-start(bf16[768,1024]{1,0:T(8,128)(2,1)} %fusion.4), channel_id=1, source_target_pairs={{0,2},{1,3},{2,0},{3,1},{4,6},{5,7},{6,4},{7,5},{8,10},{9,11},{10,... | collective-permute-start | bytes 4718600 | tf_op jit(solution)/shard_map/ppermute | solution.py:82
  366.7 12.5 %copy-start.22 = (bf16[768,896]{1,0:T(8,128)(2,1)S(1)}, bf16[768,896]{1,0:T(8,128)(2,1)}, u32[]{:S(2)}) copy-start(bf16[768,896]{1,0:T(8,128)(2,1)} %get-tuple-element.163) | copy-start | bytes 4128772
  381.2 30.8 %collective-permute-start.34 = (bf16[8,2,24,896]{3,2,0,1:T(8,128)(2,1)}, bf16[8,2,24,896]{3,2,0,1:T(8,128)(2,1)}, u32[]{:S(2)}, u32[]{:S(2)}) collective-permute-start(bf16[8,2,24,896]{3,2,0,1:T(8,128)(2,1)} %bitcast.130), channel_id=1, source_target_pairs={{0,1},{1,0},{2,3},{3,2},{4,5},{5,4},{6,7},{7,6},{8,9},{9,8},{10,11... | collective-permute-start | bytes 2064392 | tf_op jit(solution)/shard_map/ppermute | solution.py:82
  393.9 12.8 %copy-start.18 = (bf16[2,512,768]{2,1,0:T(8,128)(2,1)S(1)}, bf16[2,512,768]{2,1,0:T(8,128)(2,1)}, u32[]{:S(2)}) copy-start(bf16[2,512,768]{2,1,0:T(8,128)(2,1)} %get-tuple-element.149) | copy-start | bytes 4718596
  406.1 25.0 %collective-permute-start.30 = (bf16[2,512,768]{2,1,0:T(8,128)(2,1)}, bf16[2,512,768]{2,1,0:T(8,128)(2,1)}, u32[]{:S(2)}, u32[]{:S(2)}) collective-permute-start(bf16[2,512,768]{2,1,0:T(8,128)(2,1)} %get-tuple-element.167), channel_id=1, source_target_pairs={{0,1},{1,0},{2,3},{3,2},{4,5},{5,4},{6,7},{7,6},{8,9},{9,8},{10,11... | collective-permute-start | bytes 4718600 | tf_op jit(solution)/shard_map/ppermute | solution.py:82
  407.6 23.5 %collective-permute-start.32 = (bf16[512,768]{1,0:T(8,128)(2,1)}, bf16[512,768]{1,0:T(8,128)(2,1)}, u32[]{:S(2)}, u32[]{:S(2)}) collective-permute-start(bf16[512,768]{1,0:T(8,128)(2,1)} %fusion.10), channel_id=1, source_target_pairs={{0,2},{1,3},{2,0},{3,1},{4,6},{5,7},{6,4},{7,5},{8,10},{9,11},{10,... | collective-permute-start | bytes 2359304 | tf_op jit(solution)/shard_map/ppermute | solution.py:82
  414.2 28.2 %collective-permute-start.35 = (bf16[8,24,896]{2,1,0:T(8,128)(2,1)}, bf16[8,24,896]{2,1,0:T(8,128)(2,1)}, u32[]{:S(2)}, u32[]{:S(2)}) collective-permute-start(bf16[8,24,896]{2,1,0:T(8,128)(2,1)} %dynamic-slice_bitcast_fusion), channel_id=1, source_target_pairs={{0,2},{1,3},{2,0},{3,1},{4,6},{5,7},{6,4},{7,5},{8,10},{9,11},{10,... | collective-permute-start | bytes 1032200 | tf_op jit(solution)/shard_map/ppermute | solution.py:82
  416.2 45.4 %all-to-all-start.9 = ((bf16[32,24,640]{2,1,0:T(8,128)(2,1)}), bf16[32,24,640]{2,1,0:T(8,128)(2,1)}, u32[]{:S(2)}, u32[]{:S(2)}) async-start(bf16[32,24,640]{2,1,0:T(8,128)(2,1)} %bitcast.147), calls=%async_computation.9 | async-start | bytes 1966080 | tf_op jit(solution)/shard_map/all_to_all | solution.py:139
  422.7 13.5 %copy-start.27 = (f32[288,256]{1,0:T(8,128)S(1)}, f32[288,256]{1,0:T(8,128)}, u32[]{:S(2)}) copy-start(f32[288,256]{1,0:T(8,128)} %get-tuple-element.176) | copy-start | bytes 884740
  433.6 40.3 %collective-permute-start.33 = (bf16[512,768]{1,0:T(8,128)(2,1)}, bf16[512,768]{1,0:T(8,128)(2,1)}, u32[]{:S(2)}, u32[]{:S(2)}) collective-permute-start(bf16[512,768]{1,0:T(8,128)(2,1)} %fusion.11), channel_id=1, source_target_pairs={{0,2},{1,3},{2,0},{3,1},{4,6},{5,7},{6,4},{7,5},{8,10},{9,11},{10,... | collective-permute-start | bytes 2359304 | tf_op jit(solution)/shard_map/ppermute | solution.py:82
  442.4 18.1 %collective-permute-start.36 = (f32[2,4,24,256]{3,2,1,0:T(8,128)S(1)}, f32[2,4,24,256]{3,2,1,0:T(8,128)}, u32[]{:S(2)}, u32[]{:S(2)}) collective-permute-start(f32[2,4,24,256]{3,2,1,0:T(8,128)S(1)} %get-tuple-element.284), channel_id=1, source_target_pairs={{0,1},{1,0},{2,3},{3,2},{4,5},{5,4},{6,7},{7,6},{8,9},{9,8},{10,11... | collective-permute-start | bytes 589832 | tf_op jit(solution)/shard_map/ppermute | solution.py:82
  461.6 18.2 %all-to-all-start.10 = ((bf16[8,24,896]{2,1,0:T(8,128)(2,1)}), bf16[8,24,896]{2,1,0:T(8,128)(2,1)S(1)}, u32[]{:S(2)}, u32[]{:S(2)}) async-start(bf16[8,24,896]{2,1,0:T(8,128)(2,1)} %fusion.13), calls=%async_computation.10 | async-start | bytes 688128 | tf_op jit(solution)/shard_map/all_to_all | solution.py:139
  (26 other events, 110.0 us)

commit v3 on v2

--- a/solution.py
+++ b/solution.py
@@ -93,8 +93,12 @@
     return kept.astype(F32) + flip(away, name).astype(F32)
 
 
+def z_shards(shard):
+    return [shard] + [flip(shard, name) for name in ("z1", "z2", "z3")]
+
+
 def z_gather(shard):
-    return jnp.stack([shard] + [flip(shard, name) for name in ("z1", "z2", "z3")])
+    return jnp.stack(z_shards(shard))
 
 
 def z_sum(parts):
@@ -1202,27 +1206,26 @@
     if small:
         heads = after(heads, misc_z)
         misc_parts.append(flip(jnp.concatenate(misc_parts), "x"))
-        shards = z_gather(after(paired_shards(shared_in, shared_out), w_heads))
+        shards = z_shards(after(paired_shards(shared_in, shared_out), w_heads))
     ctx_heads, log_totals = attend(seq, heads, segments)
     ctxs = seq_send_twice(ctx_heads)
     hidden, hn, gates, w_attn, misc, ctx, *sends = middle(
         me, seq, ctxs, layer_input, misc_parts, pick, routes, experts, parts
     )
 
-    sends[0] = after(sends[0], dy_rows, shards) if small else sends[0]
+    shards = together(shards, hn) if small else None
+    sends[0] = after(sends[0], dy_rows, *shards) if small else sends[0]
 
     row_parts = [
         swap(send.reshape(experts, part, width), "dp").reshape(-1, width)
         for part, send in zip(parts, sends, strict=True)
     ]
     if small:
-        shards = after(shards, hn)
-        a0, b0 = shards[:, 0], shards[:, 1]
+        a0, b0 = jnp.stack([part[0] for part in shards]), jnp.stack([part[1] for part in shards])
         a1, b1 = flip(a0, "y"), flip(b0, "x")
-        a2, b2 = flip(jnp.concatenate([a0, a1]), "x"), flip(jnp.concatenate([b0, b1]), "y")
         hn_pair = jnp.concatenate([hn, flip(hn, "c")], axis=0)
         dy_pair = jnp.concatenate([cotangent, flip(cotangent, "c")], axis=0)
-        row_parts[0] = after(row_parts[0], a1, b1, hn_pair, dy_pair)
+        row_parts[0] = after(row_parts[0], a0, b0, hn_pair, dy_pair)
     else:
         w_gate = lax.all_gather(shared_in[:, :units], AXES, axis=0, tiled=True)
         w_up = lax.all_gather(shared_in[:, units:], AXES, axis=0, tiled=True)
@@ -1232,9 +1235,8 @@
     sets, eos, dxes, dgates, low = [], [], [], [], 0
     for k, (part, rows, other) in enumerate(zip(parts, row_parts, others, strict=True)):
         if k == 1:
-            hn_pair = after(hn_pair, dxes[0])
-            shared, dhn, share, *grads = paired(me, hn_pair, dy_pair, (a0, a1, a2), (b0, b1, b2))
-            rows = after(rows, dhn)
+            a0, b0, a1, b1 = together((a0, b0, a1, b1), dxes[0])
+            a2, b2 = flip(jnp.concatenate([a0, a1]), "x"), flip(jnp.concatenate([b0, b1]), "y")
         eo, dxe, dgate, deo, act, d_gate, d_up = expert(
             own, rows, dy_rows if small else dy_rows.reshape(-1, width), low, other, misc, expert_in,
             expert_out, dgates[0] if k == 1 else None,
@@ -1251,32 +1253,33 @@
     if not small:
         backs.append(swap(dgates[0].reshape(experts, capacity), "dp").reshape(1, slots))
     held = backs[:1]
-    if small:
-        share = flip(share, "c")
-        ka, wa, kb, wb = grads
-        ca, cb = flip(wa, "x"), flip(wb, "y")
-        held += [share, ca, cb]
-    else:
+    if not small:
         shared, dhn, grad_gate, grad_up, grad_out = dense(hn, cotangent, w_gate, w_up, w_out)
         share = jnp.zeros((2 * tokens, width), BF16)
     sets = [(after(one[0], *held),) + one[1:] for one in sets]
     in_kept, in_away, out_kept, out_away = expert_grads(seq, sets)
     if small:
-        ca, cb = together((ca, cb), in_kept)
-        wa, wb = add_up([ka[4:], ca[4:]]).astype(BF16), add_up([kb[4:], cb[4:]]).astype(BF16)
-        ea, eb = flip(wa, "y"), flip(wb, "x")
+        hn_pair = after(hn_pair, in_kept)
+        shared, dhn, share, *grads = paired(me, hn_pair, dy_pair, (a0, a1, a2), (b0, b1, b2))
+        share = flip(share, "c")
+        ka, wa, kb, wb = grads
+        ca, cb = flip(wa, "x"), flip(wb, "y")
         in_away, out_away = flip(in_away, "c"), flip(out_away, "c")
-        backs = [after(back, in_kept) for back in backs]
     dh, dctx, grad_attn = middle_back(
         dhn, share, backs, slot_of, routes, gates, misc, hidden, hn, cotangent, ctx, w_attn,
         seq, seq_devs, experts, parts,
     )
 
     dctxs = seq_send_twice(dctx)
+    if small:
+        in_kept, out_kept = together((in_kept, out_kept), dh)
     in_terms, in_far = copies_sum(in_kept, in_away)
     out_terms, out_far = copies_sum(out_kept, out_away)
     if small:
-        dctxs[0] = after(dctxs[0], in_far, out_far)
+        ca, cb = together((ca, cb), dh)
+        wa, wb = add_up([ka[4:], ca[4:]]).astype(BF16), add_up([kb[4:], cb[4:]]).astype(BF16)
+        ea, eb = flip(wa, "y"), flip(wb, "x")
+        dctxs[0] = after(dctxs[0], in_far, out_far, wa, wb)
     came = swap(after(jnp.concatenate(eos, axis=1), backs[-1]), "dp").reshape(-1, width)
     d_heads = []
     for head in range(columns // 192):
@@ -1294,10 +1297,10 @@
         ea, eb = together((ea, eb), d_heads[0])
         wa, wb = add_up([ka[:4], ca[:4], ea]).astype(BF16), add_up([kb[:4], cb[:4], eb]).astype(BF16)
         sums = z_sum(after(jnp.stack([wa, wb], axis=1), came))
-        d_heads[0] = after(d_heads[0], sums)
+        d_heads[0] = after(d_heads[0], sums, out_terms[2])
     dxn_kept, dxn_away, grad_heads = qkv_back(seq, token_blocks, d_heads, w_heads, cosine, sine)
     if small:
-        dxn_away = after(flip(dxn_away, "c"), in_terms[2], out_terms[2])
+        dxn_away = after(flip(dxn_away, "c"), in_terms[2])
     dxn_terms, dxn_far = copies_sum(dxn_kept, dxn_away)
     input_grad = input_back(layer_input, dh, w_heads, dxn_terms)
     layer_output = output_of(

time: 489 us -> 469 us (0.959)
  waiting for transfers between devices: 89.1 us -> 74.1 us
  starting transfers between devices: 101 us -> 94.7 us
    ppermute x37, waiting for transfers between devices: 71 us -> 42.8 us  [flip(): return lax.ppermute(block, AXES, FLIP[name])]
    all_to_all x10, waiting for transfers between devices: 18 us -> 31.3 us  [swap(): return lax.all_to_all(blocks, axis, split_axis=0, concat_axis=0, tiled=True)]
    unnamed x97 -> x115, local copies, waits for them, and re-layouts: 12.2 us -> 13.3 us
  transfers between devices with their start and end apart: 48 -> 48, of which waited for: 13 -> 11; matrix products, arithmetic and copies ran while one was open for 19% -> 20% of each run, Pallas kernels for 40% -> 41%
where the time goes in v3:
time: 469 us; the launch traced here: 462 us
  Pallas kernels  192 us (41%)
  starting transfers between devices  94.7 us (20%)
  waiting for transfers between devices  74.1 us (16%)
  local copies, waits for them, and re-layouts  56.1 us (12%)
  other arithmetic  41.4 us (9%)
    all_to_all x10, starting transfers between devices, swap(): return lax.all_to_all(blocks, axis, split_axis=0, concat_axis=0, tiled=True)  54.4 us
    ppermute x37, waiting for transfers between devices, flip(): return lax.ppermute(block, AXES, FLIP[name])  42.8 us
    pallas_call x2, Pallas kernels, expert(): pl.pallas_call(functools.partial(expert_kernel, low=low), grid_spec=pltpu...  38.7 us
    pallas_call x3, Pallas kernels, attend_back(): pl.pallas_call(attend_back_kernel, grid_spec=pltpu.PrefetchScalarGridSpec...  37.9 us
    ppermute x37, starting transfers between devices, flip(): return lax.ppermute(block, AXES, FLIP[name])  34.6 us
    all_to_all x10, waiting for transfers between devices, swap(): return lax.all_to_all(blocks, axis, split_axis=0, concat_axis=0, tiled=True)  31.3 us
    pallas_call x1, Pallas kernels, paired(): pl.pallas_call(paired_kernel, grid_spec=pltpu.PrefetchScalarGridSpec(num_...  24.9 us
    pallas_call x1, Pallas kernels, expert_grads(): pl.pallas_call(expert_grads_kernel, grid_spec=pltpu.PrefetchScalarGridSpe...  21 us
  transfers between devices with their start and end apart: 48, of which 11 were waited for; matrix products, arithmetic and copies ran while one was open for 20% of the time, Pallas kernels for 41%

profile of v3, /device:TPU:0, one launch (start us, length us, event | category | flops | bytes accessed | tf_op | source)
XLA Modules:
  0.0 462.4 jit_solution(6824151641065458281)
XLA Ops:
  3.8 3.9 all-to-all-start
  14.6 6.4 %all-to-all-start.1 = ((bf16[8,96,640]{2,1,0:T(8,128)(2,1)}), bf16[8,96,640]{2,1,0:T(8,128)(2,1)S(1)}, u32[]{:S(2)}, u32[]{:S(2)}) async-start(bf16[8,96,640]{2,1,0:T(8,128)(2,1)} %maximum_maximum_fusion), calls=%async_computation.1 | async-start | bytes 1966080 | tf_op jit(solution)/shard_map/all_to_all | solution.py:143
  22.8 2.4 convolution_convert_fusion
  25.2 1.8 collective-permute-start.1
  27.0 1.6 fusion.3.refs_8_
  30.2 15.9 %all-to-all-done.1 = bf16[8,96,640]{2,1,0:T(8,128)(2,1)S(1)} async-done(((bf16[8,96,640]{2,1,0:T(8,128)(2,1)}), bf16[8,96,640]{2,1,0:T(8,128)(2,1)S(1)}, u32[]{:S(2)}, u32[]{:S(2)}) %all-to-all-start.1) | async-done | bytes 983072 | tf_op jit(solution)/shard_map/all_to_all | solution.py:143
  46.1 2.1 collective-permute-start.6
  48.1 2.3 collective-permute-start.4
  50.5 2.3 collective-permute-done.6
  52.8 2.6 collective-permute-done.5
  56.0 4.5 all-to-all-start.2
  61.7 1.8 multiply_sine_fusion
  64.4 8.5 %qkv_project.1 = (bf16[4,576,512]{2,1,0:T(8,128)(2,1)}, bf16[768,640]{1,0:T(8,128)(2,1)}) custom-call(s32[1]{0:T(128)} %bitcast.1.seq_ref, s32[1]{0:T(128)} %bitcast.2.dp_ref.own_ref, bf16[512,768]{1,0:T(8,128)(2,1)} %x_ref.1, bf16[512,768]{1,0:T(8,128)(2,1)} %copy-done.29, bf16[512,768]{1,0:T(8,128)(2,1)} %collective-permute-done.1.refs_2_, ...), custom_call_target="tpu_custom_call" | custom-call | flops 1000000000 | bytes 1048576 | tf_op jit(solution)/shard_map/qkv_project/pallas_call | solution.py:207
  73.5 17.6 %attend.1 = (bf16[4,192,512]{2,1,0:T(8,128)(2,1)}, f32[3,1,2048]{2,1,0:T(1,128)}) custom-call(s32[1]{0:T(128)} %bitcast.1.seq_ref, bf16[4,576,512]{2,1,0:T(8,128)(2,1)} %get-tuple-element.178.buf_ref, s32[1,2048]{1,0:T(1,128)} %docs_ref.7), custom_call_target="tpu_custom_call" | custom-call | flops 3000000000 | bytes 1048576 | tf_op jit(solution)/shard_map/attend/pallas_call | solution.py:290
  92.2 1.7 collective-permute-start.7
  93.9 2.0 collective-permute-start.9
  98.9 4.8 %collective-permute-done.9.refs_5_ = bf16[4,48,896]{2,1,0:T(8,128)(2,1)S(1)} collective-permute-done((bf16[4,48,896]{2,1,0:T(8,128)(2,1)S(1)}, bf16[4,48,896]{2,1,0:T(8,128)(2,1)S(1)}, u32[]{:S(2)}, u32[]{:S(2)}) %collective-permute-start.9) | collective-permute-done | bytes 344096 | tf_op jit(solution)/shard_map/ppermute | solution.py:82
  108.9 2.6 collective-permute-start.13
  111.8 2.1 collective-permute-start.15
  115.5 6.2 %collective-permute-done.10.refs_6_ = bf16[8,48,896]{2,1,0:T(8,128)(2,1)S(1)} collective-permute-done((bf16[8,48,896]{2,1,0:T(8,128)(2,1)}, bf16[8,48,896]{2,1,0:T(8,128)(2,1)S(1)}, u32[]{:S(2)}, u32[]{:S(2)}) %collective-permute-start.10) | collective-permute-done | bytes 688160 | tf_op jit(solution)/shard_map/ppermute | solution.py:82
  122.6 5.9 %middle.1 = (f32[512,768]{1,0:T(8,128)}, bf16[512,768]{1,0:T(8,128)(2,1)}, f32[512,128]{1,0:T(8,128)}, bf16[768,768]{1,0:T(8,128)(2,1)}, bf16[768,128]{1,0:T(8,1...) custom-call(s32[1]{0:T(128)} %bitcast.me_ref, s32[1]{0:T(128)} %bitcast.1.seq_ref, ...), custom_call_target="tpu_custom_call" | custom-call | flops 500000000 | bytes 1048576 | tf_op jit(solution)/shard_map/middle/pallas_call | solution.py:451
  128.5 6.3 %collective-permute-done.14 = bf16[2,288,256]{2,1,0:T(8,128)(2,1)S(1)} collective-permute-done((bf16[2,288,256]{2,1,0:T(8,128)(2,1)S(1)}, bf16[2,288,256]{2,1,0:T(8,128)(2,1)S(1)}, u32[]{:S(2)}, u32[]{:S(2)}) %collective-permute-start.14) | collective-permute-done | bytes 294944 | tf_op jit(solution)/shard_map/ppermute | solution.py:82
  135.6 7.4 %all-to-all-start.3 = ((bf16[8,80,768]{2,1,0:T(8,128)(2,1)}), bf16[8,80,768]{2,1,0:T(8,128)(2,1)S(1)}, u32[]{:S(2)}, u32[]{:S(2)}) async-start(bf16[8,80,768]{2,1,0:T(8,128)(2,1)} %bitcast.134), calls=%async_computation.3 | async-start | bytes 1966080 | tf_op jit(solution)/shard_map/all_to_all | solution.py:143
  144.0 2.2 constant_dynamic-update-slice_fusion.9.dy_ref
  149.1 2.1 collective-permute-start.17
  152.8 14.2 %all-to-all-done.3 = bf16[8,80,768]{2,1,0:T(8,128)(2,1)S(1)} async-done(((bf16[8,80,768]{2,1,0:T(8,128)(2,1)}), bf16[8,80,768]{2,1,0:T(8,128)(2,1)S(1)}, u32[]{:S(2)}, u32[]{:S(2)}) %all-to-all-start.3) | async-done | bytes 983072 | tf_op jit(solution)/shard_map/all_to_all | solution.py:143
  167.0 3.5 all-to-all-start.5
  171.5 2.1 constant_dynamic-update-slice_fusion.5.x_ref
  173.6 20.8 %expert.2 = (bf16[640,768]{1,0:T(8,128)(2,1)}, bf16[640,768]{1,0:T(8,128)(2,1)}, f32[640,1]{1,0:T(8,128)}, bf16[640,768]{1,0:T(8,128)(2,1)}, bf16[640,2048]{1,0:...) custom-call(s32[1]{0:T(128)} %bitcast.2.dp_ref.own_ref, bf16[640,768]{1,0:T(8,128)(2,1)} %bitcast.124, ...), custom_call_target="tpu_custom_call" | custom-call | flops 12079595520 | bytes 41943040 | tf_op jit(solution)/shard_map/expert/pallas_call | solution.py:701
  194.4 5.9 %all-to-all-start.4 = ((bf16[8,80,768]{2,1,0:T(8,128)(2,1)}), bf16[8,80,768]{2,1,0:T(8,128)(2,1)S(1)}, u32[]{:S(2)}, u32[]{:S(2)}) async-start(bf16[8,80,768]{2,1,0:T(8,128)(2,1)} %bitcast.135), calls=%async_computation.4 | async-start | bytes 1966080 | tf_op jit(solution)/shard_map/all_to_all | solution.py:143
  202.0 2.2 pad_maximum_fusion.1
  206.0 2.1 collective-permute-start.20
  208.1 18.0 %expert.3 = (bf16[512,768]{1,0:T(8,128)(2,1)}, bf16[8,80,768]{2,1,0:T(8,128)(2,1)}, f32[512,1]{1,0:T(8,128)}, bf16[512,768]{1,0:T(8,128)(2,1)}, bf16[512,2048]{1...) custom-call(s32[1]{0:T(128)} %bitcast.2.dp_ref.own_ref, bf16[512,768]{1,0:T(8,128)(2,1)} %bitcast.127, ...), custom_call_target="tpu_custom_call" | custom-call | flops 9663676416 | bytes 41943040 | tf_op jit(solution)/shard_map/expert/pallas_call | solution.py:701
  226.1 21.0 %expert_grads.1 = (bf16[2,768,1024]{2,1,0:T(8,128)(2,1)}, bf16[2,768,1024]{2,1,0:T(8,128)(2,1)}, bf16[2,512,768]{2,1,0:T(8,128)(2,1)}, bf16[2,512,768]{2,1,0:T(8,128)(2,1)}) custom-call(s32[1]{0:T(128)} %bitcast.1.seq_ref, bf16[640,768]{1,0:T(8,128)(2,1)} %bitcast.125, bf16[640,768]{1,0:T(8,128)(2,1)} %get-tuple-element.127.refs_1_, ...), custom_call_target="tpu_custom_call" | custom-call | flops 3623878656 | bytes 4194304 | tf_op jit(solution)/shard_map/expert_grads/pallas_call | solution.py:807
  247.1 4.6 all-to-all-start.6
  251.7 24.9 %dense_pair.1 = (f32[512,768]{1,0:T(8,128)}, f32[512,768]{1,0:T(8,128)}, bf16[1024,768]{1,0:T(8,128)(2,1)}, bf16[8,288,256]{2,1,0:T(8,128)(2,1)}, bf16[8,288,256...) custom-call(s32[1]{0:T(128)} %bitcast.me_ref, ...), custom_call_target="tpu_custom_call" | custom-call | flops 14495514624 | bytes 31457280 | tf_op jit(solution)/shard_map/dense_pair/pallas_call | solution.py:595
  277.1 1.6 collective-permute-start.24
  278.7 2.0 collective-permute-start.25
  280.7 2.9 pad_maximum_fusion
  284.5 4.7 %all-to-all-start.7 = ((bf16[8,144,768]{2,1,0:T(8,128)(2,1)}), bf16[8,144,768]{2,1,0:T(8,128)(2,1)S(1)}, u32[]{:S(2)}, u32[]{:S(2)}) async-start(bf16[8,144,768]{2,1,0:T(8,128)(2,1)} %pad_maximum_fusion), calls=%async_computation.7 | async-start | bytes 3538944 | tf_op jit(solution)/shard_map/all_to_all | solution.py:143
  290.4 13.7 %middle_back.1 = (f32[512,768]{1,0:T(8,128)}, bf16[4,192,512]{2,1,0:T(8,128)(2,1)}, bf16[768,896]{1,0:T(8,128)(2,1)}) custom-call(f32[512,768]{1,0:T(8,128)} %get-tuple-element.152.dhn_ref, bf16[1024,768]{1,0:T(8,128)(2,1)} %copy-done.2, s32[512,2]{1,0:T(8,128)} %copy-done.5, s32[512,2]{1,0:T(8,128)} %copy.204.refs_9_.routes_ref, ...), custom_call_target="tpu_custom_call" | custom-call | flops 3000000000 | bytes 16777216 | tf_op jit(solution)/shard_map/middle_back/pallas_call | solution.py:900
  306.7 15.4 %collective-permute-done.25 = bf16[8,288,256]{2,1,0:T(8,128)(2,1)} collective-permute-done((bf16[8,288,256]{2,1,0:T(8,128)(2,1)}, bf16[8,288,256]{2,1,0:T(8,128)(2,1)}, u32[]{:S(2)}, u32[]{:S(2)}) %collective-permute-start.25) | collective-permute-done | bytes 1179680 | tf_op jit(solution)/shard_map/ppermute | solution.py:82
  326.2 2.2 fusion.10
  329.2 3.3 fusion.4
  332.4 12.8 %attend_back.3.refs_4_ = bf16[4,192,512]{2,1,0:T(8,128)(2,1)} custom-call(s32[1]{0:T(128)} %bitcast.1.seq_ref, bf16[4,576,512]{2,1,0:T(8,128)(2,1)} %get-tuple-element.178.buf_ref, bf16[4,192,512]{2,1,0:T(8,128)(2,1)} %get-tuple-element.168.d0_ref, bf16[1,192,512]{2,1,0:T(8,128)(2,1)} %get-tuple-element.296.d1_ref, ...), custom_call_target="tpu_custom_call" | custom-call | flops 4000000000 | bytes 1048576 | tf_op jit(solution)/shard_map/attend_back/pallas_call | solution.py:368
  349.6 5.7 %all-to-all-start.8 = ((bf16[4,2,288,256]{3,2,1,0:T(8,128)(2,1)}), bf16[4,2,288,256]{3,2,1,0:T(8,128)(2,1)S(1)}, u32[]{:S(2)}, u32[]{:S(2)}) async-start(bf16[4,2,288,256]{3,2,1,0:T(8,128)(2,1)} %copy.214), calls=%async_computation.8 | async-start | bytes 2359296 | tf_op jit(solution)/shard_map/all_to_all | solution.py:106
  355.3 2.1 slice_bitcast_fusion.2
  357.4 1.6 collective-permute-start.30
  359.4 12.5 %attend_back.4.refs_5_ = bf16[4,192,512]{2,1,0:T(8,128)(2,1)} custom-call(s32[1]{0:T(128)} %bitcast.1.seq_ref, bf16[4,576,512]{2,1,0:T(8,128)(2,1)} %get-tuple-element.178.buf_ref, bf16[4,192,512]{2,1,0:T(8,128)(2,1)} %get-tuple-element.168.d0_ref, bf16[1,192,512]{2,1,0:T(8,128)(2,1)} %get-tuple-element.296.d1_ref, ...), custom_call_target="tpu_custom_call" | custom-call | flops 4000000000 | bytes 1048576 | tf_op jit(solution)/shard_map/attend_back/pallas_call | solution.py:368
  373.9 12.6 %attend_back.5.refs_6_ = bf16[4,192,512]{2,1,0:T(8,128)(2,1)} custom-call(s32[1]{0:T(128)} %bitcast.1.seq_ref, bf16[4,576,512]{2,1,0:T(8,128)(2,1)} %get-tuple-element.178.buf_ref, bf16[4,192,512]{2,1,0:T(8,128)(2,1)} %get-tuple-element.168.d0_ref, bf16[1,192,512]{2,1,0:T(8,128)(2,1)} %get-tuple-element.296.d1_ref, ...), custom_call_target="tpu_custom_call" | custom-call | flops 4000000000 | bytes 1048576 | tf_op jit(solution)/shard_map/attend_back/pallas_call | solution.py:368
  386.7 12.3 %qkv_back.1 = (bf16[2,512,768]{2,1,0:T(8,128)(2,1)}, bf16[2,512,768]{2,1,0:T(8,128)(2,1)}, bf16[768,640]{1,0:T(8,128)(2,1)}) custom-call(s32[1]{0:T(128)} %bitcast.1.seq_ref, bf16[512,768]{1,0:T(8,128)(2,1)} %x_ref.1, bf16[512,768]{1,0:T(8,128)(2,1)} %copy-done.29, bf16[512,768]{1,0:T(8,128)(2,1)} %collective-permute-done.1.refs_2_, ...), custom_call_target="tpu_custom_call" | custom-call | flops 12000000000 | bytes 12582912 | tf_op jit(solution)/shard_map/qkv_back/pallas_call | solution.py:1009
  400.7 1.6 slice_bitcast_fusion
  404.6 1.6 collective-permute-start.35
  407.8 5.4 %all-to-all-start.9 = ((bf16[32,24,640]{2,1,0:T(8,128)(2,1)}), bf16[32,24,640]{2,1,0:T(8,128)(2,1)}, u32[]{:S(2)}, u32[]{:S(2)}) async-start(bf16[32,24,640]{2,1,0:T(8,128)(2,1)} %bitcast.133), calls=%async_computation.9 | async-start | bytes 1966080 | tf_op jit(solution)/shard_map/all_to_all | solution.py:143
  413.3 2.5 fusion.11
  415.8 1.9 collective-permute-start.33
  417.7 3.9 collective-permute-done.35
  421.8 1.9 fusion.13
  423.7 2.1 slice_bitcast_fusion.4.refs_1_
  425.8 2.6 add_bitcast_fusion.1
  428.4 4.1 add_bitcast_fusion
  433.6 6.3 %output_of.1 = f32[512,768]{1,0:T(8,128)} custom-call(f32[512,768]{1,0:T(8,128)} %get-tuple-element.112.hidden_ref, f32[512,768]{1,0:T(8,128)} %get-tuple-element.144.dense_ref, bf16[1024,768]{1,0:T(8,128)(2,1)} %copy-done.2, s32[512,2]{1,0:T(8,128)} %copy-done.4, f32[512,128]{1,0:T(8,128)} %get-tuple-element.146.gates_ref, bf16[1152,768]{1,0:T(8,128)(2,1)} %bitcast.120), custom_call_target="tpu_custom_call" | custom-call | flops 2000000000 | bytes 8388608 | tf_op jit(solution)/shard_map/output_of/pallas_call | solution.py:934
  441.0 8.0 %all-to-all-start.10 = ((bf16[8,24,896]{2,1,0:T(8,128)(2,1)}), bf16[8,24,896]{2,1,0:T(8,128)(2,1)S(1)}, u32[]{:S(2)}, u32[]{:S(2)}) async-start(bf16[8,24,896]{2,1,0:T(8,128)(2,1)} %fusion.13), calls=%async_computation.10 | async-start | bytes 688128 | tf_op jit(solution)/shard_map/all_to_all | solution.py:143
  454.3 4.6 %input_back.1 = f32[512,768]{1,0:T(8,128)} custom-call(bf16[512,768]{1,0:T(8,128)(2,1)} %x_ref.1, f32[512,768]{1,0:T(8,128)} %get-tuple-element.157.dh_ref, bf16[768,640]{1,0:T(8,128)(2,1)} %get-tuple-element.116.refs_7_.w_ref, bf16[512,768]{1,0:T(8,128)(2,1)} %slice_bitcast_fusion.5.refs_0_, bf16[512,768]{1,0:T(8,128)(2,1)} %slice_bitcast_fusion.4.refs_1_, ...), custom_call_target="tpu_custom_call" | custom-call | flops 100000000 | bytes 6291456 | tf_op jit(solution)/shard_map/input_back/pallas_call | solution.py:1043
  (286 shorter events, 72.2 us)
Async XLA Ops:
  0.6 9.1 %copy-start.50 = (s32[512]{0:T(512)S(1)}, s32[512]{0:T(512)}, u32[]{:S(2)}) copy-start(s32[512]{0:T(512)} %param.18) | copy-start | bytes 6148
  0.7 62.8 %collective-permute-start = (bf16[512,768]{1,0:T(8,128)(2,1)}, bf16[512,768]{1,0:T(8,128)(2,1)S(1)}, u32[]{:S(2)}, u32[]{:S(2)}) collective-permute-start(bf16[512,768]{1,0:T(8,128)(2,1)} %x_ref.1), channel_id=1, source_target_pairs={{0,1},{1,0},{2,3},{3,2},{4,5},{5,4},{6,7},{7,6},{8,9},{9,8},{10,11... | collective-permute-start | bytes 2359304 | tf_op jit(solution)/shard_map/ppermute | solution.py:82
  3.8 9.4 %all-to-all-start = ((bf16[4,24,640]{2,1,0:T(8,128)(2,1)}), bf16[4,24,640]{2,1,0:T(8,128)(2,1)S(1)}, u32[]{:S(2)}, u32[]{:S(2)}) async-start(bf16[4,24,640]{2,1,0:T(8,128)(2,1)} %copy.194), calls=%async_computation | async-start | bytes 245760 | tf_op jit(solution)/shard_map/all_to_all | solution.py:143
  10.6 11.8 %copy-start.5 = (s32[512,2]{1,0:T(8,128)}, s32[512,2]{1,0:T(8,128)S(1)}, u32[]{:S(2)}) copy-start(s32[512,2]{1,0:T(8,128)S(1)} %get-tuple-element.311.slots_ref) | copy-start | bytes 12292
  14.6 31.4 %all-to-all-start.1 = ((bf16[8,96,640]{2,1,0:T(8,128)(2,1)}), bf16[8,96,640]{2,1,0:T(8,128)(2,1)S(1)}, u32[]{:S(2)}, u32[]{:S(2)}) async-start(bf16[8,96,640]{2,1,0:T(8,128)(2,1)} %maximum_maximum_fusion), calls=%async_computation.1 | async-start | bytes 1966080 | tf_op jit(solution)/shard_map/all_to_all | solution.py:143
  21.8 7.5 %collective-permute-start.3 = (bf16[24,896]{1,0:T(8,128)(2,1)}, bf16[24,896]{1,0:T(8,128)(2,1)}, u32[]{:S(2)}, u32[]{:S(2)}) collective-permute-start(bf16[24,896]{1,0:T(8,128)(2,1)} %get-tuple-element.318), channel_id=1, source_target_pairs={{0,1},{1,0},{2,3},{3,2},{4,5},{5,4},{6,7},{7,6},{8,9},{9,8},{10,11... | collective-permute-start | bytes 129032 | tf_op jit(solution)/shard_map/ppermute | solution.py:82
  25.2 25.2 %collective-permute-start.1 = (bf16[512,768]{1,0:T(8,128)(2,1)S(1)}, bf16[512,768]{1,0:T(8,128)(2,1)}, u32[]{:S(2)}, u32[]{:S(2)}) collective-permute-start(bf16[512,768]{1,0:T(8,128)(2,1)S(1)} %copy-done.1), channel_id=1, source_target_pairs={{0,2},{1,3},{2,0},{3,1},{4,6},{5,7},{6,4},{7,5},{8,10},{9,11},{10,... | collective-permute-start | bytes 2359304 | tf_op jit(solution)/shard_map/ppermute | solution.py:82
  46.1 10.0 %copy-start.3 = (bf16[8,96,640]{2,1,0:T(8,128)(2,1)}, bf16[8,96,640]{2,1,0:T(8,128)(2,1)S(1)}, u32[]{:S(2)}) copy-start(bf16[8,96,640]{2,1,0:T(8,128)(2,1)S(1)} %all-to-all-done.1) | copy-start | bytes 2949124
  46.1 6.7 %collective-permute-start.6 = (bf16[48,896]{1,0:T(8,128)(2,1)S(1)}, bf16[48,896]{1,0:T(8,128)(2,1)S(1)}, u32[]{:S(2)}, u32[]{:S(2)}) collective-permute-start(bf16[48,896]{1,0:T(8,128)(2,1)S(1)} %bitcast.143), channel_id=1, source_target_pairs={{0,24},{1,25},{2,26},{3,27},{4,28},{5,29},{6,30},{7,31},{8,16},{9,... | collective-permute-start | bytes 258056 | tf_op jit(solution)/shard_map/ppermute | solution.py:82
  48.1 7.2 %collective-permute-start.5 = (bf16[48,896]{1,0:T(8,128)(2,1)S(1)}, bf16[48,896]{1,0:T(8,128)(2,1)S(1)}, u32[]{:S(2)}, u32[]{:S(2)}) collective-permute-start(bf16[48,896]{1,0:T(8,128)(2,1)S(1)} %bitcast.144), channel_id=1, source_target_pairs={{0,16},{1,17},{2,18},{3,19},{4,20},{5,21},{6,22},{7,23},{8,24},{9,... | collective-permute-start | bytes 258056 | tf_op jit(solution)/shard_map/ppermute | solution.py:82
  48.1 7.2 %collective-permute-start.4 = (bf16[48,896]{1,0:T(8,128)(2,1)S(1)}, bf16[48,896]{1,0:T(8,128)(2,1)S(1)}, u32[]{:S(2)}, u32[]{:S(2)}) collective-permute-start(bf16[48,896]{1,0:T(8,128)(2,1)S(1)} %bitcast.145), channel_id=1, source_target_pairs={{0,8},{1,9},{2,10},{3,11},{4,12},{5,13},{6,14},{7,15},{8,0},{9,1},... | collective-permute-start | bytes 258056 | tf_op jit(solution)/shard_map/ppermute | solution.py:82
  50.5 13.0 %collective-permute-start.2 = (bf16[512,768]{1,0:T(8,128)(2,1)}, bf16[512,768]{1,0:T(8,128)(2,1)}, u32[]{:S(2)}, u32[]{:S(2)}) collective-permute-start(bf16[512,768]{1,0:T(8,128)(2,1)} %collective-permute-done.1.refs_2_), channel_id=1, source_target_pairs={{0,1},{1,0},{2,3},{3,2},{4,5},{5,4},{6,7},{7,6},{8,9},{9,8},{10,11... | collective-permute-start | bytes 2359304 | tf_op jit(solution)/shard_map/ppermute | solution.py:82
  56.0 37.9 %copy-start.24 = (bf16[4,48,896]{2,1,0:T(8,128)(2,1)}, bf16[4,48,896]{2,1,0:T(8,128)(2,1)S(1)}, u32[]{:S(2)}) copy-start(bf16[4,48,896]{2,1,0:T(8,128)(2,1)S(1)} %pad_maximum_fusion.8.refs_4_) | copy-start | bytes 1032196
  56.0 78.8 %all-to-all-start.2 = ((bf16[8,144,768]{2,1,0:T(8,128)(2,1)}), bf16[8,144,768]{2,1,0:T(8,128)(2,1)}, u32[]{:S(2)}, u32[]{:S(2)}) async-start(bf16[8,144,768]{2,1,0:T(8,128)(2,1)} %bitcast.129), calls=%async_computation.2 | async-start | bytes 3538944 | tf_op jit(solution)/shard_map/all_to_all | solution.py:143
  73.5 22.4 %copy-start.38 = (bf16[48,896]{1,0:T(8,128)(2,1)S(1)}, bf16[48,896]{1,0:T(8,128)(2,1)}, u32[]{:S(2)}) copy-start(bf16[48,896]{1,0:T(8,128)(2,1)} %copy-done.37) | copy-start | bytes 258052
  73.5 23.1 %copy-start.36 = (bf16[48,896]{1,0:T(8,128)(2,1)S(1)}, bf16[48,896]{1,0:T(8,128)(2,1)}, u32[]{:S(2)}) copy-start(bf16[48,896]{1,0:T(8,128)(2,1)} %copy-done.35) | copy-start | bytes 258052
  92.2 14.7 %copy-start.32 = (bf16[2,2,4,24,256]{4,3,2,0,1:T(8,128)(2,1)S(1)}, bf16[2,2,4,24,256]{4,3,2,0,1:T(8,128)(2,1)}, u32[]{:S(2)}) copy-start(bf16[2,2,4,24,256]{4,3,2,0,1:T(8,128)(2,1)} %constant_dynamic-update-slice_fusion.7) | copy-start | bytes 589828
  92.2 13.9 %collective-permute-start.7 = (bf16[2,192,512]{2,1,0:T(8,128)(2,1)S(1)}, bf16[2,192,512]{2,1,0:T(8,128)(2,1)S(1)}, u32[]{:S(2)}, u32[]{:S(2)}) collective-permute-start(bf16[2,192,512]{2,1,0:T(8,128)(2,1)S(1)} %slice.218), channel_id=1, source_target_pairs={{0,2},{1,3},{2,0},{3,1},{4,6},{5,7},{6,4},{7,5},{8,10},{9,11},{10,... | collective-permute-start | bytes 1179656 | tf_op jit(solution)/shard_map/ppermute | solution.py:82
  93.9 9.8 %collective-permute-start.9 = (bf16[4,48,896]{2,1,0:T(8,128)(2,1)S(1)}, bf16[4,48,896]{2,1,0:T(8,128)(2,1)S(1)}, u32[]{:S(2)}, u32[]{:S(2)}) collective-permute-start(bf16[4,48,896]{2,1,0:T(8,128)(2,1)S(1)} %pad_maximum_fusion.8.refs_4_), channel_id=1, source_target_pairs={{0,4},{1,5},{2,6},{3,7},{4,0},{5,1},{6,2},{7,3},{8,12},{9,13},{10,... | collective-permute-start | bytes 1032200 | tf_op jit(solution)/shard_map/ppermute | solution.py:82
  97.3 10.3 %copy-start.45 = (bf16[64,768]{1,0:T(8,128)(2,1)S(1)}, bf16[64,768]{1,0:T(8,128)(2,1)}, u32[]{:S(2)}) copy-start(bf16[64,768]{1,0:T(8,128)(2,1)} %param.25) | copy-start | bytes 294916
  104.6 9.3 %copy-start.46 = (s32[512,2]{0,1:T(2,128)S(1)}, s32[512,2]{0,1:T(2,128)}, u32[]{:S(2)}) copy-start(s32[512,2]{0,1:T(2,128)} %param.17) | copy-start | bytes 12292
  104.6 17.2 %collective-permute-start.10 = (bf16[8,48,896]{2,1,0:T(8,128)(2,1)}, bf16[8,48,896]{2,1,0:T(8,128)(2,1)S(1)}, u32[]{:S(2)}, u32[]{:S(2)}) collective-permute-start(bf16[8,48,896]{2,1,0:T(8,128)(2,1)} %constant_dynamic-update-slice_fusion), channel_id=1, source_target_pairs={{0,2},{1,3},{2,0},{3,1},{4,6},{5,7},{6,4},{7,5},{8,10},{9,11},{10,... | collective-permute-start | bytes 2064392 | tf_op jit(solution)/shard_map/ppermute | solution.py:82
  106.9 4.9 %collective-permute-start.8 = (bf16[2,192,512]{2,1,0:T(8,128)(2,1)S(1)}, bf16[2,192,512]{2,1,0:T(8,128)(2,1)S(1)}, u32[]{:S(2)}, u32[]{:S(2)}) collective-permute-start(bf16[2,192,512]{2,1,0:T(8,128)(2,1)S(1)} %pad_maximum_fusion.6), channel_id=1, source_target_pairs={{0,1},{1,0},{2,3},{3,2},{4,5},{5,4},{6,7},{7,6},{8,9},{9,8},{10,11... | collective-permute-start | bytes 1179656 | tf_op jit(solution)/shard_map/ppermute | solution.py:82
  107.0 1.8 collective-permute-start.12
  107.5 36.4 %collective-permute-start.16 = (bf16[512,768]{1,0:T(8,128)(2,1)S(1)}, bf16[512,768]{1,0:T(8,128)(2,1)}, u32[]{:S(2)}, u32[]{:S(2)}) collective-permute-start(bf16[512,768]{1,0:T(8,128)(2,1)S(1)} %copy-done.10), channel_id=1, source_target_pairs={{0,1},{1,0},{2,3},{3,2},{4,5},{5,4},{6,7},{7,6},{8,9},{9,8},{10,11... | collective-permute-start | bytes 2359304 | tf_op jit(solution)/shard_map/ppermute | solution.py:82
  108.9 19.7 %collective-permute-start.13 = (bf16[2,288,256]{2,1,0:T(8,128)(2,1)S(1)}, bf16[2,288,256]{2,1,0:T(8,128)(2,1)S(1)}, u32[]{:S(2)}, u32[]{:S(2)}) collective-permute-start(bf16[2,288,256]{2,1,0:T(8,128)(2,1)S(1)} %pad_maximum_fusion.9), channel_id=1, source_target_pairs={{0,8},{1,9},{2,10},{3,11},{4,12},{5,13},{6,14},{7,15},{8,0},{9,1},... | collective-permute-start | bytes 884744 | tf_op jit(solution)/shard_map/ppermute | solution.py:82
  111.4 23.4 %collective-permute-start.14 = (bf16[2,288,256]{2,1,0:T(8,128)(2,1)S(1)}, bf16[2,288,256]{2,1,0:T(8,128)(2,1)S(1)}, u32[]{:S(2)}, u32[]{:S(2)}) collective-permute-start(bf16[2,288,256]{2,1,0:T(8,128)(2,1)S(1)} %pad_maximum_fusion.9), channel_id=1, source_target_pairs={{0,16},{1,17},{2,18},{3,19},{4,20},{5,21},{6,22},{7,23},{8,24},{9,... | collective-permute-start | bytes 884744 | tf_op jit(solution)/shard_map/ppermute | solution.py:82
  111.8 23.1 %collective-permute-start.15 = (bf16[2,288,256]{2,1,0:T(8,128)(2,1)S(1)}, bf16[2,288,256]{2,1,0:T(8,128)(2,1)S(1)}, u32[]{:S(2)}, u32[]{:S(2)}) collective-permute-start(bf16[2,288,256]{2,1,0:T(8,128)(2,1)S(1)} %pad_maximum_fusion.9), channel_id=1, source_target_pairs={{0,24},{1,25},{2,26},{3,27},{4,28},{5,29},{6,30},{7,31},{8,16},{9,... | collective-permute-start | bytes 884744 | tf_op jit(solution)/shard_map/ppermute | solution.py:82
  135.6 31.4 %all-to-all-start.3 = ((bf16[8,80,768]{2,1,0:T(8,128)(2,1)}), bf16[8,80,768]{2,1,0:T(8,128)(2,1)S(1)}, u32[]{:S(2)}, u32[]{:S(2)}) async-start(bf16[8,80,768]{2,1,0:T(8,128)(2,1)} %bitcast.134), calls=%async_computation.3 | async-start | bytes 1966080 | tf_op jit(solution)/shard_map/all_to_all | solution.py:143
  148.8 22.7 %collective-permute-start.11 = (bf16[512,768]{1,0:T(8,128)(2,1)S(1)}, bf16[512,768]{1,0:T(8,128)(2,1)}, u32[]{:S(2)}, u32[]{:S(2)}) collective-permute-start(bf16[512,768]{1,0:T(8,128)(2,1)S(1)} %copy-done.11), channel_id=1, source_target_pairs={{0,1},{1,0},{2,3},{3,2},{4,5},{5,4},{6,7},{7,6},{8,9},{9,8},{10,11... | collective-permute-start | bytes 2359304 | tf_op jit(solution)/shard_map/ppermute | solution.py:82
  149.0 53.0 %copy-start.19 = (bf16[4,288,256]{2,1,0:T(8,128)(2,1)}, bf16[4,288,256]{2,1,0:T(8,128)(2,1)S(1)}, u32[]{:S(2)}) copy-start(bf16[4,288,256]{2,1,0:T(8,128)(2,1)S(1)} %pad_maximum_fusion.4.refs_0_) | copy-start | bytes 1769476
  149.1 53.0 %collective-permute-start.17 = (bf16[4,288,256]{2,1,0:T(8,128)(2,1)S(1)}, bf16[4,288,256]{2,1,0:T(8,128)(2,1)}, u32[]{:S(2)}, u32[]{:S(2)}) collective-permute-start(bf16[4,288,256]{2,1,0:T(8,128)(2,1)S(1)} %pad_maximum_fusion.4.refs_0_), channel_id=1, source_target_pairs={{0,4},{1,5},{2,6},{3,7},{4,0},{5,1},{6,2},{7,3},{8,12},{9,13},{10,... | collective-permute-start | bytes 1769480 | tf_op jit(solution)/shard_map/ppermute | solution.py:82
  152.0 50.0 %collective-permute-start.18 = (bf16[4,288,256]{2,1,0:T(8,128)(2,1)}, bf16[4,288,256]{2,1,0:T(8,128)(2,1)}, u32[]{:S(2)}, u32[]{:S(2)}) collective-permute-start(bf16[4,288,256]{2,1,0:T(8,128)(2,1)} %pad_maximum_fusion.5.refs_3_), channel_id=1, source_target_pairs={{0,2},{1,3},{2,0},{3,1},{4,6},{5,7},{6,4},{7,5},{8,10},{9,11},{10,... | collective-permute-start | bytes 1769480 | tf_op jit(solution)/shard_map/ppermute | solution.py:82
  167.0 27.3 %all-to-all-start.5 = ((bf16[8,64,768]{2,1,0:T(8,128)(2,1)}), bf16[8,64,768]{2,1,0:T(8,128)(2,1)S(1)}, u32[]{:S(2)}, u32[]{:S(2)}) async-start(bf16[8,64,768]{2,1,0:T(8,128)(2,1)} %bitcast.137), calls=%async_computation.5 | async-start | bytes 1572864 | tf_op jit(solution)/shard_map/all_to_all | solution.py:143
  194.3 9.9 %copy-start.9 = (bf16[8,64,768]{2,1,0:T(8,128)(2,1)}, bf16[8,64,768]{2,1,0:T(8,128)(2,1)S(1)}, u32[]{:S(2)}) copy-start(bf16[8,64,768]{2,1,0:T(8,128)(2,1)S(1)} %all-to-all-done.5) | copy-start | bytes 2359300
  194.4 31.7 %all-to-all-start.4 = ((bf16[8,80,768]{2,1,0:T(8,128)(2,1)}), bf16[8,80,768]{2,1,0:T(8,128)(2,1)S(1)}, u32[]{:S(2)}, u32[]{:S(2)}) async-start(bf16[8,80,768]{2,1,0:T(8,128)(2,1)} %bitcast.135), calls=%async_computation.4 | async-start | bytes 1966080 | tf_op jit(solution)/shard_map/all_to_all | solution.py:143
  204.2 47.4 %collective-permute-start.19 = (bf16[8,288,256]{2,1,0:T(8,128)(2,1)}, bf16[8,288,256]{2,1,0:T(8,128)(2,1)}, u32[]{:S(2)}, u32[]{:S(2)}) collective-permute-start(bf16[8,288,256]{2,1,0:T(8,128)(2,1)} %pad_maximum_fusion.1), channel_id=1, source_target_pairs={{0,2},{1,3},{2,0},{3,1},{4,6},{5,7},{6,4},{7,5},{8,10},{9,11},{10,... | collective-permute-start | bytes 3538952 | tf_op jit(solution)/shard_map/ppermute | solution.py:82
  206.0 45.6 %collective-permute-start.20 = (bf16[8,288,256]{2,1,0:T(8,128)(2,1)S(1)}, bf16[8,288,256]{2,1,0:T(8,128)(2,1)}, u32[]{:S(2)}, u32[]{:S(2)}) collective-permute-start(bf16[8,288,256]{2,1,0:T(8,128)(2,1)S(1)} %pad_maximum_fusion.2), channel_id=1, source_target_pairs={{0,4},{1,5},{2,6},{3,7},{4,0},{5,1},{6,2},{7,3},{8,12},{9,13},{10,... | collective-permute-start | bytes 3538952 | tf_op jit(solution)/shard_map/ppermute | solution.py:82
  226.1 21.0 %copy-start.7 = (bf16[8,80,768]{2,1,0:T(8,128)(2,1)}, bf16[8,80,768]{2,1,0:T(8,128)(2,1)S(1)}, u32[]{:S(2)}) copy-start(bf16[8,80,768]{2,1,0:T(8,128)(2,1)S(1)} %all-to-all-done.4) | copy-start | bytes 2949124
  247.1 36.5 %all-to-all-start.6 = ((bf16[8,80,768]{2,1,0:T(8,128)(2,1)}), bf16[8,80,768]{2,1,0:T(8,128)(2,1)S(1)}, u32[]{:S(2)}, u32[]{:S(2)}) async-start(bf16[8,80,768]{2,1,0:T(8,128)(2,1)} %get-tuple-element.150), calls=%async_computation.6 | async-start | bytes 1966080 | tf_op jit(solution)/shard_map/all_to_all | solution.py:143
  276.6 12.6 %collective-permute-start.21 = (bf16[1024,768]{1,0:T(8,128)(2,1)}, bf16[1024,768]{1,0:T(8,128)(2,1)S(1)}, u32[]{:S(2)}, u32[]{:S(2)}) collective-permute-start(bf16[1024,768]{1,0:T(8,128)(2,1)} %get-tuple-element.145), channel_id=1, source_target_pairs={{0,1},{1,0},{2,3},{3,2},{4,5},{5,4},{6,7},{7,6},{8,9},{9,8},{10,11... | collective-permute-start | bytes 4718600 | tf_op jit(solution)/shard_map/ppermute | solution.py:82
  276.6 52.6 %collective-permute-start.22 = (bf16[2,768,1024]{2,1,0:T(8,128)(2,1)}, bf16[2,768,1024]{2,1,0:T(8,128)(2,1)}, u32[]{:S(2)}, u32[]{:S(2)}) collective-permute-start(bf16[2,768,1024]{2,1,0:T(8,128)(2,1)} %get-tuple-element.159), channel_id=1, source_target_pairs={{0,1},{1,0},{2,3},{3,2},{4,5},{5,4},{6,7},{7,6},{8,9},{9,8},{10,11... | collective-permute-start | bytes 9437192 | tf_op jit(solution)/shard_map/ppermute | solution.py:82
  277.1 29.6 %collective-permute-start.24 = (bf16[8,288,256]{2,1,0:T(8,128)(2,1)}, bf16[8,288,256]{2,1,0:T(8,128)(2,1)}, u32[]{:S(2)}, u32[]{:S(2)}) collective-permute-start(bf16[8,288,256]{2,1,0:T(8,128)(2,1)} %get-tuple-element.163), channel_id=1, source_target_pairs={{0,2},{1,3},{2,0},{3,1},{4,6},{5,7},{6,4},{7,5},{8,10},{9,11},{10,... | collective-permute-start | bytes 3538952 | tf_op jit(solution)/shard_map/ppermute | solution.py:82
  278.7 43.4 %collective-permute-start.25 = (bf16[8,288,256]{2,1,0:T(8,128)(2,1)}, bf16[8,288,256]{2,1,0:T(8,128)(2,1)}, u32[]{:S(2)}, u32[]{:S(2)}) collective-permute-start(bf16[8,288,256]{2,1,0:T(8,128)(2,1)} %get-tuple-element.164), channel_id=1, source_target_pairs={{0,4},{1,5},{2,6},{3,7},{4,0},{5,1},{6,2},{7,3},{8,12},{9,13},{10,... | collective-permute-start | bytes 3538952 | tf_op jit(solution)/shard_map/ppermute | solution.py:82
  280.7 45.5 %collective-permute-start.23 = (bf16[2,512,768]{2,1,0:T(8,128)(2,1)}, bf16[2,512,768]{2,1,0:T(8,128)(2,1)}, u32[]{:S(2)}, u32[]{:S(2)}) collective-permute-start(bf16[2,512,768]{2,1,0:T(8,128)(2,1)} %get-tuple-element.161), channel_id=1, source_target_pairs={{0,1},{1,0},{2,3},{3,2},{4,5},{5,4},{6,7},{7,6},{8,9},{9,8},{10,11... | collective-permute-start | bytes 4718600 | tf_op jit(solution)/shard_map/ppermute | solution.py:82
  284.5 63.4 %all-to-all-start.7 = ((bf16[8,144,768]{2,1,0:T(8,128)(2,1)}), bf16[8,144,768]{2,1,0:T(8,128)(2,1)S(1)}, u32[]{:S(2)}, u32[]{:S(2)}) async-start(bf16[8,144,768]{2,1,0:T(8,128)(2,1)} %pad_maximum_fusion), calls=%async_computation.7 | async-start | bytes 3538944 | tf_op jit(solution)/shard_map/all_to_all | solution.py:143
  304.1 18.0 %copy-start.26 = (bf16[8,288,256]{2,1,0:T(8,128)(2,1)S(1)}, bf16[8,288,256]{2,1,0:T(8,128)(2,1)}, u32[]{:S(2)}) copy-start(bf16[8,288,256]{2,1,0:T(8,128)(2,1)} %get-tuple-element.162) | copy-start | bytes 3538948
  305.2 18.2 %collective-permute-start.26 = (bf16[2,192,512]{2,1,0:T(8,128)(2,1)S(1)}, bf16[2,192,512]{2,1,0:T(8,128)(2,1)S(1)}, u32[]{:S(2)}, u32[]{:S(2)}) collective-permute-start(bf16[2,192,512]{2,1,0:T(8,128)(2,1)S(1)} %slice.245), channel_id=1, source_target_pairs={{0,2},{1,3},{2,0},{3,1},{4,6},{5,7},{6,4},{7,5},{8,10},{9,11},{10,... | collective-permute-start | bytes 1179656 | tf_op jit(solution)/shard_map/ppermute | solution.py:82
  323.4 21.8 %collective-permute-start.28 = (bf16[4,288,256]{2,1,0:T(8,128)(2,1)S(1)}, bf16[4,288,256]{2,1,0:T(8,128)(2,1)S(1)}, u32[]{:S(2)}, u32[]{:S(2)}) collective-permute-start(bf16[4,288,256]{2,1,0:T(8,128)(2,1)S(1)} %add_convert_fusion.6), channel_id=1, source_target_pairs={{0,4},{1,5},{2,6},{3,7},{4,0},{5,1},{6,2},{7,3},{8,12},{9,13},{10,... | collective-permute-start | bytes 1769480 | tf_op jit(solution)/shard_map/ppermute | solution.py:82
  324.2 4.2 collective-permute-start.27
  325.7 19.5 %collective-permute-start.29 = (bf16[4,288,256]{2,1,0:T(8,128)(2,1)S(1)}, bf16[4,288,256]{2,1,0:T(8,128)(2,1)S(1)}, u32[]{:S(2)}, u32[]{:S(2)}) collective-permute-start(bf16[4,288,256]{2,1,0:T(8,128)(2,1)S(1)} %add_convert_fusion.5), channel_id=1, source_target_pairs={{0,2},{1,3},{2,0},{3,1},{4,6},{5,7},{6,4},{7,5},{8,10},{9,11},{10,... | collective-permute-start | bytes 1769480 | tf_op jit(solution)/shard_map/ppermute | solution.py:82
  349.6 36.9 %all-to-all-start.8 = ((bf16[4,2,288,256]{3,2,1,0:T(8,128)(2,1)}), bf16[4,2,288,256]{3,2,1,0:T(8,128)(2,1)S(1)}, u32[]{:S(2)}, u32[]{:S(2)}) async-start(bf16[4,2,288,256]{3,2,1,0:T(8,128)(2,1)} %copy.214), calls=%async_computation.8 | async-start | bytes 2359296 | tf_op jit(solution)/shard_map/all_to_all | solution.py:106
  357.4 29.3 %collective-permute-start.30 = (bf16[512,768]{1,0:T(8,128)(2,1)S(1)}, bf16[512,768]{1,0:T(8,128)(2,1)}, u32[]{:S(2)}, u32[]{:S(2)}) collective-permute-start(bf16[512,768]{1,0:T(8,128)(2,1)S(1)} %copy-done.30), channel_id=1, source_target_pairs={{0,2},{1,3},{2,0},{3,1},{4,6},{5,7},{6,4},{7,5},{8,10},{9,11},{10,... | collective-permute-start | bytes 2359304 | tf_op jit(solution)/shard_map/ppermute | solution.py:82
  359.0 54.3 %collective-permute-start.32 = (bf16[768,1024]{1,0:T(8,128)(2,1)}, bf16[768,1024]{1,0:T(8,128)(2,1)}, u32[]{:S(2)}, u32[]{:S(2)}) collective-permute-start(bf16[768,1024]{1,0:T(8,128)(2,1)} %fusion.4), channel_id=1, source_target_pairs={{0,2},{1,3},{2,0},{3,1},{4,6},{5,7},{6,4},{7,5},{8,10},{9,11},{10,... | collective-permute-start | bytes 4718600 | tf_op jit(solution)/shard_map/ppermute | solution.py:82
  359.4 12.5 %copy-start.23 = (bf16[768,896]{1,0:T(8,128)(2,1)S(1)}, bf16[768,896]{1,0:T(8,128)(2,1)}, u32[]{:S(2)}) copy-start(bf16[768,896]{1,0:T(8,128)(2,1)} %get-tuple-element.176) | copy-start | bytes 4128772
  373.9 28.4 %collective-permute-start.34 = (bf16[8,2,24,896]{3,2,0,1:T(8,128)(2,1)}, bf16[8,2,24,896]{3,2,0,1:T(8,128)(2,1)}, u32[]{:S(2)}, u32[]{:S(2)}) collective-permute-start(bf16[8,2,24,896]{3,2,0,1:T(8,128)(2,1)} %bitcast.116), channel_id=1, source_target_pairs={{0,1},{1,0},{2,3},{3,2},{4,5},{5,4},{6,7},{7,6},{8,9},{9,8},{10,11... | collective-permute-start | bytes 2064392 | tf_op jit(solution)/shard_map/ppermute | solution.py:82
  386.7 12.9 %copy-start.21 = (bf16[2,512,768]{2,1,0:T(8,128)(2,1)S(1)}, bf16[2,512,768]{2,1,0:T(8,128)(2,1)}, u32[]{:S(2)}) copy-start(bf16[2,512,768]{2,1,0:T(8,128)(2,1)} %get-tuple-element.160) | copy-start | bytes 4718596
  386.7 13.9 %copy-start.13 = (bf16[2,768,1024]{2,1,0:T(8,128)(2,1)S(1)}, bf16[2,768,1024]{2,1,0:T(8,128)(2,1)}, u32[]{:S(2)}) copy-start(bf16[2,768,1024]{2,1,0:T(8,128)(2,1)} %get-tuple-element.158) | copy-start | bytes 9437188
  399.0 14.3 %collective-permute-start.31 = (bf16[2,512,768]{2,1,0:T(8,128)(2,1)}, bf16[2,512,768]{2,1,0:T(8,128)(2,1)}, u32[]{:S(2)}, u32[]{:S(2)}) collective-permute-start(bf16[2,512,768]{2,1,0:T(8,128)(2,1)} %get-tuple-element.180), channel_id=1, source_target_pairs={{0,1},{1,0},{2,3},{3,2},{4,5},{5,4},{6,7},{7,6},{8,9},{9,8},{10,11... | collective-permute-start | bytes 4718600 | tf_op jit(solution)/shard_map/ppermute | solution.py:82
  404.6 17.1 %collective-permute-start.35 = (bf16[8,24,896]{2,1,0:T(8,128)(2,1)}, bf16[8,24,896]{2,1,0:T(8,128)(2,1)}, u32[]{:S(2)}, u32[]{:S(2)}) collective-permute-start(bf16[8,24,896]{2,1,0:T(8,128)(2,1)} %dynamic-slice_bitcast_fusion), channel_id=1, source_target_pairs={{0,2},{1,3},{2,0},{3,1},{4,6},{5,7},{6,4},{7,5},{8,10},{9,11},{10,... | collective-permute-start | bytes 1032200 | tf_op jit(solution)/shard_map/ppermute | solution.py:82
  407.8 33.1 %all-to-all-start.9 = ((bf16[32,24,640]{2,1,0:T(8,128)(2,1)}), bf16[32,24,640]{2,1,0:T(8,128)(2,1)}, u32[]{:S(2)}, u32[]{:S(2)}) async-start(bf16[32,24,640]{2,1,0:T(8,128)(2,1)} %bitcast.133), calls=%async_computation.9 | async-start | bytes 1966080 | tf_op jit(solution)/shard_map/all_to_all | solution.py:143
  415.8 38.6 %collective-permute-start.33 = (bf16[512,768]{1,0:T(8,128)(2,1)}, bf16[512,768]{1,0:T(8,128)(2,1)}, u32[]{:S(2)}, u32[]{:S(2)}) collective-permute-start(bf16[512,768]{1,0:T(8,128)(2,1)} %fusion.11), channel_id=1, source_target_pairs={{0,2},{1,3},{2,0},{3,1},{4,6},{5,7},{6,4},{7,5},{8,10},{9,11},{10,... | collective-permute-start | bytes 2359304 | tf_op jit(solution)/shard_map/ppermute | solution.py:82
  421.7 18.2 %collective-permute-start.36 = (f32[2,4,24,256]{3,2,1,0:T(8,128)S(1)}, f32[2,4,24,256]{3,2,1,0:T(8,128)}, u32[]{:S(2)}, u32[]{:S(2)}) collective-permute-start(f32[2,4,24,256]{3,2,1,0:T(8,128)S(1)} %get-tuple-element.294), channel_id=1, source_target_pairs={{0,1},{1,0},{2,3},{3,2},{4,5},{5,4},{6,7},{7,6},{8,9},{9,8},{10,11... | collective-permute-start | bytes 589832 | tf_op jit(solution)/shard_map/ppermute | solution.py:82
  441.0 19.1 %all-to-all-start.10 = ((bf16[8,24,896]{2,1,0:T(8,128)(2,1)}), bf16[8,24,896]{2,1,0:T(8,128)(2,1)S(1)}, u32[]{:S(2)}, u32[]{:S(2)}) async-start(bf16[8,24,896]{2,1,0:T(8,128)(2,1)} %fusion.13), calls=%async_computation.10 | async-start | bytes 688128 | tf_op jit(solution)/shard_map/all_to_all | solution.py:143
  (35 other events, 133.1 us)

commit v4 on v3

--- a/solution.py
+++ b/solution.py
@@ -1280,7 +1280,7 @@
         wa, wb = add_up([ka[4:], ca[4:]]).astype(BF16), add_up([kb[4:], cb[4:]]).astype(BF16)
         ea, eb = flip(wa, "y"), flip(wb, "x")
         dctxs[0] = after(dctxs[0], in_far, out_far, wa, wb)
-    came = swap(after(jnp.concatenate(eos, axis=1), backs[-1]), "dp").reshape(-1, width)
+    came = swap(after(jnp.concatenate(eos, axis=1), dctxs[2]), "dp").reshape(-1, width)
     d_heads = []
     for head in range(columns // 192):
         held = after(heads, *d_heads) if d_heads else heads
@@ -1297,7 +1297,7 @@
         ea, eb = together((ea, eb), d_heads[0])
         wa, wb = add_up([ka[:4], ca[:4], ea]).astype(BF16), add_up([kb[:4], cb[:4], eb]).astype(BF16)
         sums = z_sum(after(jnp.stack([wa, wb], axis=1), came))
-        d_heads[0] = after(d_heads[0], sums, out_terms[2])
+        d_heads[0] = after(d_heads[0], out_terms[2])
     dxn_kept, dxn_away, grad_heads = qkv_back(seq, token_blocks, d_heads, w_heads, cosine, sine)
     if small:
         dxn_away = after(flip(dxn_away, "c"), in_terms[2])

time: 469 us -> 532 us (1.13)
  waiting for transfers between devices: 74.1 us -> 137 us
  starting transfers between devices: 94.7 us -> 103 us
    ppermute x37, waiting for transfers between devices: 42.8 us -> 79.5 us  [flip(): return lax.ppermute(block, AXES, FLIP[name])]
    all_to_all x10, waiting for transfers between devices: 31.3 us -> 53.9 us  [swap(): return lax.all_to_all(blocks, axis, split_axis=0, concat_axis=0, tiled=True)]
    all_to_all x10, starting transfers between devices: 54.4 us -> 61.5 us  [swap(): return lax.all_to_all(blocks, axis, split_axis=0, concat_axis=0, tiled=True)]
    unnamed x115 -> x127, local copies, waits for them, and re-layouts: 13.3 us -> 12.2 us
  transfers between devices with their start and end apart: 48 -> 48, of which waited for: 11 -> 18; matrix products, arithmetic and copies ran while one was open for 20% -> 17% of each run, Pallas kernels for 41% -> 29%
where the time goes in v4:
time: 532 us; the launch traced here: 530 us
  Pallas kernels  192 us (36%)
  waiting for transfers between devices  137 us (26%)
  starting transfers between devices  103 us (19%)
  local copies, waits for them, and re-layouts  54.4 us (10%)
  other arithmetic  39 us (7%)
    ppermute x37, waiting for transfers between devices, flip(): return lax.ppermute(block, AXES, FLIP[name])  79.5 us
    all_to_all x10, starting transfers between devices, swap(): return lax.all_to_all(blocks, axis, split_axis=0, concat_axis=0, tiled=True)  61.5 us
    all_to_all x10, waiting for transfers between devices, swap(): return lax.all_to_all(blocks, axis, split_axis=0, concat_axis=0, tiled=True)  53.9 us
    pallas_call x2, Pallas kernels, expert(): pl.pallas_call(functools.partial(expert_kernel, low=low), grid_spec=pltpu...  38.7 us
    pallas_call x3, Pallas kernels, attend_back(): pl.pallas_call(attend_back_kernel, grid_spec=pltpu.PrefetchScalarGridSpec...  37.9 us
    ppermute x37, starting transfers between devices, flip(): return lax.ppermute(block, AXES, FLIP[name])  37.2 us
    pallas_call x1, Pallas kernels, paired(): pl.pallas_call(paired_kernel, grid_spec=pltpu.PrefetchScalarGridSpec(num_...  25.3 us
    pallas_call x1, Pallas kernels, expert_grads(): pl.pallas_call(expert_grads_kernel, grid_spec=pltpu.PrefetchScalarGridSpe...  21 us
  transfers between devices with their start and end apart: 48, of which 18 were waited for; matrix products, arithmetic and copies ran while one was open for 17% of the time, Pallas kernels for 29%

profile of v4, /device:TPU:0, one launch (start us, length us, event | category | flops | bytes accessed | tf_op | source)
XLA Modules:
  0.0 530.2 jit_solution(6913357301290606386)
XLA Ops:
  3.8 3.9 all-to-all-start
  14.6 6.4 %all-to-all-start.1 = ((bf16[8,96,640]{2,1,0:T(8,128)(2,1)}), bf16[8,96,640]{2,1,0:T(8,128)(2,1)S(1)}, u32[]{:S(2)}, u32[]{:S(2)}) async-start(bf16[8,96,640]{2,1,0:T(8,128)(2,1)} %maximum_maximum_fusion), calls=%async_computation.1 | async-start | bytes 1966080 | tf_op jit(solution)/shard_map/all_to_all | solution.py:143
  22.9 2.4 convolution_convert_fusion
  25.3 1.8 collective-permute-start.1
  29.5 16.6 %all-to-all-done.1 = bf16[8,96,640]{2,1,0:T(8,128)(2,1)S(1)} async-done(((bf16[8,96,640]{2,1,0:T(8,128)(2,1)}), bf16[8,96,640]{2,1,0:T(8,128)(2,1)S(1)}, u32[]{:S(2)}, u32[]{:S(2)}) %all-to-all-start.1) | async-done | bytes 983072 | tf_op jit(solution)/shard_map/all_to_all | solution.py:143
  46.1 2.1 collective-permute-start.6
  48.1 2.3 collective-permute-start.4
  50.5 2.3 collective-permute-done.6
  52.8 2.6 collective-permute-done.5
  56.2 4.7 all-to-all-start.2
  63.0 1.8 multiply_sine_fusion
  64.8 8.5 %qkv_project.1 = (bf16[4,576,512]{2,1,0:T(8,128)(2,1)}, bf16[768,640]{1,0:T(8,128)(2,1)}) custom-call(s32[1]{0:T(128)} %bitcast.1.seq_ref, s32[1]{0:T(128)} %bitcast.2.dp_ref.own_ref, bf16[512,768]{1,0:T(8,128)(2,1)} %x_ref.1, bf16[512,768]{1,0:T(8,128)(2,1)} %collective-permute-done.refs_1_, bf16[512,768]{1,0:T(8,128)(2,1)} %collective-permute-done.1.refs_2_, ...), custom_call_target="tpu_custom_call" | custom-call | flops 1000000000 | bytes 1048576 | tf_op jit(solution)/shard_map/qkv_project/pallas_call | solution.py:207
  73.9 17.6 %attend.1 = (bf16[4,192,512]{2,1,0:T(8,128)(2,1)}, f32[3,1,2048]{2,1,0:T(1,128)}) custom-call(s32[1]{0:T(128)} %bitcast.1.seq_ref, bf16[4,576,512]{2,1,0:T(8,128)(2,1)} %get-tuple-element.175.buf_ref, s32[1,2048]{1,0:T(1,128)} %docs_ref.7), custom_call_target="tpu_custom_call" | custom-call | flops 3000000000 | bytes 1048576 | tf_op jit(solution)/shard_map/attend/pallas_call | solution.py:290
  92.6 1.7 collective-permute-start.7
  94.3 2.0 collective-permute-start.9
  99.3 4.8 collective-permute-done.9.refs_5_
  109.7 2.6 collective-permute-start.13
  112.6 2.1 collective-permute-start.15
  115.6 1.8 fusion.37
  117.4 4.4 collective-permute-done.10.refs_6_
  121.8 5.9 %middle.1 = (f32[512,768]{1,0:T(8,128)}, bf16[512,768]{1,0:T(8,128)(2,1)}, f32[512,128]{1,0:T(8,128)}, bf16[768,768]{1,0:T(8,128)(2,1)}, bf16[768,128]{1,0:T(8,1...) custom-call(s32[1]{0:T(128)} %bitcast.me_ref, s32[1]{0:T(128)} %bitcast.1.seq_ref, ...), custom_call_target="tpu_custom_call" | custom-call | flops 500000000 | bytes 1048576 | tf_op jit(solution)/shard_map/middle/pallas_call | solution.py:451
  127.7 8.0 %collective-permute-done.14 = bf16[2,288,256]{2,1,0:T(8,128)(2,1)S(1)} collective-permute-done((bf16[2,288,256]{2,1,0:T(8,128)(2,1)S(1)}, bf16[2,288,256]{2,1,0:T(8,128)(2,1)S(1)}, u32[]{:S(2)}, u32[]{:S(2)}) %collective-permute-start.14) | collective-permute-done | bytes 294944 | tf_op jit(solution)/shard_map/ppermute | solution.py:82
  136.4 18.1 %all-to-all-start.3 = ((bf16[8,80,768]{2,1,0:T(8,128)(2,1)}), bf16[8,80,768]{2,1,0:T(8,128)(2,1)S(1)}, u32[]{:S(2)}, u32[]{:S(2)}) async-start(bf16[8,80,768]{2,1,0:T(8,128)(2,1)} %bitcast.134), calls=%async_computation.3 | async-start | bytes 1966080 | tf_op jit(solution)/shard_map/all_to_all | solution.py:143
  155.5 2.2 constant_dynamic-update-slice_fusion.9.dy_ref
  162.4 2.0 collective-permute-start.17
  166.1 12.5 %all-to-all-done.3 = bf16[8,80,768]{2,1,0:T(8,128)(2,1)S(1)} async-done(((bf16[8,80,768]{2,1,0:T(8,128)(2,1)}), bf16[8,80,768]{2,1,0:T(8,128)(2,1)S(1)}, u32[]{:S(2)}, u32[]{:S(2)}) %all-to-all-start.3) | async-done | bytes 983072 | tf_op jit(solution)/shard_map/all_to_all | solution.py:143
  178.6 3.5 all-to-all-start.5
  183.1 2.1 constant_dynamic-update-slice_fusion.5.x_ref
  185.2 20.8 %expert.2 = (bf16[640,768]{1,0:T(8,128)(2,1)}, bf16[640,768]{1,0:T(8,128)(2,1)}, f32[640,1]{1,0:T(8,128)}, bf16[640,768]{1,0:T(8,128)(2,1)}, bf16[640,2048]{1,0:...) custom-call(s32[1]{0:T(128)} %bitcast.2.dp_ref.own_ref, bf16[640,768]{1,0:T(8,128)(2,1)} %bitcast.125, ...), custom_call_target="tpu_custom_call" | custom-call | flops 12079595520 | bytes 41943040 | tf_op jit(solution)/shard_map/expert/pallas_call | solution.py:701
  206.0 5.9 %all-to-all-start.4 = ((bf16[8,80,768]{2,1,0:T(8,128)(2,1)}), bf16[8,80,768]{2,1,0:T(8,128)(2,1)S(1)}, u32[]{:S(2)}, u32[]{:S(2)}) async-start(bf16[8,80,768]{2,1,0:T(8,128)(2,1)} %bitcast.135), calls=%async_computation.4 | async-start | bytes 1966080 | tf_op jit(solution)/shard_map/all_to_all | solution.py:143
  216.2 2.1 collective-permute-start.20
  218.3 17.9 %expert.3 = (bf16[512,768]{1,0:T(8,128)(2,1)}, bf16[8,80,768]{2,1,0:T(8,128)(2,1)}, f32[512,1]{1,0:T(8,128)}, bf16[512,768]{1,0:T(8,128)(2,1)}, bf16[512,2048]{1...) custom-call(s32[1]{0:T(128)} %bitcast.2.dp_ref.own_ref, bf16[512,768]{1,0:T(8,128)(2,1)} %bitcast.128, ...), custom_call_target="tpu_custom_call" | custom-call | flops 9663676416 | bytes 41943040 | tf_op jit(solution)/shard_map/expert/pallas_call | solution.py:701
  236.2 21.0 %expert_grads.1 = (bf16[2,768,1024]{2,1,0:T(8,128)(2,1)}, bf16[2,768,1024]{2,1,0:T(8,128)(2,1)}, bf16[2,512,768]{2,1,0:T(8,128)(2,1)}, bf16[2,512,768]{2,1,0:T(8,128)(2,1)}) custom-call(s32[1]{0:T(128)} %bitcast.1.seq_ref, bf16[640,768]{1,0:T(8,128)(2,1)} %bitcast.126, bf16[640,768]{1,0:T(8,128)(2,1)} %get-tuple-element.127.refs_1_, ...), custom_call_target="tpu_custom_call" | custom-call | flops 3623878656 | bytes 4194304 | tf_op jit(solution)/shard_map/expert_grads/pallas_call | solution.py:807
  257.2 4.6 all-to-all-start.6
  261.7 25.3 %dense_pair.1 = (f32[512,768]{1,0:T(8,128)}, f32[512,768]{1,0:T(8,128)}, bf16[1024,768]{1,0:T(8,128)(2,1)}, bf16[8,288,256]{2,1,0:T(8,128)(2,1)}, bf16[8,288,256...) custom-call(s32[1]{0:T(128)} %bitcast.me_ref, ...), custom_call_target="tpu_custom_call" | custom-call | flops 14495514624 | bytes 31457280 | tf_op jit(solution)/shard_map/dense_pair/pallas_call | solution.py:595
  289.2 2.0 collective-permute-start.26
  293.6 13.7 %middle_back.1 = (f32[512,768]{1,0:T(8,128)}, bf16[4,192,512]{2,1,0:T(8,128)(2,1)}, bf16[768,896]{1,0:T(8,128)(2,1)}) custom-call(f32[512,768]{1,0:T(8,128)} %get-tuple-element.149.dhn_ref, bf16[1024,768]{1,0:T(8,128)(2,1)} %copy-done.2, s32[512,2]{1,0:T(8,128)} %copy-done.6, s32[512,2]{1,0:T(8,128)} %copy.204.refs_9_.routes_ref, ...), custom_call_target="tpu_custom_call" | custom-call | flops 3000000000 | bytes 16777216 | tf_op jit(solution)/shard_map/middle_back/pallas_call | solution.py:900
  310.9 5.8 %collective-permute-done.25 = bf16[8,288,256]{2,1,0:T(8,128)(2,1)} collective-permute-done((bf16[8,288,256]{2,1,0:T(8,128)(2,1)}, bf16[8,288,256]{2,1,0:T(8,128)(2,1)}, u32[]{:S(2)}, u32[]{:S(2)}) %collective-permute-start.25) | collective-permute-done | bytes 1179680 | tf_op jit(solution)/shard_map/ppermute | solution.py:82
  319.7 5.4 %collective-permute-done.22 = bf16[2,192,512]{2,1,0:T(8,128)(2,1)S(1)} collective-permute-done((bf16[2,192,512]{2,1,0:T(8,128)(2,1)S(1)}, bf16[2,192,512]{2,1,0:T(8,128)(2,1)S(1)}, u32[]{:S(2)}, u32[]{:S(2)}) %collective-permute-start.22) | collective-permute-done | bytes 393248 | tf_op jit(solution)/shard_map/ppermute | solution.py:82
  325.9 2.2 add_convert_fusion.6
  328.1 2.0 add_convert_fusion.5
  330.9 3.3 fusion.4
  334.2 12.6 %attend_back.3.refs_4_ = bf16[4,192,512]{2,1,0:T(8,128)(2,1)} custom-call(s32[1]{0:T(128)} %bitcast.1.seq_ref, bf16[4,576,512]{2,1,0:T(8,128)(2,1)} %get-tuple-element.175.buf_ref, bf16[4,192,512]{2,1,0:T(8,128)(2,1)} %get-tuple-element.168.d0_ref, bf16[1,192,512]{2,1,0:T(8,128)(2,1)} %get-tuple-element.296.d1_ref, ...), custom_call_target="tpu_custom_call" | custom-call | flops 4000000000 | bytes 1048576 | tf_op jit(solution)/shard_map/attend_back/pallas_call | solution.py:368
  346.8 12.9 %attend_back.4.refs_5_ = bf16[4,192,512]{2,1,0:T(8,128)(2,1)} custom-call(s32[1]{0:T(128)} %bitcast.1.seq_ref, bf16[4,576,512]{2,1,0:T(8,128)(2,1)} %get-tuple-element.175.buf_ref, bf16[4,192,512]{2,1,0:T(8,128)(2,1)} %get-tuple-element.168.d0_ref, bf16[1,192,512]{2,1,0:T(8,128)(2,1)} %get-tuple-element.296.d1_ref, ...), custom_call_target="tpu_custom_call" | custom-call | flops 4000000000 | bytes 1048576 | tf_op jit(solution)/shard_map/attend_back/pallas_call | solution.py:368
  359.7 12.4 %attend_back.5.refs_6_ = bf16[4,192,512]{2,1,0:T(8,128)(2,1)} custom-call(s32[1]{0:T(128)} %bitcast.1.seq_ref, bf16[4,576,512]{2,1,0:T(8,128)(2,1)} %get-tuple-element.175.buf_ref, bf16[4,192,512]{2,1,0:T(8,128)(2,1)} %get-tuple-element.168.d0_ref, bf16[1,192,512]{2,1,0:T(8,128)(2,1)} %get-tuple-element.296.d1_ref, ...), custom_call_target="tpu_custom_call" | custom-call | flops 4000000000 | bytes 1048576 | tf_op jit(solution)/shard_map/attend_back/pallas_call | solution.py:368
  372.1 12.5 %qkv_back.1 = (bf16[2,512,768]{2,1,0:T(8,128)(2,1)}, bf16[2,512,768]{2,1,0:T(8,128)(2,1)}, bf16[768,640]{1,0:T(8,128)(2,1)}) custom-call(s32[1]{0:T(128)} %bitcast.1.seq_ref, bf16[512,768]{1,0:T(8,128)(2,1)} %x_ref.1, bf16[512,768]{1,0:T(8,128)(2,1)} %collective-permute-done.refs_1_, bf16[512,768]{1,0:T(8,128)(2,1)} %collective-permute-done.1.refs_2_, ...), custom_call_target="tpu_custom_call" | custom-call | flops 12000000000 | bytes 12582912 | tf_op jit(solution)/shard_map/qkv_back/pallas_call | solution.py:1009
  384.6 6.2 %all-to-all-start.8 = ((bf16[32,24,640]{2,1,0:T(8,128)(2,1)}), bf16[32,24,640]{2,1,0:T(8,128)(2,1)S(1)}, u32[]{:S(2)}, u32[]{:S(2)}) async-start(bf16[32,24,640]{2,1,0:T(8,128)(2,1)} %bitcast.136), calls=%async_computation.8 | async-start | bytes 1966080 | tf_op jit(solution)/shard_map/all_to_all | solution.py:143
  392.2 23.4 %all-to-all-done.8 = bf16[32,24,640]{2,1,0:T(8,128)(2,1)S(1)} async-done(((bf16[32,24,640]{2,1,0:T(8,128)(2,1)}), bf16[32,24,640]{2,1,0:T(8,128)(2,1)S(1)}, u32[]{:S(2)}, u32[]{:S(2)}) %all-to-all-start.8) | async-done | bytes 983072 | tf_op jit(solution)/shard_map/all_to_all | solution.py:143
  416.6 3.7 all-to-all-start.7
  420.3 2.2 slice_bitcast_fusion.2
  422.5 2.0 collective-permute-start.34
  429.1 25.4 %collective-permute-done.34 = bf16[4,288,256]{2,1,0:T(8,128)(2,1)S(1)} collective-permute-done((bf16[4,288,256]{2,1,0:T(8,128)(2,1)}, bf16[4,288,256]{2,1,0:T(8,128)(2,1)S(1)}, u32[]{:S(2)}, u32[]{:S(2)}) %collective-permute-start.34) | collective-permute-done | bytes 589856 | tf_op jit(solution)/shard_map/ppermute | solution.py:82
  454.5 2.1 fusion.15
  458.3 2.1 fusion.14
  460.5 14.3 %collective-permute-done.30 = bf16[768,1024]{1,0:T(8,128)(2,1)S(1)} collective-permute-done((bf16[768,1024]{1,0:T(8,128)(2,1)}, bf16[768,1024]{1,0:T(8,128)(2,1)S(1)}, u32[]{:S(2)}, u32[]{:S(2)}) %collective-permute-start.30) | collective-permute-done | bytes 1572896 | tf_op jit(solution)/shard_map/ppermute | solution.py:82
  476.1 4.2 collective-permute-done.33
  481.1 4.6 all-to-all-start.9
  488.4 2.7 slice_bitcast_fusion
  494.9 4.0 all-to-all-start.10
  498.9 3.2 add_bitcast_fusion.1
  502.1 2.7 add_bitcast_fusion
  508.0 6.3 %output_of.1 = f32[512,768]{1,0:T(8,128)} custom-call(f32[512,768]{1,0:T(8,128)} %get-tuple-element.112.hidden_ref, f32[512,768]{1,0:T(8,128)} %get-tuple-element.144.dense_ref, bf16[1024,768]{1,0:T(8,128)(2,1)} %copy-done.2, s32[512,2]{1,0:T(8,128)} %copy-done.5, f32[512,128]{1,0:T(8,128)} %get-tuple-element.146.gates_ref, bf16[1152,768]{1,0:T(8,128)(2,1)} %bitcast.120), custom_call_target="tpu_custom_call" | custom-call | flops 2000000000 | bytes 8388608 | tf_op jit(solution)/shard_map/output_of/pallas_call | solution.py:934
  514.3 4.6 input_back.1
  521.3 4.0 all-to-all-done.10
  (298 shorter events, 81.6 us)
Async XLA Ops:
  0.7 64.1 %collective-permute-start = (bf16[512,768]{1,0:T(8,128)(2,1)}, bf16[512,768]{1,0:T(8,128)(2,1)}, u32[]{:S(2)}, u32[]{:S(2)}) collective-permute-start(bf16[512,768]{1,0:T(8,128)(2,1)} %x_ref.1), channel_id=1, source_target_pairs={{0,1},{1,0},{2,3},{3,2},{4,5},{5,4},{6,7},{7,6},{8,9},{9,8},{10,11... | collective-permute-start | bytes 2359304 | tf_op jit(solution)/shard_map/ppermute | solution.py:82
  3.8 9.4 %all-to-all-start = ((bf16[4,24,640]{2,1,0:T(8,128)(2,1)}), bf16[4,24,640]{2,1,0:T(8,128)(2,1)S(1)}, u32[]{:S(2)}, u32[]{:S(2)}) async-start(bf16[4,24,640]{2,1,0:T(8,128)(2,1)} %copy.194), calls=%async_computation | async-start | bytes 245760 | tf_op jit(solution)/shard_map/all_to_all | solution.py:143
  10.6 11.9 %copy-start.6 = (s32[512,2]{1,0:T(8,128)}, s32[512,2]{1,0:T(8,128)S(1)}, u32[]{:S(2)}) copy-start(s32[512,2]{1,0:T(8,128)S(1)} %get-tuple-element.311.slots_ref) | copy-start | bytes 12292
  14.6 31.4 %all-to-all-start.1 = ((bf16[8,96,640]{2,1,0:T(8,128)(2,1)}), bf16[8,96,640]{2,1,0:T(8,128)(2,1)S(1)}, u32[]{:S(2)}, u32[]{:S(2)}) async-start(bf16[8,96,640]{2,1,0:T(8,128)(2,1)} %maximum_maximum_fusion), calls=%async_computation.1 | async-start | bytes 1966080 | tf_op jit(solution)/shard_map/all_to_all | solution.py:143
  21.2 8.2 %collective-permute-start.3 = (bf16[24,896]{1,0:T(8,128)(2,1)S(1)}, bf16[24,896]{1,0:T(8,128)(2,1)S(1)}, u32[]{:S(2)}, u32[]{:S(2)}) collective-permute-start(bf16[24,896]{1,0:T(8,128)(2,1)S(1)} %get-tuple-element.318), channel_id=1, source_target_pairs={{0,1},{1,0},{2,3},{3,2},{4,5},{5,4},{6,7},{7,6},{8,9},{9,8},{10,11... | collective-permute-start | bytes 129032 | tf_op jit(solution)/shard_map/ppermute | solution.py:82
  25.3 25.1 %collective-permute-start.1 = (bf16[512,768]{1,0:T(8,128)(2,1)S(1)}, bf16[512,768]{1,0:T(8,128)(2,1)}, u32[]{:S(2)}, u32[]{:S(2)}) collective-permute-start(bf16[512,768]{1,0:T(8,128)(2,1)S(1)} %copy-done.1), channel_id=1, source_target_pairs={{0,2},{1,3},{2,0},{3,1},{4,6},{5,7},{6,4},{7,5},{8,10},{9,11},{10,... | collective-permute-start | bytes 2359304 | tf_op jit(solution)/shard_map/ppermute | solution.py:82
  29.4 26.7 %copy-start.38 = (bf16[2,24,896]{2,1,0:T(8,128)(2,1)}, bf16[2,24,896]{2,1,0:T(8,128)(2,1)S(1)}, u32[]{:S(2)}) copy-start(bf16[2,24,896]{2,1,0:T(8,128)(2,1)S(1)} %maximum_select_fusion.2) | copy-start | bytes 258052
  46.1 10.1 %copy-start.4 = (bf16[8,96,640]{2,1,0:T(8,128)(2,1)}, bf16[8,96,640]{2,1,0:T(8,128)(2,1)S(1)}, u32[]{:S(2)}) copy-start(bf16[8,96,640]{2,1,0:T(8,128)(2,1)S(1)} %all-to-all-done.1) | copy-start | bytes 2949124
  46.1 6.7 %collective-permute-start.6 = (bf16[48,896]{1,0:T(8,128)(2,1)S(1)}, bf16[48,896]{1,0:T(8,128)(2,1)S(1)}, u32[]{:S(2)}, u32[]{:S(2)}) collective-permute-start(bf16[48,896]{1,0:T(8,128)(2,1)S(1)} %bitcast.143), channel_id=1, source_target_pairs={{0,24},{1,25},{2,26},{3,27},{4,28},{5,29},{6,30},{7,31},{8,16},{9,... | collective-permute-start | bytes 258056 | tf_op jit(solution)/shard_map/ppermute | solution.py:82
  48.1 7.2 %collective-permute-start.5 = (bf16[48,896]{1,0:T(8,128)(2,1)S(1)}, bf16[48,896]{1,0:T(8,128)(2,1)S(1)}, u32[]{:S(2)}, u32[]{:S(2)}) collective-permute-start(bf16[48,896]{1,0:T(8,128)(2,1)S(1)} %bitcast.144), channel_id=1, source_target_pairs={{0,16},{1,17},{2,18},{3,19},{4,20},{5,21},{6,22},{7,23},{8,24},{9,... | collective-permute-start | bytes 258056 | tf_op jit(solution)/shard_map/ppermute | solution.py:82
  48.1 7.2 %collective-permute-start.4 = (bf16[48,896]{1,0:T(8,128)(2,1)S(1)}, bf16[48,896]{1,0:T(8,128)(2,1)S(1)}, u32[]{:S(2)}, u32[]{:S(2)}) collective-permute-start(bf16[48,896]{1,0:T(8,128)(2,1)S(1)} %bitcast.145), channel_id=1, source_target_pairs={{0,8},{1,9},{2,10},{3,11},{4,12},{5,13},{6,14},{7,15},{8,0},{9,1},... | collective-permute-start | bytes 258056 | tf_op jit(solution)/shard_map/ppermute | solution.py:82
  50.5 14.3 %collective-permute-start.2 = (bf16[512,768]{1,0:T(8,128)(2,1)}, bf16[512,768]{1,0:T(8,128)(2,1)}, u32[]{:S(2)}, u32[]{:S(2)}) collective-permute-start(bf16[512,768]{1,0:T(8,128)(2,1)} %collective-permute-done.1.refs_2_), channel_id=1, source_target_pairs={{0,1},{1,0},{2,3},{3,2},{4,5},{5,4},{6,7},{7,6},{8,9},{9,8},{10,11... | collective-permute-start | bytes 2359304 | tf_op jit(solution)/shard_map/ppermute | solution.py:82
  56.2 79.6 %all-to-all-start.2 = ((bf16[8,144,768]{2,1,0:T(8,128)(2,1)}), bf16[8,144,768]{2,1,0:T(8,128)(2,1)S(1)}, u32[]{:S(2)}, u32[]{:S(2)}) async-start(bf16[8,144,768]{2,1,0:T(8,128)(2,1)} %bitcast.130), calls=%async_computation.2 | async-start | bytes 3538944 | tf_op jit(solution)/shard_map/all_to_all | solution.py:143
  73.9 20.4 %copy-start.27 = (bf16[4,48,896]{2,1,0:T(8,128)(2,1)S(1)}, bf16[4,48,896]{2,1,0:T(8,128)(2,1)}, u32[]{:S(2)}) copy-start(bf16[4,48,896]{2,1,0:T(8,128)(2,1)} %pad_maximum_fusion.8.refs_4_) | copy-start | bytes 1032196
  73.9 22.4 %copy-start.46 = (bf16[48,896]{1,0:T(8,128)(2,1)S(1)}, bf16[48,896]{1,0:T(8,128)(2,1)}, u32[]{:S(2)}) copy-start(bf16[48,896]{1,0:T(8,128)(2,1)} %copy-done.45) | copy-start | bytes 258052
  73.9 23.1 %copy-start.44 = (bf16[48,896]{1,0:T(8,128)(2,1)S(1)}, bf16[48,896]{1,0:T(8,128)(2,1)}, u32[]{:S(2)}) copy-start(bf16[48,896]{1,0:T(8,128)(2,1)} %copy-done.43) | copy-start | bytes 258052
  92.6 15.2 %copy-start.40 = (bf16[2,2,4,24,256]{4,3,2,0,1:T(8,128)(2,1)S(1)}, bf16[2,2,4,24,256]{4,3,2,0,1:T(8,128)(2,1)}, u32[]{:S(2)}) copy-start(bf16[2,2,4,24,256]{4,3,2,0,1:T(8,128)(2,1)} %constant_dynamic-update-slice_fusion.7) | copy-start | bytes 589828
  92.6 13.7 %collective-permute-start.7 = (bf16[2,192,512]{2,1,0:T(8,128)(2,1)S(1)}, bf16[2,192,512]{2,1,0:T(8,128)(2,1)S(1)}, u32[]{:S(2)}, u32[]{:S(2)}) collective-permute-start(bf16[2,192,512]{2,1,0:T(8,128)(2,1)S(1)} %slice.218), channel_id=1, source_target_pairs={{0,2},{1,3},{2,0},{3,1},{4,6},{5,7},{6,4},{7,5},{8,10},{9,11},{10,... | collective-permute-start | bytes 1179656 | tf_op jit(solution)/shard_map/ppermute | solution.py:82
  94.3 9.7 %collective-permute-start.9 = (bf16[4,48,896]{2,1,0:T(8,128)(2,1)S(1)}, bf16[4,48,896]{2,1,0:T(8,128)(2,1)S(1)}, u32[]{:S(2)}, u32[]{:S(2)}) collective-permute-start(bf16[4,48,896]{2,1,0:T(8,128)(2,1)S(1)} %copy-done.27), channel_id=1, source_target_pairs={{0,4},{1,5},{2,6},{3,7},{4,0},{5,1},{6,2},{7,3},{8,12},{9,13},{10,... | collective-permute-start | bytes 1032200 | tf_op jit(solution)/shard_map/ppermute | solution.py:82
  104.9 16.9 %collective-permute-start.10 = (bf16[8,48,896]{2,1,0:T(8,128)(2,1)}, bf16[8,48,896]{2,1,0:T(8,128)(2,1)}, u32[]{:S(2)}, u32[]{:S(2)}) collective-permute-start(bf16[8,48,896]{2,1,0:T(8,128)(2,1)} %constant_dynamic-update-slice_fusion), channel_id=1, source_target_pairs={{0,2},{1,3},{2,0},{3,1},{4,6},{5,7},{6,4},{7,5},{8,10},{9,11},{10,... | collective-permute-start | bytes 2064392 | tf_op jit(solution)/shard_map/ppermute | solution.py:82
  107.8 4.8 collective-permute-start.8
  107.8 1.8 collective-permute-start.12
  108.4 47.1 %collective-permute-start.16 = (bf16[512,768]{1,0:T(8,128)(2,1)S(1)}, bf16[512,768]{1,0:T(8,128)(2,1)}, u32[]{:S(2)}, u32[]{:S(2)}) collective-permute-start(bf16[512,768]{1,0:T(8,128)(2,1)S(1)} %copy-done.13), channel_id=1, source_target_pairs={{0,1},{1,0},{2,3},{3,2},{4,5},{5,4},{6,7},{7,6},{8,9},{9,8},{10,11... | collective-permute-start | bytes 2359304 | tf_op jit(solution)/shard_map/ppermute | solution.py:82
  109.7 18.0 %copy-start.33 = (bf16[2,288,256]{2,1,0:T(8,128)(2,1)}, bf16[2,288,256]{2,1,0:T(8,128)(2,1)S(1)}, u32[]{:S(2)}) copy-start(bf16[2,288,256]{2,1,0:T(8,128)(2,1)S(1)} %pad_maximum_fusion.9) | copy-start | bytes 884740
  109.7 18.0 %collective-permute-start.13 = (bf16[2,288,256]{2,1,0:T(8,128)(2,1)S(1)}, bf16[2,288,256]{2,1,0:T(8,128)(2,1)S(1)}, u32[]{:S(2)}, u32[]{:S(2)}) collective-permute-start(bf16[2,288,256]{2,1,0:T(8,128)(2,1)S(1)} %pad_maximum_fusion.9), channel_id=1, source_target_pairs={{0,8},{1,9},{2,10},{3,11},{4,12},{5,13},{6,14},{7,15},{8,0},{9,1},... | collective-permute-start | bytes 884744 | tf_op jit(solution)/shard_map/ppermute | solution.py:82
  112.3 23.4 %collective-permute-start.14 = (bf16[2,288,256]{2,1,0:T(8,128)(2,1)S(1)}, bf16[2,288,256]{2,1,0:T(8,128)(2,1)S(1)}, u32[]{:S(2)}, u32[]{:S(2)}) collective-permute-start(bf16[2,288,256]{2,1,0:T(8,128)(2,1)S(1)} %pad_maximum_fusion.9), channel_id=1, source_target_pairs={{0,16},{1,17},{2,18},{3,19},{4,20},{5,21},{6,22},{7,23},{8,24},{9,... | collective-permute-start | bytes 884744 | tf_op jit(solution)/shard_map/ppermute | solution.py:82
  112.6 23.1 %collective-permute-start.15 = (bf16[2,288,256]{2,1,0:T(8,128)(2,1)S(1)}, bf16[2,288,256]{2,1,0:T(8,128)(2,1)}, u32[]{:S(2)}, u32[]{:S(2)}) collective-permute-start(bf16[2,288,256]{2,1,0:T(8,128)(2,1)S(1)} %pad_maximum_fusion.9), channel_id=1, source_target_pairs={{0,24},{1,25},{2,26},{3,27},{4,28},{5,29},{6,30},{7,31},{8,16},{9,... | collective-permute-start | bytes 884744 | tf_op jit(solution)/shard_map/ppermute | solution.py:82
  135.7 18.8 %copy-start.17 = (bf16[8,144,768]{2,1,0:T(8,128)(2,1)}, bf16[8,144,768]{2,1,0:T(8,128)(2,1)S(1)}, u32[]{:S(2)}) copy-start(bf16[8,144,768]{2,1,0:T(8,128)(2,1)S(1)} %all-to-all-done.2.dy_ref) | copy-start | bytes 5308420
  136.4 42.2 %all-to-all-start.3 = ((bf16[8,80,768]{2,1,0:T(8,128)(2,1)}), bf16[8,80,768]{2,1,0:T(8,128)(2,1)S(1)}, u32[]{:S(2)}, u32[]{:S(2)}) async-start(bf16[8,80,768]{2,1,0:T(8,128)(2,1)} %bitcast.134), calls=%async_computation.3 | async-start | bytes 1966080 | tf_op jit(solution)/shard_map/all_to_all | solution.py:143
  160.4 22.7 %collective-permute-start.11 = (bf16[512,768]{1,0:T(8,128)(2,1)S(1)}, bf16[512,768]{1,0:T(8,128)(2,1)}, u32[]{:S(2)}, u32[]{:S(2)}) collective-permute-start(bf16[512,768]{1,0:T(8,128)(2,1)S(1)} %copy-done.14), channel_id=1, source_target_pairs={{0,1},{1,0},{2,3},{3,2},{4,5},{5,4},{6,7},{7,6},{8,9},{9,8},{10,11... | collective-permute-start | bytes 2359304 | tf_op jit(solution)/shard_map/ppermute | solution.py:82
  162.4 50.6 %collective-permute-start.17 = (bf16[4,288,256]{2,1,0:T(8,128)(2,1)}, bf16[4,288,256]{2,1,0:T(8,128)(2,1)}, u32[]{:S(2)}, u32[]{:S(2)}) collective-permute-start(bf16[4,288,256]{2,1,0:T(8,128)(2,1)} %pad_maximum_fusion.4.refs_0_), channel_id=1, source_target_pairs={{0,4},{1,5},{2,6},{3,7},{4,0},{5,1},{6,2},{7,3},{8,12},{9,13},{10,... | collective-permute-start | bytes 1769480 | tf_op jit(solution)/shard_map/ppermute | solution.py:82
  165.3 47.6 %collective-permute-start.18 = (bf16[4,288,256]{2,1,0:T(8,128)(2,1)}, bf16[4,288,256]{2,1,0:T(8,128)(2,1)}, u32[]{:S(2)}, u32[]{:S(2)}) collective-permute-start(bf16[4,288,256]{2,1,0:T(8,128)(2,1)} %pad_maximum_fusion.5.refs_3_), channel_id=1, source_target_pairs={{0,2},{1,3},{2,0},{3,1},{4,6},{5,7},{6,4},{7,5},{8,10},{9,11},{10,... | collective-permute-start | bytes 1769480 | tf_op jit(solution)/shard_map/ppermute | solution.py:82
  178.6 27.4 %all-to-all-start.5 = ((bf16[8,64,768]{2,1,0:T(8,128)(2,1)}), bf16[8,64,768]{2,1,0:T(8,128)(2,1)S(1)}, u32[]{:S(2)}, u32[]{:S(2)}) async-start(bf16[8,64,768]{2,1,0:T(8,128)(2,1)} %bitcast.37), calls=%async_computation.5 | async-start | bytes 1572864 | tf_op jit(solution)/shard_map/all_to_all | solution.py:143
  206.0 30.2 %all-to-all-start.4 = ((bf16[8,80,768]{2,1,0:T(8,128)(2,1)}), bf16[8,80,768]{2,1,0:T(8,128)(2,1)S(1)}, u32[]{:S(2)}, u32[]{:S(2)}) async-start(bf16[8,80,768]{2,1,0:T(8,128)(2,1)} %bitcast.135), calls=%async_computation.4 | async-start | bytes 1966080 | tf_op jit(solution)/shard_map/all_to_all | solution.py:143
  214.3 47.4 %collective-permute-start.19 = (bf16[8,288,256]{2,1,0:T(8,128)(2,1)S(1)}, bf16[8,288,256]{2,1,0:T(8,128)(2,1)}, u32[]{:S(2)}, u32[]{:S(2)}) collective-permute-start(bf16[8,288,256]{2,1,0:T(8,128)(2,1)S(1)} %pad_maximum_fusion.1), channel_id=1, source_target_pairs={{0,2},{1,3},{2,0},{3,1},{4,6},{5,7},{6,4},{7,5},{8,10},{9,11},{10,... | collective-permute-start | bytes 3538952 | tf_op jit(solution)/shard_map/ppermute | solution.py:82
  216.2 45.5 %collective-permute-start.20 = (bf16[8,288,256]{2,1,0:T(8,128)(2,1)S(1)}, bf16[8,288,256]{2,1,0:T(8,128)(2,1)}, u32[]{:S(2)}, u32[]{:S(2)}) collective-permute-start(bf16[8,288,256]{2,1,0:T(8,128)(2,1)S(1)} %pad_maximum_fusion.2), channel_id=1, source_target_pairs={{0,4},{1,5},{2,6},{3,7},{4,0},{5,1},{6,2},{7,3},{8,12},{9,13},{10,... | collective-permute-start | bytes 3538952 | tf_op jit(solution)/shard_map/ppermute | solution.py:82
  236.1 21.0 %copy-start.10 = (bf16[8,80,768]{2,1,0:T(8,128)(2,1)}, bf16[8,80,768]{2,1,0:T(8,128)(2,1)S(1)}, u32[]{:S(2)}) copy-start(bf16[8,80,768]{2,1,0:T(8,128)(2,1)S(1)} %all-to-all-done.4) | copy-start | bytes 2949124
  257.2 35.0 %all-to-all-start.6 = ((bf16[8,80,768]{2,1,0:T(8,128)(2,1)}), bf16[8,80,768]{2,1,0:T(8,128)(2,1)S(1)}, u32[]{:S(2)}, u32[]{:S(2)}) async-start(bf16[8,80,768]{2,1,0:T(8,128)(2,1)} %get-tuple-element.153), calls=%async_computation.6 | async-start | bytes 1966080 | tf_op jit(solution)/shard_map/all_to_all | solution.py:143
  287.0 5.2 collective-permute-start.21
  287.1 43.8 %collective-permute-start.23 = (bf16[2,768,1024]{2,1,0:T(8,128)(2,1)}, bf16[2,768,1024]{2,1,0:T(8,128)(2,1)}, u32[]{:S(2)}, u32[]{:S(2)}) collective-permute-start(bf16[2,768,1024]{2,1,0:T(8,128)(2,1)} %get-tuple-element.159), channel_id=1, source_target_pairs={{0,1},{1,0},{2,3},{3,2},{4,5},{5,4},{6,7},{7,6},{8,9},{9,8},{10,11... | collective-permute-start | bytes 9437192 | tf_op jit(solution)/shard_map/ppermute | solution.py:82
  287.6 30.3 %collective-permute-start.24 = (bf16[2,512,768]{2,1,0:T(8,128)(2,1)}, bf16[2,512,768]{2,1,0:T(8,128)(2,1)}, u32[]{:S(2)}, u32[]{:S(2)}) collective-permute-start(bf16[2,512,768]{2,1,0:T(8,128)(2,1)} %get-tuple-element.161), channel_id=1, source_target_pairs={{0,1},{1,0},{2,3},{3,2},{4,5},{5,4},{6,7},{7,6},{8,9},{9,8},{10,11... | collective-permute-start | bytes 4718600 | tf_op jit(solution)/shard_map/ppermute | solution.py:82
  287.7 29.1 %collective-permute-start.25 = (bf16[8,288,256]{2,1,0:T(8,128)(2,1)}, bf16[8,288,256]{2,1,0:T(8,128)(2,1)}, u32[]{:S(2)}, u32[]{:S(2)}) collective-permute-start(bf16[8,288,256]{2,1,0:T(8,128)(2,1)} %get-tuple-element.163), channel_id=1, source_target_pairs={{0,2},{1,3},{2,0},{3,1},{4,6},{5,7},{6,4},{7,5},{8,10},{9,11},{10,... | collective-permute-start | bytes 3538952 | tf_op jit(solution)/shard_map/ppermute | solution.py:82
  289.2 28.6 %collective-permute-start.26 = (bf16[8,288,256]{2,1,0:T(8,128)(2,1)}, bf16[8,288,256]{2,1,0:T(8,128)(2,1)}, u32[]{:S(2)}, u32[]{:S(2)}) collective-permute-start(bf16[8,288,256]{2,1,0:T(8,128)(2,1)} %get-tuple-element.164), channel_id=1, source_target_pairs={{0,4},{1,5},{2,6},{3,7},{4,0},{5,1},{6,2},{7,3},{8,12},{9,13},{10,... | collective-permute-start | bytes 3538952 | tf_op jit(solution)/shard_map/ppermute | solution.py:82
  293.6 24.2 %copy-start.18 = (bf16[2,512,768]{2,1,0:T(8,128)(2,1)S(1)}, bf16[2,512,768]{2,1,0:T(8,128)(2,1)}, u32[]{:S(2)}) copy-start(bf16[2,512,768]{2,1,0:T(8,128)(2,1)} %get-tuple-element.160) | copy-start | bytes 4718596
  308.4 16.7 %collective-permute-start.22 = (bf16[2,192,512]{2,1,0:T(8,128)(2,1)S(1)}, bf16[2,192,512]{2,1,0:T(8,128)(2,1)S(1)}, u32[]{:S(2)}, u32[]{:S(2)}) collective-permute-start(bf16[2,192,512]{2,1,0:T(8,128)(2,1)S(1)} %slice.236), channel_id=1, source_target_pairs={{0,2},{1,3},{2,0},{3,1},{4,6},{5,7},{6,4},{7,5},{8,10},{9,11},{10,... | collective-permute-start | bytes 1179656 | tf_op jit(solution)/shard_map/ppermute | solution.py:82
  310.9 15.0 %copy-start.29 = (bf16[8,288,256]{2,1,0:T(8,128)(2,1)S(1)}, bf16[8,288,256]{2,1,0:T(8,128)(2,1)}, u32[]{:S(2)}) copy-start(bf16[8,288,256]{2,1,0:T(8,128)(2,1)} %get-tuple-element.162) | copy-start | bytes 3538948
  319.2 27.6 %collective-permute-start.28 = (bf16[512,768]{1,0:T(8,128)(2,1)S(1)}, bf16[512,768]{1,0:T(8,128)(2,1)S(1)}, u32[]{:S(2)}, u32[]{:S(2)}) collective-permute-start(bf16[512,768]{1,0:T(8,128)(2,1)S(1)} %fusion.10), channel_id=1, source_target_pairs={{0,2},{1,3},{2,0},{3,1},{4,6},{5,7},{6,4},{7,5},{8,10},{9,11},{10,... | collective-permute-start | bytes 2359304 | tf_op jit(solution)/shard_map/ppermute | solution.py:82
  325.8 4.3 collective-permute-start.27
  346.8 12.9 %copy-start.37 = (bf16[512,768]{1,0:T(8,128)(2,1)}, bf16[512,768]{1,0:T(8,128)(2,1)S(1)}, u32[]{:S(2)}) copy-start(bf16[512,768]{1,0:T(8,128)(2,1)S(1)} %collective-permute-done.28) | copy-start | bytes 2359300
  384.6 31.0 %all-to-all-start.8 = ((bf16[32,24,640]{2,1,0:T(8,128)(2,1)}), bf16[32,24,640]{2,1,0:T(8,128)(2,1)S(1)}, u32[]{:S(2)}, u32[]{:S(2)}) async-start(bf16[32,24,640]{2,1,0:T(8,128)(2,1)} %bitcast.136), calls=%async_computation.8 | async-start | bytes 1966080 | tf_op jit(solution)/shard_map/all_to_all | solution.py:143
  416.6 64.5 %all-to-all-start.7 = ((bf16[8,144,768]{2,1,0:T(8,128)(2,1)}), bf16[8,144,768]{2,1,0:T(8,128)(2,1)S(1)}, u32[]{:S(2)}, u32[]{:S(2)}) async-start(bf16[8,144,768]{2,1,0:T(8,128)(2,1)} %pad_maximum_fusion), calls=%async_computation.7 | async-start | bytes 3538944 | tf_op jit(solution)/shard_map/all_to_all | solution.py:143
  422.5 31.9 %collective-permute-start.34 = (bf16[4,288,256]{2,1,0:T(8,128)(2,1)}, bf16[4,288,256]{2,1,0:T(8,128)(2,1)S(1)}, u32[]{:S(2)}, u32[]{:S(2)}) collective-permute-start(bf16[4,288,256]{2,1,0:T(8,128)(2,1)} %add_convert_fusion.6), channel_id=1, source_target_pairs={{0,4},{1,5},{2,6},{3,7},{4,0},{5,1},{6,2},{7,3},{8,12},{9,13},{10,... | collective-permute-start | bytes 1769480 | tf_op jit(solution)/shard_map/ppermute | solution.py:82
  424.6 29.9 %collective-permute-start.35 = (bf16[4,288,256]{2,1,0:T(8,128)(2,1)}, bf16[4,288,256]{2,1,0:T(8,128)(2,1)S(1)}, u32[]{:S(2)}, u32[]{:S(2)}) collective-permute-start(bf16[4,288,256]{2,1,0:T(8,128)(2,1)} %add_convert_fusion.5), channel_id=1, source_target_pairs={{0,2},{1,3},{2,0},{3,1},{4,6},{5,7},{6,4},{7,5},{8,10},{9,11},{10,... | collective-permute-start | bytes 1769480 | tf_op jit(solution)/shard_map/ppermute | solution.py:82
  426.0 48.8 %collective-permute-start.30 = (bf16[768,1024]{1,0:T(8,128)(2,1)}, bf16[768,1024]{1,0:T(8,128)(2,1)S(1)}, u32[]{:S(2)}, u32[]{:S(2)}) collective-permute-start(bf16[768,1024]{1,0:T(8,128)(2,1)} %fusion.4), channel_id=1, source_target_pairs={{0,2},{1,3},{2,0},{3,1},{4,6},{5,7},{6,4},{7,5},{8,10},{9,11},{10,... | collective-permute-start | bytes 4718600 | tf_op jit(solution)/shard_map/ppermute | solution.py:82
  426.6 33.9 %collective-permute-start.29 = (bf16[2,512,768]{2,1,0:T(8,128)(2,1)}, bf16[2,512,768]{2,1,0:T(8,128)(2,1)S(1)}, u32[]{:S(2)}, u32[]{:S(2)}) collective-permute-start(bf16[2,512,768]{2,1,0:T(8,128)(2,1)} %get-tuple-element.177), channel_id=1, source_target_pairs={{0,1},{1,0},{2,3},{3,2},{4,5},{5,4},{6,7},{7,6},{8,9},{9,8},{10,11... | collective-permute-start | bytes 4718600 | tf_op jit(solution)/shard_map/ppermute | solution.py:82
  426.9 29.7 %collective-permute-start.32 = (bf16[8,2,24,896]{3,2,0,1:T(8,128)(2,1)S(1)}, bf16[8,2,24,896]{3,2,0,1:T(8,128)(2,1)S(1)}, u32[]{:S(2)}, u32[]{:S(2)}) collective-permute-start(bf16[8,2,24,896]{3,2,0,1:T(8,128)(2,1)S(1)} %bitcast.148), channel_id=1, source_target_pairs={{0,1},{1,0},{2,3},{3,2},{4,5},{5,4},{6,7},{7,6},{8,9},{9,8},{10,11... | collective-permute-start | bytes 2064392 | tf_op jit(solution)/shard_map/ppermute | solution.py:82
  429.0 25.5 %copy-start.32 = (bf16[8,288,256]{2,1,0:T(8,128)(2,1)S(1)}, bf16[8,288,256]{2,1,0:T(8,128)(2,1)}, u32[]{:S(2)}) copy-start(bf16[8,288,256]{2,1,0:T(8,128)(2,1)} %get-tuple-element.166) | copy-start | bytes 3538948
  456.8 18.0 %copy-start.20 = (bf16[2,512,768]{2,1,0:T(8,128)(2,1)S(1)}, bf16[2,512,768]{2,1,0:T(8,128)(2,1)}, u32[]{:S(2)}) copy-start(bf16[2,512,768]{2,1,0:T(8,128)(2,1)} %get-tuple-element.176) | copy-start | bytes 4718596
  456.8 23.5 %collective-permute-start.33 = (bf16[8,24,896]{2,1,0:T(8,128)(2,1)S(1)}, bf16[8,24,896]{2,1,0:T(8,128)(2,1)S(1)}, u32[]{:S(2)}, u32[]{:S(2)}) collective-permute-start(bf16[8,24,896]{2,1,0:T(8,128)(2,1)S(1)} %dynamic-slice_bitcast_fusion), channel_id=1, source_target_pairs={{0,2},{1,3},{2,0},{3,1},{4,6},{5,7},{6,4},{7,5},{8,10},{9,11},{10,... | collective-permute-start | bytes 1032200 | tf_op jit(solution)/shard_map/ppermute | solution.py:82
  460.5 20.7 %copy-start.22 = (bf16[2,512,768]{2,1,0:T(8,128)(2,1)}, bf16[2,512,768]{2,1,0:T(8,128)(2,1)S(1)}, u32[]{:S(2)}) copy-start(bf16[2,512,768]{2,1,0:T(8,128)(2,1)S(1)} %collective-permute-done.29) | copy-start | bytes 4718596
  481.1 13.7 %all-to-all-start.9 = ((bf16[8,24,896]{2,1,0:T(8,128)(2,1)}), bf16[8,24,896]{2,1,0:T(8,128)(2,1)}, u32[]{:S(2)}, u32[]{:S(2)}) async-start(bf16[8,24,896]{2,1,0:T(8,128)(2,1)} %fusion.13), calls=%async_computation.9 | async-start | bytes 688128 | tf_op jit(solution)/shard_map/all_to_all | solution.py:143
  491.1 23.2 %collective-permute-start.31 = (bf16[512,768]{1,0:T(8,128)(2,1)}, bf16[512,768]{1,0:T(8,128)(2,1)}, u32[]{:S(2)}, u32[]{:S(2)}) collective-permute-start(bf16[512,768]{1,0:T(8,128)(2,1)} %fusion.11), channel_id=1, source_target_pairs={{0,2},{1,3},{2,0},{3,1},{4,6},{5,7},{6,4},{7,5},{8,10},{9,11},{10,... | collective-permute-start | bytes 2359304 | tf_op jit(solution)/shard_map/ppermute | solution.py:82
  494.9 30.4 %all-to-all-start.10 = ((bf16[4,2,288,256]{3,2,1,0:T(8,128)(2,1)}), bf16[4,2,288,256]{3,2,1,0:T(8,128)(2,1)S(1)}, u32[]{:S(2)}, u32[]{:S(2)}) async-start(bf16[4,2,288,256]{3,2,1,0:T(8,128)(2,1)} %copy.217), calls=%async_computation.10 | async-start | bytes 2359296 | tf_op jit(solution)/shard_map/all_to_all | solution.py:106
  525.6 1.9 collective-permute-start.36
  (41 other events, 195.6 us)
